TPU v7x, 128 devices: a whole 4x4x4 slice. The times are simulated.
128 devices in a mesh: gx: 8 (over z_lo, x), gy: 4 (over y), gz: 4 (over z_hi, core).
Axes of the slice: x: 4, y: 4, z: 4 (z_hi: 2, z_lo: 2; z = z_hi * 2 + z_lo), core: 2. Of those that a mesh axis runs over, the one named last changes fastest.
Arguments:
- force: float32 [3, 128, 32, 512], P(None, 'gx', 'gy', 'gz')
- kappa: float32 [128, 32, 512], P('gx', 'gy', 'gz'), may hold values from 0.5 to 4
- mortar_blocks: float32 [8, 4, 4, 192, 4096], P('gx', 'gy', 'gz'), may hold values from -0.375 to 0.375
- mortar_index: int32 [8, 4, 4, 48, 4], P('gx', 'gy', 'gz'), may hold values from 0 to 47, as said below
- mortar_count: int32 [8, 4, 4, 48], P('gx', 'gy', 'gz'), may hold values from 1 to 4, as said below
- agg_map: int32 [128, 32, 512], P('gx', 'gy', 'gz'), may hold values from 0 to 511
- coarse_matrix: float32 [8, 4, 512, 512], P('gx', 'gy', 'gz'), may hold values from -0.125 to 0.125
- coarse_diag: float32 [8, 4, 512], P('gx', 'gy', 'gz'), may hold values from 1 to 3
Outputs:
- velocity: float32 [3, 128, 32, 512], P(None, 'gx', 'gy', 'gz')
- multipliers: float32 [8, 3, 32, 512], P('gx', None, 'gy', 'gz')
Inputs may be any that keep to these rules, and one draw needn't show every extreme that they name: `mortar_index`: entry k of block j's list is block (j + s + k) modulo 48, for a shift s of -3 to 0 drawn for each block; the entries of one list are distinct. `mortar_count`: some block of every device uses all 4 entries.
All inputs are finite; a program needn't handle non-finite values.
Results may differ from a plain program's by a relative error of at most 0.0003.
Values sent between devices are 32-bit elements; how exact they have to be, the bound alone decides.
No kernel may reach another device: no remote copies, remote signals or barrier semaphores. Data moves between devices by JAX's collectives and lax.ppermute only.
A program may use at most 64 MiB of HBM per device.

v0:
```python
import functools

import jax
import jax.numpy as jnp
from jax import lax
from jax.experimental import pallas as pl
from jax.experimental.pallas import tpu as pltpu
from jax.sharding import PartitionSpec as P

BLK = 64
NAGG = 512
TAIL = 7
HEAD = 15
NP = TAIL + HEAD
NF = 3 * NP
LINES = 72
LOW = TAIL
UPP = TAIL - 1
RET = 4
COARSE_OMEGA = 0.8
PROLONG_GAIN = 0.5
F32 = jnp.float32
BF16 = jnp.bfloat16

VMEM = pl.BlockSpec(memory_space=pltpu.VMEM)
SMEM = pl.BlockSpec(memory_space=pltpu.SMEM)


def call(body, outs, scratch=(), n_smem=0, n_in=0, aliases=None, limit=40):
    return pl.pallas_call(
        body,
        out_shape=[jax.ShapeDtypeStruct(s, d) for s, d in outs],
        in_specs=[SMEM] * n_smem + [VMEM] * n_in,
        out_specs=[VMEM] * len(outs),
        scratch_shapes=list(scratch),
        input_output_aliases=aliases or {},
        compiler_params=pltpu.CompilerParams(vmem_limit_bytes=limit * 1024 * 1024),
    )


def prepare_kernel(blocks, by_col, by_row, piece):
    zero = jnp.zeros((8, 128), F32)

    def chunk(i, _):
        piece[...] = blocks[:, pl.ds(pl.multiple_of(i * 128, 128), 128)]
        for tile in range(2):
            rows = []
            for k in (2 * tile, 2 * tile + 1):
                for par in range(2):
                    rows += [piece[pl.ds(4 * par + k, 24, stride=8), :], zero]
            turned = jnp.concatenate(rows, 0).T
            for half in range(2):
                part = turned[64 * half : 64 * half + 64]
                by_row[tile, pl.ds(pl.multiple_of(i * 128 + 64 * half, 64), 64), :] = part
                by_col[tile, pl.ds(2 * i + half, 64, stride=64), :] = part
        return 0

    lax.fori_loop(0, 32, chunk, 0)


def weigh(matrices, rows, wide):
    def body(i, accs):
        first, second = accs
        at = pl.multiple_of(i * 64, 64)
        one = rows[0, pl.ds(i, 1), :]
        two = rows[1, pl.ds(i, 1), :] if wide else one
        first = first + matrices[0, pl.ds(at, 64), :] * one
        second = second + matrices[1, pl.ds(at, 64), :] * two
        return first, second

    zero = jnp.zeros((64, 128), F32)
    return lax.fori_loop(0, 64, body, (zero, zero), unroll=8)


def split(x):
    high = x.astype(BF16)
    return high, (x - high.astype(F32)).astype(BF16)


def project(by_col, spots, used, work, values):
    for tile in range(2):
        lanes = slice(128 * tile, 128 * tile + 128)
        for g in range(8):
            rows = slice(8 * g, 8 * g + 8)
            picked = jnp.take_along_axis(values[rows], spots[:, lanes], axis=1, mode="promise_in_bounds")
            work[tile, rows, :] = picked * used[:, lanes]
    first, second = weigh(by_col, work, True)
    total = first + second
    return total + pltpu.roll(total, 64, 1)


def project_back(by_row, place, work, values):
    work[0] = values
    first, second = weigh(by_row, work, False)
    high, low = split(jnp.concatenate([first, second], 1))
    both = lax.dot_general(
        jnp.concatenate([high, low], 0), place[...], (((1,), (1,)), ((), ())), preferred_element_type=F32
    )
    return both[0:64] + both[64:128]


def turn(lower, upper):
    left = lax.broadcasted_iota(jnp.int32, (24, 128), 1) < 64
    even = jnp.where(left, lower, pltpu.roll(upper, 64, 1))
    odd = jnp.where(left, pltpu.roll(lower, 64, 1), upper)
    zero = jnp.zeros((8, 128), F32)
    turned = jnp.concatenate([even, zero, odd, zero, even, zero, odd, zero], 0).T
    return turned[0:64], turned[64:128]


def turn_back(lower, upper):
    left = lax.broadcasted_iota(jnp.int32, (24, 128), 1) < 64
    rows = jnp.concatenate([lower, upper], 0).T
    even, odd = rows[0:24], rows[32:56]
    return (
        jnp.where(left, even, pltpu.roll(odd, 64, 1)),
        jnp.where(left, pltpu.roll(even, 64, 1), odd),
    )


def solve_interface(lower, upper, face, inverse, mortar, work):
    by_col, by_row, spots, used, place = mortar
    low_t, upp_t = turn(lower, upper)
    rhs = low_t - project(by_col, spots, used, work, upp_t)
    first = face * rhs
    back = project_back(by_row, place, work, first) * inverse
    rest = 0.6 * rhs - project(by_col, spots, used, work, back)
    increment = first + face * rest
    return turn_back(increment, project_back(by_row, place, work, increment))


def tall(plane):
    return jnp.concatenate([plane] * 3, 0)


class Halo:
    def __init__(self, flags, y_first, y_second, z_first, z_second):
        y_even, z_even = flags[0] == 1, flags[1] == 1
        self.y_low = jnp.where(y_even, y_second[...], y_first[...]) * flags[2].astype(F32)
        self.y_high = jnp.where(y_even, y_first[...], y_second[...]) * flags[3].astype(F32)
        self.z_low = jnp.where(z_even, z_second[0:8], z_first[0:8]) * flags[4].astype(F32)
        self.z_high = jnp.where(z_even, z_first[0:8], z_second[0:8]) * flags[5].astype(F32)


def residual_of(p, c, force, weight, velocity, halo):
    i = 3 * p + c
    sub = lax.broadcasted_iota(jnp.int32, (8, 128), 0)
    lane = lax.broadcasted_iota(jnp.int32, (8, 128), 1)
    v = velocity[p, c]
    total = force[p, c] - weight[p] * v
    if p not in (0, LOW):
        total = total + velocity[p - 1, c]
    if p not in (NP - 1, UPP):
        total = total + velocity[p + 1, c]
    total = total + jnp.where(sub == 0, halo.y_low[i : i + 1], pltpu.roll(v, 1, 0))
    total = total + jnp.where(sub == 7, halo.y_high[i : i + 1], pltpu.roll(v, 7, 0))
    total = total + jnp.where(lane == 0, pltpu.roll(halo.z_low, (128 - i) % 128, 1), pltpu.roll(v, 1, 1))
    total = total + jnp.where(lane == 127, pltpu.roll(halo.z_high, 127 - i, 1), pltpu.roll(v, 127, 1))
    return total


def write_lines(flags, get, y_first, y_second):
    y_even = flags[0] == 1
    for i in range(NF):
        v = get(i // 3, i % 3)
        top, bottom = v[0:1], v[7:8]
        y_first[i : i + 1] = jnp.where(y_even, bottom, top)
        y_second[i : i + 1] = jnp.where(y_even, top, bottom)
    rest = jnp.zeros((LINES - NF, 128), F32)
    y_first[NF:LINES] = rest
    y_second[NF:LINES] = rest


def columns(get):
    lane = lax.broadcasted_iota(jnp.int32, (8, 128), 1)
    first = jnp.zeros((8, 128), F32)
    last = first
    for i in range(NF):
        v = get(i // 3, i % 3)
        first = jnp.where(lane == i, pltpu.roll(v, i, 1) if i else v, first)
        last = jnp.where(lane == i, pltpu.roll(v, i + 1, 1), last)
    return first, last


def write_columns(flags, get, z_first, z_second, row=0):
    z_even = flags[1] == 1
    first, last = columns(get)
    z_first[row : row + 8] = jnp.where(z_even, last, first)
    z_second[row : row + 8] = jnp.where(z_even, first, last)


def first_sweep_kernel(
    flags, force_in, kappa_in, agg_in, tail, by_col, by_row, spots, used, place,
    force, weight, inverse, agg, velocity, mult, mult_up, face, inverse_t, y1, y2, z1, z2, work,
):
    for p in range(NP):
        here = p - TAIL
        kappa = tail[p, 3] if here < 0 else kappa_in[here]
        w = 6.0 + kappa
        weight[p] = w
        inverse[p] = 1.0 / (1.5 * w)
        agg[p] = tail[p, 4].astype(jnp.int32) if here < 0 else agg_in[here]
        for c in range(3):
            f = tail[p, c] if here < 0 else force_in[c, here]
            force[p, c] = f
            velocity[p, c] = f * inverse[p]
    low_w, upp_inv = turn(tall(weight[LOW]), tall(inverse[UPP]))
    face[...] = 0.6 * low_w
    inverse_t[...] = upp_inv
    lower = velocity[LOW].reshape(24, 128)
    upper = velocity[UPP].reshape(24, 128)
    increment, pulled = solve_interface(
        lower, upper, face[...], upp_inv, (by_col, by_row, spots, used, place), work
    )
    mult[...] = increment.reshape(3, 8, 128)
    mult_up[...] = pulled.reshape(3, 8, 128)
    velocity[LOW] = (lower - increment * tall(inverse[LOW])).reshape(3, 8, 128)
    velocity[UPP] = (upper + pulled * tall(inverse[UPP])).reshape(3, 8, 128)
    get = lambda p, c: velocity[p, c]
    write_lines(flags, get, y1, y2)
    write_columns(flags, get, z1, z2)
    write_columns(flags, lambda p, c: agg[p].astype(F32), z1, z2, 8)


def sweep(
    flags, force, weight, inverse, velocity, mult, mult_up, face, inverse_t, by_col, by_row, spots, used, place,
    halo, work, out, out_mult, out_up,
):
    def residuals(p):
        return jnp.concatenate([residual_of(p, c, force, weight, velocity, halo) for c in range(3)], 0)

    res_low = residuals(LOW) - mult[...].reshape(24, 128)
    res_upp = residuals(UPP) + mult_up[...].reshape(24, 128)
    inv_low, inv_upp = tall(inverse[LOW]), tall(inverse[UPP])
    lower = velocity[LOW].reshape(24, 128) + res_low * inv_low
    upper = velocity[UPP].reshape(24, 128) + res_upp * inv_upp
    increment, pulled = solve_interface(
        lower, upper, face[...], inverse_t[...], (by_col, by_row, spots, used, place), work
    )
    out_mult[...] = mult[...] + increment.reshape(3, 8, 128)
    out_up[...] = mult_up[...] + pulled.reshape(3, 8, 128)
    for p in range(NP):
        if p in (LOW, UPP):
            continue
        for c in range(3):
            out[p, c] = velocity[p, c] + residual_of(p, c, force, weight, velocity, halo) * inverse[p]
    out[LOW] = (lower - increment * inv_low).reshape(3, 8, 128)
    out[UPP] = (upper + pulled * inv_upp).reshape(3, 8, 128)


def second_sweep_kernel(
    flags, force, weight, inverse, velocity, mult, mult_up, face, inverse_t, by_col, by_row, spots, used, place,
    y1, y2, z1, z2, out, out_mult, out_up, oy1, oy2, oz1, oz2, work,
):
    halo = Halo(flags, y1, y2, z1, z2)
    sweep(
        flags, force, weight, inverse, velocity, mult, mult_up, face, inverse_t, by_col, by_row, spots, used, place,
        halo, work, out, out_mult, out_up,
    )
    get = lambda p, c: out[p, c]
    write_lines(flags, get, oy1, oy2)
    write_columns(flags, get, oz1, oz2)


def third_sweep_kernel(
    flags, force, weight, inverse, velocity, mult, mult_up, face, inverse_t, by_col, by_row, spots, used, place,
    y1, y2, z_low, z_high, out, out_mult, out_up, oy1, oy2, oz1, oz2, work,
):
    halo = Halo(flags, y1, y2, z_low, z_high)
    halo.z_low, halo.z_high = z_low[...], z_high[...]
    sweep(
        flags, force, weight, inverse, velocity, mult, mult_up, face, inverse_t, by_col, by_row, spots, used, place,
        halo, work, out, out_mult, out_up,
    )
    get = lambda p, c: out[p, c]
    write_lines(flags, get, oy1, oy2)
    write_columns(flags, get, oz1, oz2)


def last_sweep_kernel(
    flags, force, weight, inverse, velocity, mult, mult_up, face, inverse_t, by_col, by_row, spots, used, place,
    y1, y2, z1, z2, head, tail, out_mult, out, out_up, work,
):
    halo = Halo(flags, y1, y2, z1, z2)
    sweep(
        flags, force, weight, inverse, velocity, mult, mult_up, face, inverse_t, by_col, by_row, spots, used, place,
        halo, work, out, out_mult, out_up,
    )
    for c in range(3):
        for p in range(16 - RET):
            head[c, p] = out[LOW + p, c]
        for p in range(RET):
            tail[c, p] = out[TAIL - RET + p, c]


def restrict_kernel(
    flags, force, weight, velocity, mult, mult_up, agg, y1, y2, z1, z2, own, prev, res,
):
    halo = Halo(flags, y1, y2, z1, z2)
    for p in range(TAIL - 3, NP - 2):
        for c in range(3):
            r = residual_of(p, c, force, weight, velocity, halo)
            if p == LOW:
                r = r - mult[c]
            if p == UPP:
                r = r + mult_up[c]
            res[p, c] = r
    down = lax.broadcasted_iota(jnp.int32, (128, 128), 0)
    sub = lax.broadcasted_iota(jnp.int32, (8, 128), 0)

    def plane(p, total):
        labels = agg[p]
        lows = labels & 127
        highs = lax.shift_right_logical(labels, 7)
        values = []
        for c in range(3):
            r = res[p, c]
            high = r.astype(BF16).astype(F32)
            values.append((high, r - high))
        for pair in range(4):
            tables, terms = [], []
            for y in (2 * pair, 2 * pair + 1):
                tables.append(jnp.where(down == lows[y : y + 1], 1.0, 0.0).astype(BF16))
                here = highs[y : y + 1] == (sub & 3)
                rows = [
                    jnp.where(here, jnp.where(sub < 4, high[y : y + 1], low[y : y + 1]), 0.0)
                    for high, low in values
                ]
                terms.append(jnp.concatenate(rows, 0).astype(BF16))
            total = total + lax.dot_general(
                jnp.concatenate(terms, 1), jnp.concatenate(tables, 1), (((1,), (1,)), ((), ())),
                preferred_element_type=F32,
            )
        return total

    empty = jnp.zeros((24, 128), F32)
    prev[...] = lax.fori_loop(TAIL - 3, TAIL, plane, empty)
    own[...] = lax.fori_loop(LOW, NP - 2, plane, empty)


def split_matrix_kernel(rows, high, low, scale):
    for block in range(4):
        at = slice(block * 128, block * 128 + 128)
        a = rows[block, 0:128, :].T
        h = a.astype(BF16)
        high[:, at] = h
        low[:, at] = (a - h.astype(F32)).astype(BF16)
        scale[:, at] = jnp.broadcast_to(rows[block, 128:129, 0:128], (8, 128))


def solve_kernel(own, other, high, low, scale, out, rhs):
    total = own[...] + other[...]
    rhs[...] = jnp.zeros((8, NAGG), F32)
    for c in range(3):
        for h in range(4):
            at = 8 * c + h
            rhs[c : c + 1, 128 * h : 128 * h + 128] = total[at : at + 1] + total[at + 4 : at + 5]
    gain = (16 * 8 * 512 / NAGG) ** -0.5
    step = COARSE_OMEGA / scale[...]
    start = (rhs[...] * gain) * step
    x = start
    for _ in range(3):
        xh, xl = split(x)
        both = jnp.concatenate([xh, xl], 0)
        first = jnp.dot(both, high[...], preferred_element_type=F32)
        second = jnp.dot(xh, low[...], preferred_element_type=F32)
        product = first[0:8] + first[8:16] + second
        x = (1.0 - COARSE_OMEGA) * x + (start - step * product)
    out[...] = x


def spread_kernel(
    flags, velocity, agg, iterate, below, z1, z2, az1, az2, out, y1, y2, z_low, z_high,
):
    def table(ref):
        return [
            [jnp.broadcast_to(ref[c : c + 1, 128 * h : 128 * h + 128], (8, 128)) * PROLONG_GAIN for h in range(4)]
            for c in range(3)
        ]

    own, prev = table(iterate), table(below)

    def pick(rows, lows, highs):
        got = [jnp.take_along_axis(row, lows, axis=1, mode="promise_in_bounds") for row in rows]
        return jnp.where(
            highs < 2, jnp.where(highs == 0, got[0], got[1]), jnp.where(highs == 2, got[2], got[3])
        )

    for p in range(NP):
        lows = agg[p] & 127
        highs = lax.shift_right_logical(agg[p], 7)
        for c in range(3):
            out[p, c] = velocity[p, c] + pick((prev if p < TAIL else own)[c], lows, highs)
    write_lines(flags, lambda p, c: out[p, c], y1, y2)
    z_even = flags[1] == 1
    lane = lax.broadcasted_iota(jnp.int32, (8, 128), 1)
    comp = lax.rem(lane, 3)
    for side, (v_even, v_odd, a_even, a_odd, flag, dest) in enumerate(
        ((z2, z1, az2, az1, 4, z_low), (z1, z2, az1, az2, 5, z_high))
    ):
        values = jnp.where(z_even, v_even[0:8], v_odd[0:8])
        labels = jnp.where(z_even, a_even[8:16], a_odd[8:16]).astype(jnp.int32)
        lows = labels & 127
        highs = lax.shift_right_logical(labels, 7)
        extra = jnp.zeros((8, 128), F32)
        for c in range(3):
            got = jnp.where(lane < 3 * TAIL, pick(prev[c], lows, highs), pick(own[c], lows, highs))
            extra = jnp.where(comp == c, got, extra)
        dest[...] = (values + extra) * flags[flag].astype(F32)


def ring(axis, by):
    n = lax.axis_size(axis)
    return [(i, (i + by) % n) for i in range(n)]


def swaps(axis, first):
    n = lax.axis_size(axis)
    pairs = []
    for i in range(first, first + n, 2):
        a, b = i % n, (i + 1) % n
        pairs += [(a, b), (b, a)]
    return pairs


def trade(y1, y2, z1=None, z2=None):
    got = [lax.ppermute(y1, "gy", swaps("gy", 0))]
    if z1 is not None:
        got_z = [lax.ppermute(z1, "gz", swaps("gz", 0))]
    got.append(lax.ppermute(y2, "gy", swaps("gy", 1)))
    if z1 is not None:
        got_z.append(lax.ppermute(z2, "gz", swaps("gz", 1)))
        got = got + got_z
    return got


def shards(force, kappa, mortar_blocks, mortar_index, mortar_count, agg_map, coarse_matrix, coarse_diag):
    gy, gz = lax.axis_index("gy"), lax.axis_index("gz")
    ny, nz = lax.axis_size("gy"), lax.axis_size("gz")
    flags = jnp.stack(
        [gy % 2 == 0, gz % 2 == 0, gy > 0, gy < ny - 1, gz > 0, gz < nz - 1]
    ).astype(jnp.int32)
    start = force.shape[1] - TAIL
    tail_in = jnp.concatenate(
        [
            jnp.transpose(force[:, start:], (1, 0, 2, 3)),
            kappa[start:, None],
            agg_map[start:, None].astype(F32),
        ],
        1,
    )
    tail_in = lax.ppermute(tail_in, "gx", ring("gx", 1))

    index = mortar_index.reshape(24, 2, 4)
    count = mortar_count.reshape(24, 2, 1)
    spots = (index % 2) * 32 + index // 2
    used = (jnp.arange(4)[None, None, :] < count).astype(F32)

    def lanes(x):
        x = jnp.pad(jnp.transpose(x, (2, 1, 0)), ((0, 0), (0, 0), (0, 8)))
        return jnp.broadcast_to(x.reshape(1, 256), (8, 256))

    spots, used = lanes(spots), lanes(used)
    place = jnp.where(
        lax.broadcasted_iota(jnp.int32, (128, 256), 0) % 64 == spots[0:1], used[0:1], 0.0
    ).astype(BF16)
    by_col, by_row = call(
        prepare_kernel, [((2, 4096, 128), F32)] * 2, [pltpu.VMEM((192, 128), F32)], n_in=1
    )(mortar_blocks.reshape(192, 4096))
    mortar = (by_col, by_row, spots, used, place)

    rows = jnp.concatenate(
        [coarse_matrix[0, 0], jnp.pad(coarse_diag[0], ((0, 7), (0, NAGG - 128)))], 0
    )
    rows = lax.all_gather(rows, "gz")
    k_high, k_low, scale = call(
        split_matrix_kernel, [((NAGG, NAGG), BF16), ((NAGG, NAGG), BF16), ((8, NAGG), F32)], n_in=1
    )(rows)

    field = ((NP, 3, 8, 128), F32)
    plane = ((3, 8, 128), F32)
    y_msg, z_msg = ((LINES, 128), F32), ((8, 128), F32)
    work = [pltpu.VMEM((2, 64, 128), F32)]
    out = call(
        first_sweep_kernel,
        [field, ((NP, 8, 128), F32), ((NP, 8, 128), F32), ((NP, 8, 128), jnp.int32), field, plane, plane,
         ((64, 128), F32), ((64, 128), F32), y_msg, y_msg, ((16, 128), F32), ((16, 128), F32)],
        work, 1, 9,
    )(flags, force, kappa, agg_map, tail_in, *mortar)
    force_e, weight, inverse, agg, velocity, mult, mult_up, face, inverse_t = out[:9]
    got = trade(*out[9:])
    az1, az2 = got[2], got[3]
    velocity, mult, mult_up, *msgs = call(
        second_sweep_kernel, [field, plane, plane, y_msg, y_msg, z_msg, z_msg], work, 1, 17
    )(flags, force_e, weight, inverse, velocity, mult, mult_up, face, inverse_t, *mortar, *got)
    got = trade(*msgs)
    own, prev = call(
        restrict_kernel, [((24, 128), F32)] * 2, [pltpu.VMEM((NP, 3, 8, 128), F32)], 1, 10
    )(flags, force_e, weight, velocity, mult, mult_up, agg, *got)
    total = own + lax.ppermute(prev, "gx", ring("gx", -1))
    total = total + lax.ppermute(total, "gz", swaps("gz", 0))
    other = lax.ppermute(total, "gz", ring("gz", 2))
    iterate = call(solve_kernel, [((8, NAGG), F32)], [pltpu.VMEM((8, NAGG), F32)], 0, 5)(
        total, other, k_high, k_low, scale
    )[0]
    below = lax.ppermute(iterate, "gx", ring("gx", 1))
    velocity, y1, y2, z_low, z_high = call(
        spread_kernel, [field, y_msg, y_msg, z_msg, z_msg], (), 1, 8
    )(flags, velocity, agg, iterate, below, got[2], got[3], az1, az2)
    got = trade(y1, y2)
    velocity, mult, mult_up, *msgs = call(
        third_sweep_kernel, [field, plane, plane, y_msg, y_msg, z_msg, z_msg], work, 1, 17
    )(flags, force_e, weight, inverse, velocity, mult, mult_up, face, inverse_t, *mortar, *got, z_low, z_high)
    got = trade(*msgs)
    head, tail, mult = call(
        last_sweep_kernel, [((3, 16 - RET, 8, 128), F32), ((3, RET, 8, 128), F32), plane],
        [pltpu.VMEM((NP, 3, 8, 128), F32), pltpu.VMEM((3, 8, 128), F32)] + work, 1, 17
    )(flags, force_e, weight, inverse, velocity, mult, mult_up, face, inverse_t, *mortar, *got)
    tail = lax.ppermute(tail, "gx", ring("gx", -1))
    return jnp.concatenate([head, tail], 1), mult[None]


def solution(mesh):
    in_specs = (
        P(None, "gx", "gy", "gz"),
        P("gx", "gy", "gz"),
        P("gx", "gy", "gz", None, None),
        P("gx", "gy", "gz", None, None),
        P("gx", "gy", "gz", None),
        P("gx", "gy", "gz"),
        P("gx", "gy", "gz", None),
        P("gx", "gy", "gz"),
    )
    out_specs = (P(None, "gx", "gy", "gz"), P("gx", None, "gy", "gz"))
    return jax.shard_map(shards, mesh=mesh, in_specs=in_specs, out_specs=out_specs, check_vma=False)
```

profile of v0, /device:TPU:6, one launch (start us, length us, event | category | flops | bytes accessed | tf_op | source)
XLA Modules:
  0.0 107.3 jit_solution(3738128451647363627)
XLA Ops:
  7.2 1.8 %select_maximum_fusion = f32[136,512]{1,0:T(8,128)} fusion(f32[1,128]{1,0:T(1,128)} %bitcast.26, f32[128,512]{1,0:T(8,128)} %bitcast.23), kind=kLoop, calls=%fused_computation | loop fusion | flops 208896 | bytes 541184 | tf_op jit(solution)/shard_map/concatenate | solution.py:472
  10.6 0.9 copy_bitcast_fusion
  11.5 1.9 %collective-permute-start = (f32[7,5,8,128]{3,2,1,0:T(8,128)S(1)}, f32[7,5,8,128]{3,2,1,0:T(8,128)S(1)}, u32[]{:S(2)}, u32[]{:S(2)}) collective-permute-start(f32[7,5,8,128]{3,2,1,0:T(8,128)S(1)} %pad_maximum_fusion.1), channel_id=1, source_target_pairs={{0,16},{16,32},{32,48},{48,64},{64,80},{80,96},{96,112},{112,0},{1... | collective-permute-start | bytes 430088 | tf_op jit(solution)/shard_map/ppermute | solution.py:452
  14.0 1.3 %reduce.3 = s32[48]{0:T(128)S(1)} reduce(s32[1,1,1,48]{3,2,1,0:T(1,128)} %param.12, s32[]{:T(128)} %broadcast.48), dimensions={0,1,2}, to_apply=%param.12.reduce_sub_computation.3 | reduce | bytes 388 | tf_op args[4]
  16.6 1.9 %copy-done.4 = f32[1,1,1,192,4096]{4,3,2,1,0:T(8,128)S(1)} copy-done((f32[1,1,1,192,4096]{4,3,2,1,0:T(8,128)S(1)}, f32[1,1,1,192,4096]{4,3,2,1,0:T(8,128)}, u32[]{:S(2)}) %copy-start.4) | copy-done | bytes 3145752
  18.5 7.4 %shard_map.95 = (f32[2,4096,128]{2,1,0:T(8,128)S(1)}, f32[2,4096,128]{2,1,0:T(8,128)S(1)}) custom-call(f32[192,4096]{1,0:T(8,128)S(1)} %bitcast.21), custom_call_target="tpu_custom_call" | custom-call | tf_op jit(solution)/shard_map/pallas_call | solution.py:467
  26.2 3.0 %shard_map.96 = (f32[22,3,8,128]{3,2,1,0:T(8,128)S(1)}, f32[22,8,128]{2,1,0:T(8,128)S(1)}, f32[22,8,128]{2,1,0:T(8,128)S(1)}, s32[22,8,128]{2,1,0:T(8,128)S(1)},...) custom-call(s32[6]{0:T(128)S(1)} %convert_element_type.18.flags, ...), custom_call_target="tpu_custom_call" | custom-call | tf_op jit(solution)/shard_map/pallas_call | solution.py:484
  29.2 1.7 %collective-permute-start.1 = (f32[72,128]{1,0:T(8,128)S(1)}, f32[72,128]{1,0:T(8,128)S(1)}, u32[]{:S(2)}, u32[]{:S(2)}) collective-permute-start(f32[72,128]{1,0:T(8,128)S(1)} %get-tuple-element.54), channel_id=1, source_target_pairs={{0,4},{4,0},{8,12},{12,8},{1,5},{5,1},{9,13},{13,9},{2,6},{6,2},{1... | collective-permute-start | bytes 110600 | tf_op jit(solution)/shard_map/ppermute | solution.py:427
  30.9 2.2 %collective-permute-start.2 = (f32[72,128]{1,0:T(8,128)S(1)}, f32[72,128]{1,0:T(8,128)S(1)}, u32[]{:S(2)}, u32[]{:S(2)}) collective-permute-start(f32[72,128]{1,0:T(8,128)S(1)} %get-tuple-element.55), channel_id=1, source_target_pairs={{4,8},{8,4},{12,0},{0,12},{5,9},{9,5},{13,1},{1,13},{6,10},{10,6},... | collective-permute-start | bytes 110600 | tf_op jit(solution)/shard_map/ppermute | solution.py:430
  33.1 3.7 %collective-permute-start.4 = (f32[16,128]{1,0:T(8,128)S(1)}, f32[16,128]{1,0:T(8,128)S(1)}, u32[]{:S(2)}, u32[]{:S(2)}) collective-permute-start(f32[16,128]{1,0:T(8,128)S(1)} %get-tuple-element.57), channel_id=1, source_target_pairs={{1,2},{2,1},{3,0},{0,3},{5,6},{6,5},{7,4},{4,7},{9,10},{10,9},{11,... | collective-permute-start | bytes 24584 | tf_op jit(solution)/shard_map/ppermute | solution.py:432
  36.8 1.4 %collective-permute-done.4.z2.az2 = f32[16,128]{1,0:T(8,128)S(1)} collective-permute-done((f32[16,128]{1,0:T(8,128)S(1)}, f32[16,128]{1,0:T(8,128)S(1)}, u32[]{:S(2)}, u32[]{:S(2)}) %collective-permute-start.4) | collective-permute-done | bytes 8224 | tf_op jit(solution)/shard_map/ppermute | solution.py:432
  38.1 3.2 %shard_map.97 = (f32[22,3,8,128]{3,2,1,0:T(8,128)S(1)}, f32[3,8,128]{2,1,0:T(8,128)S(1)}, f32[3,8,128]{2,1,0:T(8,128)S(1)}, f32[72,128]{1,0:T(8,128)S(1)}, f32[7...) custom-call(s32[6]{0:T(128)S(1)} %convert_element_type.18.flags, ...), custom_call_target="tpu_custom_call" | custom-call | tf_op jit(solution)/shard_map/pallas_call | solution.py:493
  42.7 3.2 %collective-permute-start.8 = (f32[8,128]{1,0:T(8,128)S(1)}, f32[8,128]{1,0:T(8,128)S(1)}, u32[]{:S(2)}, u32[]{:S(2)}) collective-permute-start(f32[8,128]{1,0:T(8,128)S(1)} %get-tuple-element.65), channel_id=1, source_target_pairs={{1,2},{2,1},{3,0},{0,3},{5,6},{6,5},{7,4},{4,7},{9,10},{10,9},{11,... | collective-permute-start | bytes 12296 | tf_op jit(solution)/shard_map/ppermute | solution.py:432
  46.0 1.3 %collective-permute-done.8.z2 = f32[8,128]{1,0:T(8,128)S(1)} collective-permute-done((f32[8,128]{1,0:T(8,128)S(1)}, f32[8,128]{1,0:T(8,128)S(1)}, u32[]{:S(2)}, u32[]{:S(2)}) %collective-permute-start.8) | collective-permute-done | bytes 4128 | tf_op jit(solution)/shard_map/ppermute | solution.py:432
  47.3 4.1 %shard_map.98 = (f32[24,128]{1,0:T(8,128)S(1)}, f32[24,128]{1,0:T(8,128)S(1)}) custom-call(s32[6]{0:T(128)S(1)} %convert_element_type.18.flags, f32[22,3,8,128]{3,2,1,0:T(8,128)S(1)} %get-tuple-element.46.force, f32[22,8,128]{2,1,0:T(8,128)S(1)} %get-tuple-element.47.weight, f32[22,3,8,128]{3,2,1,0:T(8,128)S(1)} %get-tuple-element.58.velocity, ...), custom_call_target="tpu_custom_call" | custom-call | tf_op jit(solution)/shard_map/pallas_call | solution.py:497
  51.9 5.3 %collective-permute-done.9 = f32[24,128]{1,0:T(8,128)S(1)} collective-permute-done((f32[24,128]{1,0:T(8,128)S(1)}, f32[24,128]{1,0:T(8,128)S(1)}, u32[]{:S(2)}, u32[]{:S(2)}) %collective-permute-start.9) | collective-permute-done | bytes 12320 | tf_op jit(solution)/shard_map/ppermute | solution.py:500
  57.2 1.2 %collective-permute-done.10 = f32[24,128]{1,0:T(8,128)S(1)} collective-permute-done((f32[24,128]{1,0:T(8,128)S(1)}, f32[24,128]{1,0:T(8,128)S(1)}, u32[]{:S(2)}, u32[]{:S(2)}) %collective-permute-start.10) | collective-permute-done | bytes 12320 | tf_op jit(solution)/shard_map/ppermute | solution.py:501
  58.4 3.2 %collective-permute-start.11 = (f32[24,128]{1,0:T(8,128)S(1)}, f32[24,128]{1,0:T(8,128)S(1)}, u32[]{:S(2)}, u32[]{:S(2)}) collective-permute-start(f32[24,128]{1,0:T(8,128)S(1)} %add.40.own), channel_id=1, source_target_pairs={{0,2},{1,3},{2,0},{3,1},{4,6},{5,7},{6,4},{7,5},{8,10},{9,11},{10,... | collective-permute-start | bytes 36872 | tf_op jit(solution)/shard_map/ppermute | solution.py:502
  61.5 1.2 %copy-done.5 = f32[544,512]{1,0:T(8,128)S(1)} copy-done((f32[544,512]{1,0:T(8,128)S(1)}, f32[544,512]{1,0:T(8,128)}, u32[]{:S(2)}) %copy-start.5) | copy-done | bytes 1114136
  64.3 3.7 %collective-permute-done.12.below = f32[8,512]{1,0:T(8,128)S(1)} collective-permute-done((f32[8,512]{1,0:T(8,128)S(1)}, f32[8,512]{1,0:T(8,128)S(1)}, u32[]{:S(2)}, u32[]{:S(2)}) %collective-permute-start.12) | collective-permute-done | bytes 16416 | tf_op jit(solution)/shard_map/ppermute | solution.py:506
  68.0 1.0 shard_map.101
  69.0 1.3 %collective-permute-start.13 = (f32[72,128]{1,0:T(8,128)S(1)}, f32[72,128]{1,0:T(8,128)S(1)}, u32[]{:S(2)}, u32[]{:S(2)}) collective-permute-start(f32[72,128]{1,0:T(8,128)S(1)} %get-tuple-element.72), channel_id=1, source_target_pairs={{0,4},{4,0},{8,12},{12,8},{1,5},{5,1},{9,13},{13,9},{2,6},{6,2},{1... | collective-permute-start | bytes 110600 | tf_op jit(solution)/shard_map/ppermute | solution.py:427
  70.3 2.2 %collective-permute-start.14 = (f32[72,128]{1,0:T(8,128)S(1)}, f32[72,128]{1,0:T(8,128)S(1)}, u32[]{:S(2)}, u32[]{:S(2)}) collective-permute-start(f32[72,128]{1,0:T(8,128)S(1)} %get-tuple-element.73), channel_id=1, source_target_pairs={{4,8},{8,4},{12,0},{0,12},{5,9},{9,5},{13,1},{1,13},{6,10},{10,6},... | collective-permute-start | bytes 110600 | tf_op jit(solution)/shard_map/ppermute | solution.py:430
  73.0 2.4 %collective-permute-done.14.y2 = f32[72,128]{1,0:T(8,128)S(1)} collective-permute-done((f32[72,128]{1,0:T(8,128)S(1)}, f32[72,128]{1,0:T(8,128)S(1)}, u32[]{:S(2)}, u32[]{:S(2)}) %collective-permute-start.14) | collective-permute-done | bytes 36896 | tf_op jit(solution)/shard_map/ppermute | solution.py:430
  75.4 2.2 %copy-done.1 = f32[2,4096,128]{2,1,0:T(8,128)S(1)} copy-done((f32[2,4096,128]{2,1,0:T(8,128)S(1)}, f32[2,4096,128]{2,1,0:T(8,128)}, u32[]{:S(2)}) %copy-start.1) | copy-done | bytes 4194328
  77.6 2.2 %copy-done.3 = f32[2,4096,128]{2,1,0:T(8,128)S(1)} copy-done((f32[2,4096,128]{2,1,0:T(8,128)S(1)}, f32[2,4096,128]{2,1,0:T(8,128)}, u32[]{:S(2)}) %copy-start.3) | copy-done | bytes 4194328
  79.8 3.2 %shard_map.102 = (f32[22,3,8,128]{3,2,1,0:T(8,128)S(1)}, f32[3,8,128]{2,1,0:T(8,128)S(1)}, f32[3,8,128]{2,1,0:T(8,128)S(1)}, f32[72,128]{1,0:T(8,128)S(1)}, f32[...) custom-call(s32[6]{0:T(128)S(1)} %convert_element_type.18.flags, ...), custom_call_target="tpu_custom_call" | custom-call | tf_op jit(solution)/shard_map/pallas_call | solution.py:511
  83.1 2.3 %collective-permute-start.16 = (f32[72,128]{1,0:T(8,128)S(1)}, f32[72,128]{1,0:T(8,128)S(1)}, u32[]{:S(2)}, u32[]{:S(2)}) collective-permute-start(f32[72,128]{1,0:T(8,128)S(1)} %get-tuple-element.80), channel_id=1, source_target_pairs={{4,8},{8,4},{12,0},{0,12},{5,9},{9,5},{13,1},{1,13},{6,10},{10,6},... | collective-permute-start | bytes 110600 | tf_op jit(solution)/shard_map/ppermute | solution.py:430
  85.4 3.2 %collective-permute-start.18 = (f32[8,128]{1,0:T(8,128)S(1)}, f32[8,128]{1,0:T(8,128)S(1)}, u32[]{:S(2)}, u32[]{:S(2)}) collective-permute-start(f32[8,128]{1,0:T(8,128)S(1)} %get-tuple-element.82), channel_id=1, source_target_pairs={{1,2},{2,1},{3,0},{0,3},{5,6},{6,5},{7,4},{4,7},{9,10},{10,9},{11,... | collective-permute-start | bytes 12296 | tf_op jit(solution)/shard_map/ppermute | solution.py:432
  88.6 1.3 %collective-permute-done.18.z2 = f32[8,128]{1,0:T(8,128)S(1)} collective-permute-done((f32[8,128]{1,0:T(8,128)S(1)}, f32[8,128]{1,0:T(8,128)S(1)}, u32[]{:S(2)}, u32[]{:S(2)}) %collective-permute-start.18) | collective-permute-done | bytes 4128 | tf_op jit(solution)/shard_map/ppermute | solution.py:432
  89.9 3.6 %shard_map.103 = (f32[3,12,8,128]{3,2,1,0:T(8,128)S(1)}, f32[3,4,8,128]{3,2,1,0:T(8,128)S(1)}, f32[3,8,128]{2,1,0:T(8,128)}) custom-call(s32[6]{0:T(128)S(1)} %convert_element_type.18.flags, f32[22,3,8,128]{3,2,1,0:T(8,128)S(1)} %get-tuple-element.46.force, f32[22,8,128]{2,1,0:T(8,128)S(1)} %get-tuple-element.47.weight, ...), custom_call_target="tpu_custom_call" | custom-call | tf_op jit(solution)/shard_map/pallas_call | solution.py:515
  93.5 6.3 %collective-permute-done.19 = f32[3,4,8,128]{3,2,1,0:T(8,128)S(1)} collective-permute-done((f32[3,4,8,128]{3,2,1,0:T(8,128)S(1)}, f32[3,4,8,128]{3,2,1,0:T(8,128)S(1)}, u32[]{:S(2)}, u32[]{:S(2)}) %collective-permute-start.19) | collective-permute-done | bytes 49184 | tf_op jit(solution)/shard_map/ppermute | solution.py:519
  (65 shorter events, 8.5 us)
Async XLA Ops:
  7.2 19.0 %copy-start.7 = (f32[16,8,128]{2,1,0:T(8,128)S(1)}, f32[16,8,128]{2,1,0:T(8,128)}, u32[]{:S(2)}) copy-start(f32[16,8,128]{2,1,0:T(8,128)} %kappa_in.1) | copy-start | bytes 196612
  7.2 19.0 %copy-start.8 = (s32[16,8,128]{2,1,0:T(8,128)S(1)}, s32[16,8,128]{2,1,0:T(8,128)}, u32[]{:S(2)}) copy-start(s32[16,8,128]{2,1,0:T(8,128)} %agg_in.1) | copy-start | bytes 196612
  7.2 19.0 %copy-start.6 = (f32[3,16,8,128]{3,2,1,0:T(8,128)S(1)}, f32[3,16,8,128]{3,2,1,0:T(8,128)}, u32[]{:S(2)}) copy-start(f32[3,16,8,128]{3,2,1,0:T(8,128)} %force_in.1) | copy-start | bytes 589828
  7.2 54.3 %all-gather.3.cloned.1.call-start = ((), (), s32[]{:S(2)}) async-start(), calls=%async_computation | async-start | bytes 1392640 | tf_op jit(solution)/shard_map/all_gather | solution.py:475
  11.5 14.7 %collective-permute-start = (f32[7,5,8,128]{3,2,1,0:T(8,128)S(1)}, f32[7,5,8,128]{3,2,1,0:T(8,128)S(1)}, u32[]{:S(2)}, u32[]{:S(2)}) collective-permute-start(f32[7,5,8,128]{3,2,1,0:T(8,128)S(1)} %pad_maximum_fusion.1), channel_id=1, source_target_pairs={{0,16},{16,32},{32,48},{48,64},{64,80},{80,96},{96,112},{112,0},{1... | collective-permute-start | bytes 430088 | tf_op jit(solution)/shard_map/ppermute | solution.py:452
  16.6 1.9 %copy-start.4 = (f32[1,1,1,192,4096]{4,3,2,1,0:T(8,128)S(1)}, f32[1,1,1,192,4096]{4,3,2,1,0:T(8,128)}, u32[]{:S(2)}) copy-start(f32[1,1,1,192,4096]{4,3,2,1,0:T(8,128)} %param.10) | copy-start | bytes 9437188
  26.0 12.1 %copy-start = (f32[2,4096,128]{2,1,0:T(8,128)}, f32[2,4096,128]{2,1,0:T(8,128)S(1)}, u32[]{:S(2)}) copy-start(f32[2,4096,128]{2,1,0:T(8,128)S(1)} %get-tuple-element.44.by_col) | copy-start | bytes 12582916
  26.0 12.1 %copy-start.2 = (f32[2,4096,128]{2,1,0:T(8,128)}, f32[2,4096,128]{2,1,0:T(8,128)S(1)}, u32[]{:S(2)}) copy-start(f32[2,4096,128]{2,1,0:T(8,128)S(1)} %get-tuple-element.45.by_row) | copy-start | bytes 12582916
  29.2 8.9 %collective-permute-start.1 = (f32[72,128]{1,0:T(8,128)S(1)}, f32[72,128]{1,0:T(8,128)S(1)}, u32[]{:S(2)}, u32[]{:S(2)}) collective-permute-start(f32[72,128]{1,0:T(8,128)S(1)} %get-tuple-element.54), channel_id=1, source_target_pairs={{0,4},{4,0},{8,12},{12,8},{1,5},{5,1},{9,13},{13,9},{2,6},{6,2},{1... | collective-permute-start | bytes 110600 | tf_op jit(solution)/shard_map/ppermute | solution.py:427
  30.9 7.3 %collective-permute-start.2 = (f32[72,128]{1,0:T(8,128)S(1)}, f32[72,128]{1,0:T(8,128)S(1)}, u32[]{:S(2)}, u32[]{:S(2)}) collective-permute-start(f32[72,128]{1,0:T(8,128)S(1)} %get-tuple-element.55), channel_id=1, source_target_pairs={{4,8},{8,4},{12,0},{0,12},{5,9},{9,5},{13,1},{1,13},{6,10},{10,6},... | collective-permute-start | bytes 110600 | tf_op jit(solution)/shard_map/ppermute | solution.py:430
  33.0 3.7 %collective-permute-start.3 = (f32[16,128]{1,0:T(8,128)S(1)}, f32[16,128]{1,0:T(8,128)S(1)}, u32[]{:S(2)}, u32[]{:S(2)}) collective-permute-start(f32[16,128]{1,0:T(8,128)S(1)} %get-tuple-element.56), channel_id=1, source_target_pairs={{0,1},{1,0},{2,3},{3,2},{4,5},{5,4},{6,7},{7,6},{8,9},{9,8},{10,11... | collective-permute-start | bytes 24584 | tf_op jit(solution)/shard_map/ppermute | solution.py:429
  33.1 5.1 %collective-permute-start.4 = (f32[16,128]{1,0:T(8,128)S(1)}, f32[16,128]{1,0:T(8,128)S(1)}, u32[]{:S(2)}, u32[]{:S(2)}) collective-permute-start(f32[16,128]{1,0:T(8,128)S(1)} %get-tuple-element.57), channel_id=1, source_target_pairs={{1,2},{2,1},{3,0},{0,3},{5,6},{6,5},{7,4},{4,7},{9,10},{10,9},{11,... | collective-permute-start | bytes 24584 | tf_op jit(solution)/shard_map/ppermute | solution.py:432
  41.4 5.9 %collective-permute-start.5 = (f32[72,128]{1,0:T(8,128)S(1)}, f32[72,128]{1,0:T(8,128)S(1)}, u32[]{:S(2)}, u32[]{:S(2)}) collective-permute-start(f32[72,128]{1,0:T(8,128)S(1)} %get-tuple-element.62), channel_id=1, source_target_pairs={{0,4},{4,0},{8,12},{12,8},{1,5},{5,1},{9,13},{13,9},{2,6},{6,2},{1... | collective-permute-start | bytes 110600 | tf_op jit(solution)/shard_map/ppermute | solution.py:427
  42.1 5.2 %collective-permute-start.6 = (f32[72,128]{1,0:T(8,128)S(1)}, f32[72,128]{1,0:T(8,128)S(1)}, u32[]{:S(2)}, u32[]{:S(2)}) collective-permute-start(f32[72,128]{1,0:T(8,128)S(1)} %get-tuple-element.63), channel_id=1, source_target_pairs={{4,8},{8,4},{12,0},{0,12},{5,9},{9,5},{13,1},{1,13},{6,10},{10,6},... | collective-permute-start | bytes 110600 | tf_op jit(solution)/shard_map/ppermute | solution.py:430
  42.7 3.2 %collective-permute-start.7 = (f32[8,128]{1,0:T(8,128)S(1)}, f32[8,128]{1,0:T(8,128)S(1)}, u32[]{:S(2)}, u32[]{:S(2)}) collective-permute-start(f32[8,128]{1,0:T(8,128)S(1)} %get-tuple-element.64), channel_id=1, source_target_pairs={{0,1},{1,0},{2,3},{3,2},{4,5},{5,4},{6,7},{7,6},{8,9},{9,8},{10,11... | collective-permute-start | bytes 12296 | tf_op jit(solution)/shard_map/ppermute | solution.py:429
  42.7 4.6 %collective-permute-start.8 = (f32[8,128]{1,0:T(8,128)S(1)}, f32[8,128]{1,0:T(8,128)S(1)}, u32[]{:S(2)}, u32[]{:S(2)}) collective-permute-start(f32[8,128]{1,0:T(8,128)S(1)} %get-tuple-element.65), channel_id=1, source_target_pairs={{1,2},{2,1},{3,0},{0,3},{5,6},{6,5},{7,4},{4,7},{9,10},{10,9},{11,... | collective-permute-start | bytes 12296 | tf_op jit(solution)/shard_map/ppermute | solution.py:432
  51.4 5.8 %collective-permute-start.9 = (f32[24,128]{1,0:T(8,128)S(1)}, f32[24,128]{1,0:T(8,128)S(1)}, u32[]{:S(2)}, u32[]{:S(2)}) collective-permute-start(f32[24,128]{1,0:T(8,128)S(1)} %get-tuple-element.67), channel_id=1, source_target_pairs={{0,112},{16,0},{32,16},{48,32},{64,48},{80,64},{96,80},{112,96},{1... | collective-permute-start | bytes 36872 | tf_op jit(solution)/shard_map/ppermute | solution.py:500
  57.2 1.2 %collective-permute-start.10 = (f32[24,128]{1,0:T(8,128)S(1)}, f32[24,128]{1,0:T(8,128)S(1)}, u32[]{:S(2)}, u32[]{:S(2)}) collective-permute-start(f32[24,128]{1,0:T(8,128)S(1)} %add.39), channel_id=1, source_target_pairs={{0,1},{1,0},{2,3},{3,2},{4,5},{5,4},{6,7},{7,6},{8,9},{9,8},{10,11... | collective-permute-start | bytes 36872 | tf_op jit(solution)/shard_map/ppermute | solution.py:501
  58.4 5.2 %collective-permute-start.11 = (f32[24,128]{1,0:T(8,128)S(1)}, f32[24,128]{1,0:T(8,128)S(1)}, u32[]{:S(2)}, u32[]{:S(2)}) collective-permute-start(f32[24,128]{1,0:T(8,128)S(1)} %add.40.own), channel_id=1, source_target_pairs={{0,2},{1,3},{2,0},{3,1},{4,6},{5,7},{6,4},{7,5},{8,10},{9,11},{10,... | collective-permute-start | bytes 36872 | tf_op jit(solution)/shard_map/ppermute | solution.py:502
  61.5 1.2 %copy-start.5 = (f32[544,512]{1,0:T(8,128)S(1)}, f32[544,512]{1,0:T(8,128)}, u32[]{:S(2)}) copy-start(f32[544,512]{1,0:T(8,128)} %all-gather.3.cloned.1.call-done) | copy-start | bytes 3342340
  64.2 3.8 %collective-permute-start.12 = (f32[8,512]{1,0:T(8,128)S(1)}, f32[8,512]{1,0:T(8,128)S(1)}, u32[]{:S(2)}, u32[]{:S(2)}) collective-permute-start(f32[8,512]{1,0:T(8,128)S(1)} %shard_map.100.iterate), channel_id=1, source_target_pairs={{0,16},{16,32},{32,48},{48,64},{64,80},{80,96},{96,112},{112,0},{1... | collective-permute-start | bytes 49160 | tf_op jit(solution)/shard_map/ppermute | solution.py:506
  69.0 4.0 %collective-permute-start.13 = (f32[72,128]{1,0:T(8,128)S(1)}, f32[72,128]{1,0:T(8,128)S(1)}, u32[]{:S(2)}, u32[]{:S(2)}) collective-permute-start(f32[72,128]{1,0:T(8,128)S(1)} %get-tuple-element.72), channel_id=1, source_target_pairs={{0,4},{4,0},{8,12},{12,8},{1,5},{5,1},{9,13},{13,9},{2,6},{6,2},{1... | collective-permute-start | bytes 110600 | tf_op jit(solution)/shard_map/ppermute | solution.py:427
  70.3 5.2 %collective-permute-start.14 = (f32[72,128]{1,0:T(8,128)S(1)}, f32[72,128]{1,0:T(8,128)S(1)}, u32[]{:S(2)}, u32[]{:S(2)}) collective-permute-start(f32[72,128]{1,0:T(8,128)S(1)} %get-tuple-element.73), channel_id=1, source_target_pairs={{4,8},{8,4},{12,0},{0,12},{5,9},{9,5},{13,1},{1,13},{6,10},{10,6},... | collective-permute-start | bytes 110600 | tf_op jit(solution)/shard_map/ppermute | solution.py:430
  75.4 2.2 %copy-start.1 = (f32[2,4096,128]{2,1,0:T(8,128)S(1)}, f32[2,4096,128]{2,1,0:T(8,128)}, u32[]{:S(2)}) copy-start(f32[2,4096,128]{2,1,0:T(8,128)} %copy-done) | copy-start | bytes 12582916
  77.6 2.2 %copy-start.3 = (f32[2,4096,128]{2,1,0:T(8,128)S(1)}, f32[2,4096,128]{2,1,0:T(8,128)}, u32[]{:S(2)}) copy-start(f32[2,4096,128]{2,1,0:T(8,128)} %copy-done.2) | copy-start | bytes 12582916
  83.0 6.9 %collective-permute-start.15 = (f32[72,128]{1,0:T(8,128)S(1)}, f32[72,128]{1,0:T(8,128)S(1)}, u32[]{:S(2)}, u32[]{:S(2)}) collective-permute-start(f32[72,128]{1,0:T(8,128)S(1)} %get-tuple-element.79), channel_id=1, source_target_pairs={{0,4},{4,0},{8,12},{12,8},{1,5},{5,1},{9,13},{13,9},{2,6},{6,2},{1... | collective-permute-start | bytes 110600 | tf_op jit(solution)/shard_map/ppermute | solution.py:427
  83.1 6.8 %collective-permute-start.16 = (f32[72,128]{1,0:T(8,128)S(1)}, f32[72,128]{1,0:T(8,128)S(1)}, u32[]{:S(2)}, u32[]{:S(2)}) collective-permute-start(f32[72,128]{1,0:T(8,128)S(1)} %get-tuple-element.80), channel_id=1, source_target_pairs={{4,8},{8,4},{12,0},{0,12},{5,9},{9,5},{13,1},{1,13},{6,10},{10,6},... | collective-permute-start | bytes 110600 | tf_op jit(solution)/shard_map/ppermute | solution.py:430
  85.4 3.2 %collective-permute-start.17 = (f32[8,128]{1,0:T(8,128)S(1)}, f32[8,128]{1,0:T(8,128)S(1)}, u32[]{:S(2)}, u32[]{:S(2)}) collective-permute-start(f32[8,128]{1,0:T(8,128)S(1)} %get-tuple-element.81), channel_id=1, source_target_pairs={{0,1},{1,0},{2,3},{3,2},{4,5},{5,4},{6,7},{7,6},{8,9},{9,8},{10,11... | collective-permute-start | bytes 12296 | tf_op jit(solution)/shard_map/ppermute | solution.py:429
  85.4 4.5 %collective-permute-start.18 = (f32[8,128]{1,0:T(8,128)S(1)}, f32[8,128]{1,0:T(8,128)S(1)}, u32[]{:S(2)}, u32[]{:S(2)}) collective-permute-start(f32[8,128]{1,0:T(8,128)S(1)} %get-tuple-element.82), channel_id=1, source_target_pairs={{1,2},{2,1},{3,0},{0,3},{5,6},{6,5},{7,4},{4,7},{9,10},{10,9},{11,... | collective-permute-start | bytes 12296 | tf_op jit(solution)/shard_map/ppermute | solution.py:432
  93.5 6.3 %collective-permute-start.19 = (f32[3,4,8,128]{3,2,1,0:T(8,128)S(1)}, f32[3,4,8,128]{3,2,1,0:T(8,128)S(1)}, u32[]{:S(2)}, u32[]{:S(2)}) collective-permute-start(f32[3,4,8,128]{3,2,1,0:T(8,128)S(1)} %get-tuple-element.84), channel_id=1, source_target_pairs={{0,112},{16,0},{32,16},{48,32},{64,48},{80,64},{96,80},{112,96},{1... | collective-permute-start | bytes 147464 | tf_op jit(solution)/shard_map/ppermute | solution.py:519
Sparse Core Ops, SparseCore 0:
  9.7 23.6 all-gather.2
where the time goes:
time: 108 us; the launch traced here: 107 us
  starting transfers between devices  26.8 us (25%)
  Pallas kernels  26.5 us (25%)
  waiting for transfers between devices  23.9 us (22%)
  between operations  14.2 us (13%)
  local copies, waits for them, and re-layouts  11 us (10%)
  other arithmetic  4.8 us (4%)
    ppermute x3, starting transfers between devices, trade(): got_z.append(lax.ppermute(z2, 'gz', swaps('gz', 1)))  10.1 us
    unnamed x21, local copies, waits for them, and re-layouts  8.92 us
    pallas_call x1, Pallas kernels, shards(): call(prepare_kernel, [((2, 4096, 128), F32)] * 2, [pltpu.VMEM((192, 128),...  7.44 us
    ppermute x4, starting transfers between devices, trade(): got.append(lax.ppermute(y2, 'gy', swaps('gy', 1)))  7.23 us
    ppermute x1, waiting for transfers between devices, shards(): tail = lax.ppermute(tail, 'gx', ring('gx', -1))  6.26 us
    ppermute x1, waiting for transfers between devices, shards(): total = own + lax.ppermute(prev, 'gx', ring('gx', -1))  5.3 us
    pallas_call x1, Pallas kernels, shards(): call(restrict_kernel, [((24, 128), F32)] * 2, [pltpu.VMEM((NP, 3, 8, 128)...  4.05 us
    ppermute x3, waiting for transfers between devices, trade(): got_z.append(lax.ppermute(z2, 'gz', swaps('gz', 1)))  4.01 us
  transfers between devices with their start and end apart: 21, of which 10 were waited for; matrix products, arithmetic and copies ran while one was open for 5% of the time, Pallas kernels for 17%

commit v1 on v0

v1 whole, which is shorter than its diff:
```python
import functools

import jax
import jax.numpy as jnp
from jax import lax
from jax.experimental import pallas as pl
from jax.experimental.pallas import tpu as pltpu
from jax.sharding import PartitionSpec as P

BLK = 64
NAGG = 512
TAIL = 7
HEAD = 15
NP = TAIL + HEAD
ROWS = 24
LINES = 3 * ROWS
LOW = TAIL
UPP = TAIL - 1
RET = 4
COARSE_OMEGA = 0.8
PROLONG_GAIN = 0.5
F32 = jnp.float32
BF16 = jnp.bfloat16

VMEM = pl.BlockSpec(memory_space=pltpu.VMEM)
SMEM = pl.BlockSpec(memory_space=pltpu.SMEM)
HBM = pl.BlockSpec(memory_space=pltpu.HBM)


def keep(x):
    return pltpu.with_memory_space_constraint(x, pltpu.VMEM)


def call(body, outs, scratch=(), n_smem=0, n_in=0, n_far=0, limit=12, results=()):
    kernel = pl.pallas_call(
        body,
        out_shape=[jax.ShapeDtypeStruct(s, d) if i in results else pltpu.VMEM(s, d) for i, (s, d) in enumerate(outs)],
        in_specs=[SMEM] * n_smem + [VMEM] * n_in + [HBM] * n_far,
        out_specs=[VMEM] * len(outs),
        scratch_shapes=list(scratch),
        compiler_params=pltpu.CompilerParams(vmem_limit_bytes=limit * 1024 * 1024),
    )

    def run(*args):
        near = n_smem + n_in
        far = [pltpu.with_memory_space_constraint(x, pltpu.HBM) for x in args[near:]]
        held = [keep(x) for x in args[n_smem:near]]
        return kernel(*args[:n_smem], *held, *far)

    return run


def prepare_kernel(flags, blocks, index, count, by_row, spots, place, near, piece, lists, index_near, count_near, sems):
    copies = [
        pltpu.make_async_copy(blocks.at[:, pl.ds(1024 * i, 1024)], near.at[i], sems.at[i]) for i in range(4)
    ]
    for copy in copies:
        copy.start()
    zero = jnp.zeros((8, 128), F32)
    lane = lax.broadcasted_iota(jnp.int32, (8, 128), 1)
    spot = lane & 31
    source = jnp.where(spot < 24, 2 * spot + (lax.shift_right_logical(lane, 5) & 1), 0)
    lists[...] = jnp.zeros((8, 128), jnp.int32)
    small = [
        pltpu.make_async_copy(index, index_near, sems.at[4]),
        pltpu.make_async_copy(count, count_near, sems.at[5]),
    ]
    for copy in small:
        copy.start()
    for copy in small:
        copy.wait()
    lists[0:4, 0:48] = index_near[...]
    lists[4:5, 0:48] = count_near[...]

    def pick(row):
        full = jnp.broadcast_to(lists[row : row + 1, :], (8, 128))
        return jnp.take_along_axis(full, source, axis=1, mode="promise_in_bounds")

    used = pick(4)
    down = lax.broadcasted_iota(jnp.int32, (128, 128), 0) & 63
    for tile in range(2):
        k = 2 * tile + lax.shift_right_logical(lane, 6)
        block = jnp.where(lane < 64, pick(2 * tile), pick(2 * tile + 1))
        at = (block & 1) * 32 + lax.shift_right_logical(block, 1)
        live = (k < used) & (spot < 24)
        at = jnp.where(live, at, 31)
        spots[:, 128 * tile : 128 * tile + 128] = at
        hit = (down == at[0:1]) & (at[0:1] != 31)
        place[:, 128 * tile : 128 * tile + 128] = jnp.where(hit, 1.0, 0.0).astype(BF16)

    for i, copy in enumerate(copies):
        copy.wait()

        def chunk(g, _):
            for s in range(2):
                at = pl.multiple_of((2 * g + s) * 128, 128)
                piece[s] = near[i, :, pl.ds(at, 128)]
                for tile in range(2):
                    rows = []
                    for k in (2 * tile, 2 * tile + 1):
                        for par in range(2):
                            rows += [piece[s, pl.ds(4 * par + k, 24, stride=8), :], zero]
                    by_row[tile, pl.ds(1024 * i + at, 128), :] = jnp.concatenate(rows, 0).T
            return 0

        lax.fori_loop(0, 4, chunk, 0)


def split(x):
    high = x.astype(BF16)
    return high, (x - high.astype(F32)).astype(BF16)


def fold(parts):
    sub = lax.broadcasted_iota(jnp.int32, (8, 128), 0)
    m = sub < 4
    a = [
        jnp.where(m, parts[i], parts[i + 4]) + pltpu.roll(jnp.where(m, parts[i + 4], parts[i]), 4, 0)
        for i in range(4)
    ]
    m = (sub & 2) == 0
    a = [
        jnp.where(m, a[i], pltpu.roll(a[i + 2], 2, 0)) + jnp.where(m, pltpu.roll(a[i], 6, 0), a[i + 2])
        for i in range(2)
    ]
    m = (sub & 1) == 0
    return jnp.where(m, a[0], pltpu.roll(a[1], 1, 0)) + jnp.where(m, pltpu.roll(a[0], 7, 0), a[1])


def project(by_row, spots, values):
    total = None
    for tile in range(2):
        picked = [
            jnp.take_along_axis(
                values[8 * g : 8 * g + 8], spots[:, 128 * tile : 128 * tile + 128], axis=1,
                mode="promise_in_bounds",
            )
            for g in range(8)
        ]
        rows = []
        for group in range(8):
            parts = []
            for s in range(8):
                base = 64 * (8 * group + s)
                terms = [by_row[tile, base + 8 * g : base + 8 * g + 8, :] * picked[g] for g in range(8)]
                while len(terms) > 1:
                    terms = [terms[i] + terms[i + 1] for i in range(0, len(terms), 2)]
                parts.append(terms[0])
            rows.append(fold(parts))
        part = jnp.concatenate(rows, 0)
        total = part if total is None else total + part
    return total + pltpu.roll(total, 64, 1)


def project_back(by_row, place, values):
    first = second = jnp.zeros((64, 128), F32)
    for i in range(64):
        row = jnp.broadcast_to(values[i : i + 1], (64, 128))
        first = first + by_row[0, 64 * i : 64 * i + 64, :] * row
        second = second + by_row[1, 64 * i : 64 * i + 64, :] * row
    high, low = split(jnp.concatenate([first, second], 1))
    both = lax.dot_general(
        jnp.concatenate([high, low], 0), place[...], (((1,), (1,)), ((), ())), preferred_element_type=F32
    )
    return both[0:64] + both[64:128]


def turn(lower, upper):
    left = lax.broadcasted_iota(jnp.int32, (24, 128), 1) < 64
    even = jnp.where(left, lower, pltpu.roll(upper, 64, 1))
    odd = jnp.where(left, pltpu.roll(lower, 64, 1), upper)
    zero = jnp.zeros((8, 128), F32)
    turned = jnp.concatenate([even, zero, odd, zero, even, zero, odd, zero], 0).T
    return turned[0:64], turned[64:128]


def turn_back(lower, upper):
    left = lax.broadcasted_iota(jnp.int32, (24, 128), 1) < 64
    rows = jnp.concatenate([lower, upper], 0).T
    even, odd = rows[0:24], rows[32:56]
    return (
        jnp.where(left, even, pltpu.roll(odd, 64, 1)),
        jnp.where(left, pltpu.roll(even, 64, 1), odd),
    )


def solve_interface(lower, upper, face, inverse, mortar):
    by_row, spots, place = mortar
    low_t, upp_t = turn(lower, upper)
    rhs = low_t - project(by_row, spots, upp_t)
    first = face * rhs
    back = project_back(by_row, place, first) * inverse
    rest = 0.6 * rhs - project(by_row, spots, back)
    increment = first + face * rest
    return turn_back(increment, project_back(by_row, place, increment))


def tall(plane):
    return jnp.concatenate([plane] * 3, 0)


def yes(flags, row, shape):
    line = jnp.concatenate([flags[row : row + 1, :]] * (shape[1] // 128), 1)
    return jnp.broadcast_to(line, shape) == 1


def sides(flags, y_first, y_second, z_first, z_second):
    tall_shape, zero = (LINES, 128), jnp.zeros((LINES, 128), F32)
    y_even, z_even = yes(flags, 0, tall_shape), yes(flags, 1, (8, 128))
    a, b, c, d = y_first[0:LINES], y_second[0:LINES], z_first[0:8], z_second[0:8]
    return (
        jnp.where(yes(flags, 2, tall_shape), jnp.where(y_even, b, a), zero),
        jnp.where(yes(flags, 3, tall_shape), jnp.where(y_even, a, b), zero),
        jnp.where(yes(flags, 4, (8, 128)), jnp.where(z_even, d, c), zero[0:8]),
        jnp.where(yes(flags, 5, (8, 128)), jnp.where(z_even, c, d), zero[0:8]),
    )


def place_of(p, c):
    return ROWS * c + p


def residual_of(p, c, force, weight, velocity, halo):
    y_low, y_high, z_low, z_high = halo
    i = place_of(p, c)
    sub = lax.broadcasted_iota(jnp.int32, (8, 128), 0)
    lane = lax.broadcasted_iota(jnp.int32, (8, 128), 1)
    v = velocity[p, c]
    total = force[p, c] - weight[p] * v
    if p not in (0, LOW):
        total = total + velocity[p - 1, c]
    if p not in (NP - 1, UPP):
        total = total + velocity[p + 1, c]
    total = total + jnp.where(sub == 0, y_low[i : i + 1], pltpu.roll(v, 1, 0))
    total = total + jnp.where(sub == 7, y_high[i : i + 1], pltpu.roll(v, 7, 0))
    total = total + jnp.where(lane == 0, pltpu.roll(z_low, (128 - i) % 128, 1), pltpu.roll(v, 1, 1))
    total = total + jnp.where(lane == 127, pltpu.roll(z_high, 127 - i, 1), pltpu.roll(v, 127, 1))
    return total


def write_lines(flags, get, y_first, y_second, row=0, count=3):
    y_even = yes(flags, 0, (1, 128))
    for c in range(count):
        for p in range(NP):
            v = get(p, c)
            i = row + place_of(p, c)
            y_first[i : i + 1] = jnp.where(y_even, v[7:8], v[0:1])
            y_second[i : i + 1] = jnp.where(y_even, v[0:1], v[7:8])
        i = row + place_of(NP, c)
        y_first[i : i + ROWS - NP] = jnp.zeros((ROWS - NP, 128), F32)
        y_second[i : i + ROWS - NP] = jnp.zeros((ROWS - NP, 128), F32)


def write_columns(flags, get, z_first, z_second, row=0):
    z_even = yes(flags, 1, (8, 128))
    lane = lax.broadcasted_iota(jnp.int32, (8, 128), 1)
    first = jnp.zeros((8, 128), F32)
    last = first
    for c in range(3):
        for p in range(NP):
            v, i = get(p, c), place_of(p, c)
            first = jnp.where(lane == i, pltpu.roll(v, i, 1) if i else v, first)
            last = jnp.where(lane == i, pltpu.roll(v, i + 1, 1), last)
    z_first[row : row + 8] = jnp.where(z_even, last, first)
    z_second[row : row + 8] = jnp.where(z_even, first, last)


def first_sweep_kernel(
    flags, force_in, kappa_in, agg_in, tail, by_row, spots, place,
    force, weight, inverse, agg, velocity, mult, mult_up, face, inverse_t, y1, y2, z1, z2,
):
    for p in range(NP):
        here = p - TAIL
        kappa = tail[p, 3] if here < 0 else kappa_in[here]
        w = 6.0 + kappa
        weight[p] = w
        inverse[p] = 1.0 / (1.5 * w)
        agg[p] = tail[p, 4].astype(jnp.int32) if here < 0 else agg_in[here]
        for c in range(3):
            f = tail[p, c] if here < 0 else force_in[c, here]
            force[p, c] = f
            velocity[p, c] = f * inverse[p]
    low_w, upp_inv = turn(tall(weight[LOW]), tall(inverse[UPP]))
    face[...] = 0.6 * low_w
    inverse_t[...] = upp_inv
    lower = velocity[LOW].reshape(24, 128)
    upper = velocity[UPP].reshape(24, 128)
    increment, pulled = solve_interface(
        lower, upper, face[...], upp_inv, (by_row, spots, place)
    )
    mult[...] = increment.reshape(3, 8, 128)
    mult_up[...] = pulled.reshape(3, 8, 128)
    velocity[LOW] = (lower - increment * tall(inverse[LOW])).reshape(3, 8, 128)
    velocity[UPP] = (upper + pulled * tall(inverse[UPP])).reshape(3, 8, 128)
    get = lambda p, c: velocity[p, c]
    write_lines(flags, get, y1, y2)
    write_columns(flags, get, z1, z2)
    label = lambda p, c: agg[p].astype(F32)
    write_lines(flags, label, y1, y2, LINES, 1)
    write_columns(flags, label, z1, z2, 8)


def sweep(
    flags, force, weight, inverse, velocity, mult, mult_up, face, inverse_t, by_row, spots, place,
    halo, out, out_mult, out_up,
):
    def residuals(p):
        return jnp.concatenate([residual_of(p, c, force, weight, velocity, halo) for c in range(3)], 0)

    res_low = residuals(LOW) - mult[...].reshape(24, 128)
    res_upp = residuals(UPP) + mult_up[...].reshape(24, 128)
    inv_low, inv_upp = tall(inverse[LOW]), tall(inverse[UPP])
    lower = velocity[LOW].reshape(24, 128) + res_low * inv_low
    upper = velocity[UPP].reshape(24, 128) + res_upp * inv_upp
    increment, pulled = solve_interface(
        lower, upper, face[...], inverse_t[...], (by_row, spots, place)
    )
    out_mult[...] = mult[...] + increment.reshape(3, 8, 128)
    out_up[...] = mult_up[...] + pulled.reshape(3, 8, 128)
    for p in range(NP):
        if p in (LOW, UPP):
            continue
        for c in range(3):
            out[p, c] = velocity[p, c] + residual_of(p, c, force, weight, velocity, halo) * inverse[p]
    out[LOW] = (lower - increment * inv_low).reshape(3, 8, 128)
    out[UPP] = (upper + pulled * inv_upp).reshape(3, 8, 128)


def second_sweep_kernel(
    flags, force, weight, inverse, velocity, mult, mult_up, face, inverse_t, by_row, spots, place,
    y1, y2, z1, z2, out, out_mult, out_up, oy1, oy2, oz1, oz2,
):
    halo = sides(flags, y1, y2, z1, z2)
    sweep(
        flags, force, weight, inverse, velocity, mult, mult_up, face, inverse_t, by_row, spots, place,
        halo, out, out_mult, out_up,
    )
    get = lambda p, c: out[p, c]
    write_lines(flags, get, oy1, oy2)
    write_columns(flags, get, oz1, oz2)


def third_sweep_kernel(
    flags, force, weight, inverse, old, mult, mult_up, face, inverse_t, by_row, spots, place,
    y1, y2, z1, z2, ay1, ay2, az1, az2, agg, iterate, got, swapped,
    out, out_mult, out_up, oy1, oy2, oz1, oz2, velocity,
):
    core_zero = yes(flags, 1, (24, NAGG))
    a = jnp.where(core_zero, got[...], swapped[...])
    b = jnp.where(core_zero, swapped[...], got[...])
    own, prev = table(iterate[...]), table(a[0:8])
    low, low_prev = table(b[0:8]), table(b[8:16])
    high, high_prev = table(a[8:16]), table(a[16:24])
    for p in range(NP):
        at = where_in(agg[p])
        for c in range(3):
            velocity[p, c] = old[p, c] + pick((prev if p < TAIL else own)[c], at)

    y_low, y_high, z_low, z_high = sides(flags, y1, y2, z1, z2)
    y_even, z_even = yes(flags, 0, (ROWS, 128)), yes(flags, 1, (8, 128))
    ay1, ay2, az1, az2 = ay1[LINES : LINES + ROWS], ay2[LINES : LINES + ROWS], az1[8:16], az2[8:16]
    sub = lax.broadcasted_iota(jnp.int32, (8, 128), 0)
    lane = lax.broadcasted_iota(jnp.int32, (8, 128), 1)

    def lines(values, labels, mine, below, flag):
        labels = labels.astype(jnp.int32)
        parts = []
        for c in range(3):
            for block in range(ROWS // 8):
                at = where_in(labels[8 * block : 8 * block + 8])
                extra = pick(mine[c], at)
                if block == 0:
                    extra = jnp.where(sub < TAIL, pick(below[c], at), extra)
                row = place_of(8 * block, c)
                parts.append(jnp.where(yes(flags, flag, (8, 128)), values[row : row + 8] + extra, 0.0))
        return jnp.concatenate(parts, 0)

    def column(values, labels, flag):
        at = where_in(labels.astype(jnp.int32))
        extra = jnp.zeros((8, 128), F32)
        for c in range(3):
            here = lane - ROWS * c
            extra = jnp.where((here >= 0) & (here < TAIL), pick(prev[c], at), extra)
            extra = jnp.where((here >= TAIL) & (here < NP), pick(own[c], at), extra)
        return jnp.where(yes(flags, flag, (8, 128)), values + extra, 0.0)

    halo = (
        lines(y_low, jnp.where(y_even, ay2, ay1), low, low_prev, 2),
        lines(y_high, jnp.where(y_even, ay1, ay2), high, high_prev, 3),
        column(z_low, jnp.where(z_even, az2, az1), 4),
        column(z_high, jnp.where(z_even, az1, az2), 5),
    )
    sweep(
        flags, force, weight, inverse, velocity, mult, mult_up, face, inverse_t, by_row, spots, place,
        halo, out, out_mult, out_up,
    )
    get = lambda p, c: out[p, c]
    write_lines(flags, get, oy1, oy2)
    write_columns(flags, get, oz1, oz2)


def last_sweep_kernel(
    flags, force, weight, inverse, velocity, mult, mult_up, face, inverse_t, by_row, spots, place,
    y1, y2, z1, z2, head, tail, out_mult, out, out_up,
):
    halo = sides(flags, y1, y2, z1, z2)
    sweep(
        flags, force, weight, inverse, velocity, mult, mult_up, face, inverse_t, by_row, spots, place,
        halo, out, out_mult, out_up,
    )
    for c in range(3):
        for p in range(16 - RET):
            head[c, p] = out[LOW + p, c]
        for p in range(RET):
            tail[c, p] = out[TAIL - RET + p, c]


def restrict_kernel(
    flags, force, weight, velocity, mult, mult_up, agg, diag, y1, y2, z1, z2, out, res,
):
    halo = sides(flags, y1, y2, z1, z2)
    for p in range(TAIL - 3, NP - 2):
        for c in range(3):
            r = residual_of(p, c, force, weight, velocity, halo)
            if p == LOW:
                r = r - mult[c]
            if p == UPP:
                r = r + mult_up[c]
            res[p, c] = r
    down = lax.broadcasted_iota(jnp.int32, (64, 128), 0)
    sub = lax.broadcasted_iota(jnp.int32, (8, 128), 0)

    def plane(p, total):
        labels = agg[p]
        lows = labels & 63
        highs = lax.shift_right_logical(labels, 6)
        values = []
        for c in range(3):
            r = res[p, c]
            high = r.astype(BF16).astype(F32)
            values += [high, r - high]
        for pair in range(4):
            tables, terms = [], []
            for y in (2 * pair, 2 * pair + 1):
                tables.append(jnp.where(down == lows[y : y + 1], 1.0, 0.0).astype(BF16))
                here = highs[y : y + 1] == sub
                terms.append(jnp.concatenate([jnp.where(here, v[y : y + 1], 0.0) for v in values], 0).astype(BF16))
            total = total + lax.dot_general(
                jnp.concatenate(tables, 1), jnp.concatenate(terms, 1), (((1,), (1,)), ((), ())),
                preferred_element_type=F32,
            )
        return total

    def four(i, total):
        for s in range(4):
            total = plane(LOW + 4 * i + s, total)
        return total

    below = jnp.zeros((64, 48), F32)
    for p in range(TAIL - 3, TAIL):
        below = plane(p, below)
    own = lax.fori_loop(0, 3, four, plane(NP - 3, jnp.zeros((64, 48), F32)))
    both = jnp.concatenate([own, below], 0)
    turned = jnp.concatenate([both, jnp.zeros((128, 80), F32)], 1).T
    for c in range(3):
        out[8 * c : 8 * c + 8] = turned[16 * c : 16 * c + 8] + turned[16 * c + 8 : 16 * c + 16]
    out[24:32] = jnp.where(sub == flags[6:7], jnp.broadcast_to(diag[...], (8, 128)), 0.0)


def gather_sums_kernel(flags, mine, first, second, kept, passed):
    core_zero = yes(flags, 1, (32, 128))
    across = jnp.where(core_zero, first[...], second[...])
    above = jnp.where(core_zero, second[...], first[...])
    kept[...] = mine[...] + across
    lane = lax.broadcasted_iota(jnp.int32, (24, 128), 1)
    passed[...] = jnp.where(lane < 64, pltpu.roll(above[0:24], 64, 1), 0.0)


def add_kernel(one, two, out):
    out[...] = one[...] + two[...]


def join_kernel(a, b, c, after, out):
    out[0:8], out[8:16], out[16:24] = a[...], b[...], c[...]


def add(one, two):
    return call(add_kernel, [(one.shape, F32)], n_in=2)(one, two)[0]


def pack_kernel(force, kappa, agg, out, force_near, kappa_near, agg_near, flags, sems):
    copies = [
        pltpu.make_async_copy(far, near, sems.at[i])
        for i, (far, near) in enumerate(((force, force_near), (kappa, kappa_near), (agg, agg_near)))
    ]
    for copy in copies:
        copy.start()
    gy, gz = lax.axis_index("gy"), lax.axis_index("gz")
    ny, nz = lax.axis_size("gy"), lax.axis_size("gz")
    facts = (gy % 2 == 0, gz % 2 == 0, gy > 0, gy < ny - 1, gz > 0, gz < nz - 1, gz, gz)
    for row, fact in enumerate(facts):
        flags[row : row + 1, :] = jnp.full((1, 128), fact.astype(jnp.int32), jnp.int32)
    for copy in copies:
        copy.wait()
    start = kappa.shape[0] - TAIL
    for p in range(TAIL):
        for c in range(3):
            out[p, c] = force_near[c, start + p]
        out[p, 3] = kappa_near[start + p]
        out[p, 4] = agg_near[start + p].astype(F32)


def split_matrix_kernel(rows, high, low):
    a = rows[...].T
    h = a.astype(BF16)
    high[...] = h
    low[...] = (a - h.astype(F32)).astype(BF16)


def solve_kernel(kept, passed, swapped, high, low, out, rhs):
    sums = kept[0:24] + passed[...] + swapped[...]
    other = pltpu.roll(sums, 64, 1)
    rhs[...] = jnp.zeros((8, NAGG), F32)
    left = lax.broadcasted_iota(jnp.int32, (1, 128), 1) < 64
    for c in range(3):
        for t in range(4):
            at = 8 * c + 2 * t
            rhs[c : c + 1, 128 * t : 128 * t + 128] = jnp.where(left, sums[at : at + 1], other[at + 1 : at + 2])
    gain = (16 * 8 * 512 / NAGG) ** -0.5
    scale = jnp.concatenate([kept[24 + b : 25 + b] for b in range(4)], 1)
    step = jnp.broadcast_to(COARSE_OMEGA / scale, (8, NAGG))
    start = (rhs[...] * gain) * step
    x = start
    for _ in range(3):
        xh, xl = split(x)
        both = jnp.concatenate([xh, xl], 0)
        first = jnp.dot(both, high[...], preferred_element_type=F32)
        second = jnp.dot(xh, low[...], preferred_element_type=F32)
        product = first[0:8] + first[8:16] + second
        x = (1.0 - COARSE_OMEGA) * x + (start - step * product)
    out[...] = x


def table(rows):
    return [
        [jnp.broadcast_to(rows[c : c + 1, 128 * t : 128 * t + 128], (8, 128)) * PROLONG_GAIN for t in range(4)]
        for c in range(3)
    ]


def where_in(labels):
    return labels & 127, lax.shift_right_logical(labels, 7)


def pick(rows, at):
    lane, tile = at
    got = [jnp.take_along_axis(row, lane, axis=1, mode="promise_in_bounds") for row in rows]
    return jnp.where(tile < 2, jnp.where(tile == 0, got[0], got[1]), jnp.where(tile == 2, got[2], got[3]))


def reload_kernel(after, far, near, sem):
    copy = pltpu.make_async_copy(far, near, sem)
    copy.start()
    copy.wait()


def ring(axis, by):
    n = lax.axis_size(axis)
    return [(i, (i + by) % n) for i in range(n)]


def swaps(axis, first):
    n = lax.axis_size(axis)
    pairs = []
    for i in range(first, first + n, 2):
        a, b = i % n, (i + 1) % n
        pairs += [(a, b), (b, a)]
    return pairs


def trade(y1, y2, z1, z2):
    got_z = lax.ppermute(z2, "gz", swaps("gz", 1))
    got = [lax.ppermute(y1, "gy", swaps("gy", 0)), lax.ppermute(y2, "gy", swaps("gy", 1))]
    return got + [lax.ppermute(z1, "gz", swaps("gz", 0)), got_z]


def by_core(x, rule_zero, rule_one):
    nx, ny, nz = lax.axis_size("gx"), lax.axis_size("gy"), lax.axis_size("gz")
    pairs = []
    for g in range(nx):
        for y in range(ny):
            for z in range(nz):
                dx, dy, dz = rule_one if z % 2 else rule_zero
                to = (((g + dx) % nx) * ny + (y + dy) % ny) * nz + (z + dz) % nz
                pairs.append(((g * ny + y) * nz + z, to))
    return lax.ppermute(x, ("gx", "gy", "gz"), pairs)


def shards(force, kappa, mortar_blocks, mortar_index, mortar_count, agg_map, coarse_matrix, coarse_diag):
    tail_in, force, kappa, agg_map, flags = call(
        pack_kernel,
        [((TAIL, 5, 8, 128), F32), (force.shape, F32), (kappa.shape, F32), (agg_map.shape, jnp.int32),
         ((8, 128), jnp.int32)],
        [pltpu.SemaphoreType.DMA((3,))],
        n_far=3,
    )(force, kappa, agg_map)
    rows, flags = lax.optimization_barrier((coarse_matrix.reshape(128, NAGG), flags))
    rows = lax.all_gather(rows, "gz", tiled=True)
    tail_in = lax.ppermute(tail_in, "gx", ring("gx", 1))

    by_row, spots, place = call(
        prepare_kernel,
        [((2, 4096, 128), F32), ((8, 256), jnp.int32), ((128, 256), BF16)],
        [pltpu.VMEM((4, 192, 1024), F32), pltpu.VMEM((2, 192, 128), F32), pltpu.VMEM((8, 128), jnp.int32),
         pltpu.VMEM((4, 48), jnp.int32), pltpu.VMEM((1, 48), jnp.int32), pltpu.SemaphoreType.DMA((6,))],
        n_in=1,
        n_far=3,
    )(
        flags,
        mortar_blocks.reshape(192, 4096),
        jnp.transpose(mortar_index.reshape(48, 4), (1, 0)),
        mortar_count.reshape(1, 48),
    )

    k_high, k_low = call(split_matrix_kernel, [((NAGG, NAGG), BF16)] * 2, n_in=1)(rows)
    by_row_again = call(
        reload_kernel, [((2, 4096, 128), F32)], [pltpu.SemaphoreType.DMA], n_in=1, n_far=1
    )(k_high, by_row)[0]

    field = ((NP, 3, 8, 128), F32)
    plane = ((3, 8, 128), F32)
    turned = ((64, 128), F32)
    y_msg, z_msg = ((LINES, 128), F32), ((8, 128), F32)
    y_more, z_more = ((LINES + ROWS, 128), F32), ((16, 128), F32)
    out = call(
        first_sweep_kernel,
        [field, ((NP, 8, 128), F32), ((NP, 8, 128), F32), ((NP, 8, 128), jnp.int32), field, plane, plane,
         turned, turned, y_more, y_more, z_more, z_more],
        n_in=8,
    )(flags, force, kappa, agg_map, tail_in, by_row, spots, place)
    force_e, weight, inverse, agg, velocity, mult, mult_up, face, inverse_t = out[:9]
    labels = trade(*out[9:])
    velocity, mult, mult_up, *msgs = call(
        second_sweep_kernel, [field, plane, plane, y_msg, y_msg, z_msg, z_msg], n_in=16
    )(flags, force_e, weight, inverse, velocity, mult, mult_up, face, inverse_t, by_row, spots, place, *labels)
    edges = trade(*msgs)
    sums = call(
        restrict_kernel, [((32, 128), F32)], [pltpu.VMEM((NP, 3, 8, 128), F32)], n_in=12
    )(flags, force_e, weight, velocity, mult, mult_up, agg, coarse_diag.reshape(1, 128), *edges)[0]
    sums = add(sums, lax.ppermute(sums, "gz", swaps("gz", 0)))
    first = by_core(sums, (0, 0, 2), (-1, 0, 0))
    second = by_core(sums, (-1, 0, 2), (0, 0, 2))
    kept, passed = call(gather_sums_kernel, [((32, 128), F32), ((24, 128), F32)], n_in=4)(flags, sums, first, second)
    swapped = lax.ppermute(passed, "gz", swaps("gz", 0))
    iterate = call(solve_kernel, [((8, NAGG), F32)], [pltpu.VMEM((8, NAGG), F32)], n_in=5)(
        kept, passed, swapped, k_high, k_low
    )[0]
    got = [
        by_core(iterate, (1, 0, 0), (0, 1, 0)),
        by_core(iterate, (0, -1, 0), (1, 1, 0)),
        by_core(iterate, (1, -1, 0), (1, 0, 0)),
    ]
    got = call(join_kernel, [((24, NAGG), F32)], n_in=4)(*got, by_row_again)[0]
    swapped = lax.ppermute(got, "gz", swaps("gz", 0))
    velocity, mult, mult_up, *msgs = call(
        third_sweep_kernel, [field, plane, plane, y_msg, y_msg, z_msg, z_msg],
        [pltpu.VMEM((NP, 3, 8, 128), F32)], n_in=24,
    )(
        flags, force_e, weight, inverse, velocity, mult, mult_up, face, inverse_t, by_row_again, spots, place,
        *edges, *labels, agg, iterate, got, swapped,
    )
    edges = trade(*msgs)
    head, tail, mult = call(
        last_sweep_kernel, [((3, 16 - RET, 8, 128), F32), ((3, RET, 8, 128), F32), plane],
        [pltpu.VMEM((NP, 3, 8, 128), F32), pltpu.VMEM((3, 8, 128), F32)], n_in=16, results=(0, 2),
    )(flags, force_e, weight, inverse, velocity, mult, mult_up, face, inverse_t, by_row_again, spots, place, *edges)
    tail = lax.ppermute(tail, "gx", ring("gx", -1))
    return jnp.concatenate([head, tail], 1), mult[None]


def solution(mesh):
    in_specs = (
        P(None, "gx", "gy", "gz"),
        P("gx", "gy", "gz"),
        P("gx", "gy", "gz", None, None),
        P("gx", "gy", "gz", None, None),
        P("gx", "gy", "gz", None),
        P("gx", "gy", "gz"),
        P("gx", "gy", "gz", None),
        P("gx", "gy", "gz"),
    )
    out_specs = (P(None, "gx", "gy", "gz"), P("gx", None, "gy", "gz"))
    return jax.shard_map(shards, mesh=mesh, in_specs=in_specs, out_specs=out_specs, check_vma=False)
```

time: 108 us -> 87.1 us (0.81)
  local copies, waits for them, and re-layouts: 11 us -> 1.23 us
  Pallas kernels: 26.5 us -> 21 us
  other arithmetic: 4.8 us -> 0.69 us
    unnamed x21 -> x6, local copies, waits for them, and re-layouts: 8.92 us -> 1.23 us
    pallas_call x9 -> x13, Pallas kernels: 26.5 us -> 21 us  [run(): return kernel(*args[:n_smem], *held, *far)]
    concatenate x2 -> x0, other arithmetic: 1.79 us -> none  [the longest x1 1.78 us: shards(): jnp.concatenate([coarse_matrix[0, 0], jnp.pad(coarse_diag[0], ((0, 7), (0...]
    unnamed x1 -> x0, other arithmetic: 1.32 us -> none
    ppermute x18 -> x20, waiting for transfers between devices: 17.7 us -> 17.2 us  [the longest x5 9.13 us: by_core(): return lax.ppermute(x, ('gx', 'gy', 'gz'), pairs)]
    ppermute x18 -> x20, starting transfers between devices: 24.9 us -> 24.4 us  [the longest x5 8.26 us: by_core(): return lax.ppermute(x, ('gx', 'gy', 'gz'), pairs)]
  transfers between devices with their start and end apart: 21 -> 23, of which waited for: 10 -> 9; matrix products, arithmetic and copies ran while one was open for 5% -> 0% of each run, Pallas kernels for 17% -> 15%
where the time goes in v1:
time: 87.1 us; the launch traced here: 86.9 us
  starting transfers between devices  26.6 us (31%)
  waiting for transfers between devices  23.2 us (27%)
  Pallas kernels  21 us (24%)
  between operations  14.2 us (16%)
  local copies, waits for them, and re-layouts  1.23 us (1%)
    pallas_call x13, Pallas kernels, run(): return kernel(*args[:n_smem], *held, *far)  21 us
    ppermute x5, waiting for transfers between devices, by_core(): return lax.ppermute(x, ('gx', 'gy', 'gz'), pairs)  9.13 us
    ppermute x5, starting transfers between devices, by_core(): return lax.ppermute(x, ('gx', 'gy', 'gz'), pairs)  8.26 us
    ppermute x3, starting transfers between devices, trade(): got_z = lax.ppermute(z2, 'gz', swaps('gz', 1))  8.19 us
    ppermute x1, waiting for transfers between devices, shards(): tail = lax.ppermute(tail, 'gx', ring('gx', -1))  6 us
    ppermute x3, waiting for transfers between devices, trade(): got_z = lax.ppermute(z2, 'gz', swaps('gz', 1))  5.95 us
    ppermute x3, starting transfers between devices, trade(): lax.ppermute(y2, 'gy', swaps('gy', 1))  4.82 us
    ppermute x3, starting transfers between devices, trade(): lax.ppermute(y1, 'gy', swaps('gy', 0))  2.5 us
  transfers between devices with their start and end apart: 23, of which 9 were waited for; matrix products, arithmetic and copies ran while one was open for 0% of the time, Pallas kernels for 15%

profile of v1, /device:TPU:6, one launch (start us, length us, event | category | flops | bytes accessed | tf_op | source)
XLA Modules:
  0.0 86.9 jit_solution(6992961103680572205)
XLA Ops:
  7.2 1.0 %shard_map.95 = (f32[7,5,8,128]{3,2,1,0:T(8,128)S(1)}, f32[3,16,8,128]{3,2,1,0:T(8,128)S(1)}, f32[16,8,128]{2,1,0:T(8,128)S(1)}, s32[16,8,128]{2,1,0:T(8,128)S(1)}, s32[8,128]{1,0:T(8,128)S(1)}) custom-call(f32[3,16,8,128]{3,2,1,0:T(8,128)} %force.1, f32[16,8,128]{2,1,0:T(8,128)} %kappa.1, s32[16,8,128]{2,1,0:T(8,128)} %agg.1), custom_call_target="tpu_custom_call" | custom-call | tf_op jit(solution)/shard_map/pallas_call | solution.py:48
  8.2 1.9 %collective-permute-start = (f32[7,5,8,128]{3,2,1,0:T(8,128)S(1)}, f32[7,5,8,128]{3,2,1,0:T(8,128)S(1)}, u32[]{:S(2)}, u32[]{:S(2)}) collective-permute-start(f32[7,5,8,128]{3,2,1,0:T(8,128)S(1)} %get-tuple-element.51), channel_id=1, source_target_pairs={{0,16},{16,32},{32,48},{48,64},{64,80},{80,96},{96,112},{112,0},{1... | collective-permute-start | bytes 430088 | tf_op jit(solution)/shard_map/ppermute | solution.py:609
  10.1 4.2 %shard_map.96 = (f32[2,4096,128]{2,1,0:T(8,128)S(1)}, s32[8,256]{1,0:T(8,128)S(1)}, bf16[128,256]{1,0:T(8,128)(2,1)S(1)}) custom-call(s32[8,128]{1,0:T(8,128)S(1)} %get-tuple-element.47.flags, f32[192,4096]{1,0:T(8,128)} %bitcast.9, s32[4,48]{1,0:T(4,128)} %bitcast.11, s32[1,48]{1,0:T(1,128)} %bitcast.12), custom_call_target="tpu_custom_call" | custom-call | tf_op jit(solution)/shard_map/pallas_call | solution.py:48
  14.4 2.4 %shard_map.97 = (f32[22,3,8,128]{3,2,1,0:T(8,128)S(1)}, f32[22,8,128]{2,1,0:T(8,128)S(1)}, f32[22,8,128]{2,1,0:T(8,128)S(1)}, s32[22,8,128]{2,1,0:T(8,128)S(1)},...) custom-call(s32[8,128]{1,0:T(8,128)S(1)} %get-tuple-element.47.flags, ...), custom_call_target="tpu_custom_call" | custom-call | tf_op jit(solution)/shard_map/pallas_call | solution.py:48
  16.8 1.7 %collective-permute-start.1 = (f32[96,128]{1,0:T(8,128)S(1)}, f32[96,128]{1,0:T(8,128)S(1)}, u32[]{:S(2)}, u32[]{:S(2)}) collective-permute-start(f32[96,128]{1,0:T(8,128)S(1)} %get-tuple-element.63), channel_id=1, source_target_pairs={{0,4},{4,0},{8,12},{12,8},{1,5},{5,1},{9,13},{13,9},{2,6},{6,2},{1... | collective-permute-start | bytes 147464 | tf_op jit(solution)/shard_map/ppermute | solution.py:583
  18.5 2.2 %collective-permute-start.2 = (f32[96,128]{1,0:T(8,128)S(1)}, f32[96,128]{1,0:T(8,128)S(1)}, u32[]{:S(2)}, u32[]{:S(2)}) collective-permute-start(f32[96,128]{1,0:T(8,128)S(1)} %get-tuple-element.64), channel_id=1, source_target_pairs={{4,8},{8,4},{12,0},{0,12},{5,9},{9,5},{13,1},{1,13},{6,10},{10,6},... | collective-permute-start | bytes 147464 | tf_op jit(solution)/shard_map/ppermute | solution.py:583
  20.6 3.7 %collective-permute-start.4 = (f32[16,128]{1,0:T(8,128)S(1)}, f32[16,128]{1,0:T(8,128)S(1)}, u32[]{:S(2)}, u32[]{:S(2)}) collective-permute-start(f32[16,128]{1,0:T(8,128)S(1)} %get-tuple-element.66), channel_id=1, source_target_pairs={{1,2},{2,1},{3,0},{0,3},{5,6},{6,5},{7,4},{4,7},{9,10},{10,9},{11,... | collective-permute-start | bytes 24584 | tf_op jit(solution)/shard_map/ppermute | solution.py:582
  24.3 1.4 %collective-permute-done.4.z2.az2 = f32[16,128]{1,0:T(8,128)S(1)} collective-permute-done((f32[16,128]{1,0:T(8,128)S(1)}, f32[16,128]{1,0:T(8,128)S(1)}, u32[]{:S(2)}, u32[]{:S(2)}) %collective-permute-start.4) | collective-permute-done | bytes 8224 | tf_op jit(solution)/shard_map/ppermute | solution.py:582
  25.7 2.6 %shard_map.98 = (f32[22,3,8,128]{3,2,1,0:T(8,128)S(1)}, f32[3,8,128]{2,1,0:T(8,128)S(1)}, f32[3,8,128]{2,1,0:T(8,128)S(1)}, f32[72,128]{1,0:T(8,128)S(1)}, f32[7...) custom-call(s32[8,128]{1,0:T(8,128)S(1)} %get-tuple-element.47.flags, ...), custom_call_target="tpu_custom_call" | custom-call | tf_op jit(solution)/shard_map/pallas_call | solution.py:48
  28.3 0.8 collective-permute-start.5
  29.1 0.6 collective-permute-start.6
  29.7 3.2 %collective-permute-start.8 = (f32[8,128]{1,0:T(8,128)S(1)}, f32[8,128]{1,0:T(8,128)S(1)}, u32[]{:S(2)}, u32[]{:S(2)}) collective-permute-start(f32[8,128]{1,0:T(8,128)S(1)} %get-tuple-element.75), channel_id=1, source_target_pairs={{1,2},{2,1},{3,0},{0,3},{5,6},{6,5},{7,4},{4,7},{9,10},{10,9},{11,... | collective-permute-start | bytes 12296 | tf_op jit(solution)/shard_map/ppermute | solution.py:582
  32.9 1.3 %collective-permute-done.8.z2 = f32[8,128]{1,0:T(8,128)S(1)} collective-permute-done((f32[8,128]{1,0:T(8,128)S(1)}, f32[8,128]{1,0:T(8,128)S(1)}, u32[]{:S(2)}, u32[]{:S(2)}) %collective-permute-start.8) | collective-permute-done | bytes 4128 | tf_op jit(solution)/shard_map/ppermute | solution.py:582
  34.3 1.4 %shard_map.101.one = f32[32,128]{1,0:T(8,128)S(1)} custom-call(s32[8,128]{1,0:T(8,128)S(1)} %get-tuple-element.47.flags, f32[22,3,8,128]{3,2,1,0:T(8,128)S(1)} %get-tuple-element.55.force, f32[22,8,128]{2,1,0:T(8,128)S(1)} %get-tuple-element.56.weight, f32[22,3,8,128]{3,2,1,0:T(8,128)S(1)} %get-tuple-element.67.velocity.old, ...), custom_call_target="tpu_custom_call" | custom-call | tf_op jit(solution)/shard_map/pallas_call | solution.py:48
  36.2 0.8 collective-permute-done.9.two
  37.1 3.4 %collective-permute-start.10 = (f32[32,128]{1,0:T(8,128)S(1)}, f32[32,128]{1,0:T(8,128)S(1)}, u32[]{:S(2)}, u32[]{:S(2)}) collective-permute-start(f32[32,128]{1,0:T(8,128)S(1)} %shard_map.102.mine), channel_id=1, source_target_pairs={{0,2},{1,113},{2,0},{3,115},{4,6},{5,117},{6,4},{7,119},{8,10},{9,... | collective-permute-start | bytes 49160 | tf_op jit(solution)/shard_map/ppermute | solution.py:596
  40.6 1.7 %collective-permute-done.10.first = f32[32,128]{1,0:T(8,128)S(1)} collective-permute-done((f32[32,128]{1,0:T(8,128)S(1)}, f32[32,128]{1,0:T(8,128)S(1)}, u32[]{:S(2)}, u32[]{:S(2)}) %collective-permute-start.10) | collective-permute-done | bytes 16416 | tf_op jit(solution)/shard_map/ppermute | solution.py:596
  42.3 5.2 %collective-permute-done.11.second = f32[32,128]{1,0:T(8,128)S(1)} collective-permute-done((f32[32,128]{1,0:T(8,128)S(1)}, f32[32,128]{1,0:T(8,128)S(1)}, u32[]{:S(2)}, u32[]{:S(2)}) %collective-permute-start.11) | collective-permute-done | bytes 16416 | tf_op jit(solution)/shard_map/ppermute | solution.py:596
  47.7 1.2 %copy-done.1 = f32[512,512]{1,0:T(8,128)S(1)} copy-done((f32[512,512]{1,0:T(8,128)S(1)}, f32[512,512]{1,0:T(8,128)}, u32[]{:S(2)}) %copy-start.1) | copy-done | bytes 1048600
  49.3 0.7 shard_map.104.iterate
  50.0 2.0 %collective-permute-start.13 = (f32[8,512]{1,0:T(8,128)S(1)}, f32[8,512]{1,0:T(8,128)S(1)}, u32[]{:S(2)}, u32[]{:S(2)}) collective-permute-start(f32[8,512]{1,0:T(8,128)S(1)} %shard_map.104.iterate), channel_id=1, source_target_pairs={{0,16},{1,5},{2,18},{3,7},{4,20},{5,9},{6,22},{7,11},{8,24},{9,13}... | collective-permute-start | bytes 49160 | tf_op jit(solution)/shard_map/ppermute | solution.py:596
  52.0 2.5 %collective-permute-start.14 = (f32[8,512]{1,0:T(8,128)S(1)}, f32[8,512]{1,0:T(8,128)S(1)}, u32[]{:S(2)}, u32[]{:S(2)}) collective-permute-start(f32[8,512]{1,0:T(8,128)S(1)} %shard_map.104.iterate), channel_id=1, source_target_pairs={{0,12},{1,21},{2,14},{3,23},{4,0},{5,25},{6,2},{7,27},{8,4},{9,29}... | collective-permute-start | bytes 49160 | tf_op jit(solution)/shard_map/ppermute | solution.py:596
  54.7 2.2 %shard_map.100.after.by_row = f32[2,4096,128]{2,1,0:T(8,128)S(1)} custom-call(bf16[512,512]{1,0:T(8,128)(2,1)S(1)} %get-tuple-element.71.after.high, f32[2,4096,128]{2,1,0:T(8,128)} %copy-done), custom_call_target="tpu_custom_call" | custom-call | tf_op jit(solution)/shard_map/pallas_call | solution.py:48
  56.9 2.2 %collective-permute-done.15.c = f32[8,512]{1,0:T(8,128)S(1)} collective-permute-done((f32[8,512]{1,0:T(8,128)S(1)}, f32[8,512]{1,0:T(8,128)S(1)}, u32[]{:S(2)}, u32[]{:S(2)}) %collective-permute-start.15) | collective-permute-done | bytes 16416 | tf_op jit(solution)/shard_map/ppermute | solution.py:596
  59.1 1.2 %collective-permute-done.16.swapped = f32[24,512]{1,0:T(8,128)S(1)} collective-permute-done((f32[24,512]{1,0:T(8,128)S(1)}, f32[24,512]{1,0:T(8,128)S(1)}, u32[]{:S(2)}, u32[]{:S(2)}) %collective-permute-start.16) | collective-permute-done | bytes 49184 | tf_op jit(solution)/shard_map/ppermute | solution.py:664
  60.3 3.1 %shard_map.106 = (f32[22,3,8,128]{3,2,1,0:T(8,128)S(1)}, f32[3,8,128]{2,1,0:T(8,128)S(1)}, f32[3,8,128]{2,1,0:T(8,128)S(1)}, f32[72,128]{1,0:T(8,128)S(1)}, f32[...) custom-call(s32[8,128]{1,0:T(8,128)S(1)} %get-tuple-element.47.flags, ...), custom_call_target="tpu_custom_call" | custom-call | tf_op jit(solution)/shard_map/pallas_call | solution.py:48
  63.5 2.0 %collective-permute-start.18 = (f32[72,128]{1,0:T(8,128)S(1)}, f32[72,128]{1,0:T(8,128)S(1)}, u32[]{:S(2)}, u32[]{:S(2)}) collective-permute-start(f32[72,128]{1,0:T(8,128)S(1)} %get-tuple-element.84), channel_id=1, source_target_pairs={{4,8},{8,4},{12,0},{0,12},{5,9},{9,5},{13,1},{1,13},{6,10},{10,6},... | collective-permute-start | bytes 110600 | tf_op jit(solution)/shard_map/ppermute | solution.py:583
  65.5 1.3 %collective-permute-start.20 = (f32[8,128]{1,0:T(8,128)S(1)}, f32[8,128]{1,0:T(8,128)S(1)}, u32[]{:S(2)}, u32[]{:S(2)}) collective-permute-start(f32[8,128]{1,0:T(8,128)S(1)} %get-tuple-element.86), channel_id=1, source_target_pairs={{1,2},{2,1},{3,0},{0,3},{5,6},{6,5},{7,4},{4,7},{9,10},{10,9},{11,... | collective-permute-start | bytes 12296 | tf_op jit(solution)/shard_map/ppermute | solution.py:582
  66.8 3.3 %collective-permute-done.20.z2 = f32[8,128]{1,0:T(8,128)S(1)} collective-permute-done((f32[8,128]{1,0:T(8,128)S(1)}, f32[8,128]{1,0:T(8,128)S(1)}, u32[]{:S(2)}, u32[]{:S(2)}) %collective-permute-start.20) | collective-permute-done | bytes 4128 | tf_op jit(solution)/shard_map/ppermute | solution.py:582
  70.1 3.0 %shard_map.107 = (f32[3,12,8,128]{3,2,1,0:T(8,128)S(1)}, f32[3,4,8,128]{3,2,1,0:T(8,128)S(1)}, f32[3,8,128]{2,1,0:T(8,128)}) custom-call(s32[8,128]{1,0:T(8,128)S(1)} %get-tuple-element.47.flags, f32[22,3,8,128]{3,2,1,0:T(8,128)S(1)} %get-tuple-element.55.force, f32[22,8,128]{2,1,0:T(8,128)S(1)} %get-tuple-element.56.weight, ...), custom_call_target="tpu_custom_call" | custom-call | tf_op jit(solution)/shard_map/pallas_call | solution.py:48
  73.4 6.0 %collective-permute-done.21 = f32[3,4,8,128]{3,2,1,0:T(8,128)S(1)} collective-permute-done((f32[3,4,8,128]{3,2,1,0:T(8,128)S(1)}, f32[3,4,8,128]{3,2,1,0:T(8,128)S(1)}, u32[]{:S(2)}, u32[]{:S(2)}) %collective-permute-start.21) | collective-permute-done | bytes 49184 | tf_op jit(solution)/shard_map/ppermute | solution.py:677
  79.4 0.7 pad_maximum_fusion
  (35 shorter events, 1.8 us)
Async XLA Ops:
  7.2 40.5 %all-gather.2.cloned.1.call-start = ((), (), s32[]{:S(2)}) async-start(), calls=%async_computation | async-start | bytes 1310720 | tf_op jit(solution)/shard_map/all_gather | solution.py:608
  8.2 6.1 %collective-permute-start = (f32[7,5,8,128]{3,2,1,0:T(8,128)S(1)}, f32[7,5,8,128]{3,2,1,0:T(8,128)S(1)}, u32[]{:S(2)}, u32[]{:S(2)}) collective-permute-start(f32[7,5,8,128]{3,2,1,0:T(8,128)S(1)} %get-tuple-element.51), channel_id=1, source_target_pairs={{0,16},{16,32},{32,48},{48,64},{64,80},{80,96},{96,112},{112,0},{1... | collective-permute-start | bytes 430088 | tf_op jit(solution)/shard_map/ppermute | solution.py:609
  14.4 14.0 %copy-start = (f32[2,4096,128]{2,1,0:T(8,128)}, f32[2,4096,128]{2,1,0:T(8,128)S(1)}, u32[]{:S(2)}) copy-start(f32[2,4096,128]{2,1,0:T(8,128)S(1)} %get-tuple-element.52.by_row.far) | copy-start | bytes 12582916
  14.4 19.9 %copy-start.2 = (f32[1,1,128]{2,1,0:T(1,128)S(1)}, f32[1,1,128]{2,1,0:T(1,128)}, u32[]{:S(2)}) copy-start(f32[1,1,128]{2,1,0:T(1,128)} %param.15) | copy-start | bytes 1540
  16.8 8.9 %collective-permute-start.1 = (f32[96,128]{1,0:T(8,128)S(1)}, f32[96,128]{1,0:T(8,128)S(1)}, u32[]{:S(2)}, u32[]{:S(2)}) collective-permute-start(f32[96,128]{1,0:T(8,128)S(1)} %get-tuple-element.63), channel_id=1, source_target_pairs={{0,4},{4,0},{8,12},{12,8},{1,5},{5,1},{9,13},{13,9},{2,6},{6,2},{1... | collective-permute-start | bytes 147464 | tf_op jit(solution)/shard_map/ppermute | solution.py:583
  18.5 7.3 %collective-permute-start.2 = (f32[96,128]{1,0:T(8,128)S(1)}, f32[96,128]{1,0:T(8,128)S(1)}, u32[]{:S(2)}, u32[]{:S(2)}) collective-permute-start(f32[96,128]{1,0:T(8,128)S(1)} %get-tuple-element.64), channel_id=1, source_target_pairs={{4,8},{8,4},{12,0},{0,12},{5,9},{9,5},{13,1},{1,13},{6,10},{10,6},... | collective-permute-start | bytes 147464 | tf_op jit(solution)/shard_map/ppermute | solution.py:583
  20.6 3.7 %collective-permute-start.3 = (f32[16,128]{1,0:T(8,128)S(1)}, f32[16,128]{1,0:T(8,128)S(1)}, u32[]{:S(2)}, u32[]{:S(2)}) collective-permute-start(f32[16,128]{1,0:T(8,128)S(1)} %get-tuple-element.65), channel_id=1, source_target_pairs={{0,1},{1,0},{2,3},{3,2},{4,5},{5,4},{6,7},{7,6},{8,9},{9,8},{10,11... | collective-permute-start | bytes 24584 | tf_op jit(solution)/shard_map/ppermute | solution.py:584
  20.6 5.1 %collective-permute-start.4 = (f32[16,128]{1,0:T(8,128)S(1)}, f32[16,128]{1,0:T(8,128)S(1)}, u32[]{:S(2)}, u32[]{:S(2)}) collective-permute-start(f32[16,128]{1,0:T(8,128)S(1)} %get-tuple-element.66), channel_id=1, source_target_pairs={{1,2},{2,1},{3,0},{0,3},{5,6},{6,5},{7,4},{4,7},{9,10},{10,9},{11,... | collective-permute-start | bytes 24584 | tf_op jit(solution)/shard_map/ppermute | solution.py:582
  28.3 5.9 %collective-permute-start.5 = (f32[72,128]{1,0:T(8,128)S(1)}, f32[72,128]{1,0:T(8,128)S(1)}, u32[]{:S(2)}, u32[]{:S(2)}) collective-permute-start(f32[72,128]{1,0:T(8,128)S(1)} %get-tuple-element.72), channel_id=1, source_target_pairs={{0,4},{4,0},{8,12},{12,8},{1,5},{5,1},{9,13},{13,9},{2,6},{6,2},{1... | collective-permute-start | bytes 110600 | tf_op jit(solution)/shard_map/ppermute | solution.py:583
  29.1 5.2 %collective-permute-start.6 = (f32[72,128]{1,0:T(8,128)S(1)}, f32[72,128]{1,0:T(8,128)S(1)}, u32[]{:S(2)}, u32[]{:S(2)}) collective-permute-start(f32[72,128]{1,0:T(8,128)S(1)} %get-tuple-element.73), channel_id=1, source_target_pairs={{4,8},{8,4},{12,0},{0,12},{5,9},{9,5},{13,1},{1,13},{6,10},{10,6},... | collective-permute-start | bytes 110600 | tf_op jit(solution)/shard_map/ppermute | solution.py:583
  29.7 3.2 %collective-permute-start.7 = (f32[8,128]{1,0:T(8,128)S(1)}, f32[8,128]{1,0:T(8,128)S(1)}, u32[]{:S(2)}, u32[]{:S(2)}) collective-permute-start(f32[8,128]{1,0:T(8,128)S(1)} %get-tuple-element.74), channel_id=1, source_target_pairs={{0,1},{1,0},{2,3},{3,2},{4,5},{5,4},{6,7},{7,6},{8,9},{9,8},{10,11... | collective-permute-start | bytes 12296 | tf_op jit(solution)/shard_map/ppermute | solution.py:584
  29.7 4.5 %collective-permute-start.8 = (f32[8,128]{1,0:T(8,128)S(1)}, f32[8,128]{1,0:T(8,128)S(1)}, u32[]{:S(2)}, u32[]{:S(2)}) collective-permute-start(f32[8,128]{1,0:T(8,128)S(1)} %get-tuple-element.75), channel_id=1, source_target_pairs={{1,2},{2,1},{3,0},{0,3},{5,6},{6,5},{7,4},{4,7},{9,10},{10,9},{11,... | collective-permute-start | bytes 12296 | tf_op jit(solution)/shard_map/ppermute | solution.py:582
  35.7 1.4 %collective-permute-start.9 = (f32[32,128]{1,0:T(8,128)S(1)}, f32[32,128]{1,0:T(8,128)S(1)}, u32[]{:S(2)}, u32[]{:S(2)}) collective-permute-start(f32[32,128]{1,0:T(8,128)S(1)} %shard_map.101.one), channel_id=1, source_target_pairs={{0,1},{1,0},{2,3},{3,2},{4,5},{5,4},{6,7},{7,6},{8,9},{9,8},{10,11... | collective-permute-start | bytes 49160 | tf_op jit(solution)/shard_map/ppermute | solution.py:650
  37.1 5.2 %collective-permute-start.10 = (f32[32,128]{1,0:T(8,128)S(1)}, f32[32,128]{1,0:T(8,128)S(1)}, u32[]{:S(2)}, u32[]{:S(2)}) collective-permute-start(f32[32,128]{1,0:T(8,128)S(1)} %shard_map.102.mine), channel_id=1, source_target_pairs={{0,2},{1,113},{2,0},{3,115},{4,6},{5,117},{6,4},{7,119},{8,10},{9,... | collective-permute-start | bytes 49160 | tf_op jit(solution)/shard_map/ppermute | solution.py:596
  40.5 7.1 %collective-permute-start.11 = (f32[32,128]{1,0:T(8,128)S(1)}, f32[32,128]{1,0:T(8,128)S(1)}, u32[]{:S(2)}, u32[]{:S(2)}) collective-permute-start(f32[32,128]{1,0:T(8,128)S(1)} %shard_map.102.mine), channel_id=1, source_target_pairs={{0,114},{1,3},{2,112},{3,1},{4,118},{5,7},{6,116},{7,5},{8,122},{9... | collective-permute-start | bytes 49160 | tf_op jit(solution)/shard_map/ppermute | solution.py:596
  47.6 1.6 %collective-permute-start.12 = (f32[24,128]{1,0:T(8,128)S(1)}, f32[24,128]{1,0:T(8,128)S(1)}, u32[]{:S(2)}, u32[]{:S(2)}) collective-permute-start(f32[24,128]{1,0:T(8,128)S(1)} %get-tuple-element.78.passed), channel_id=1, source_target_pairs={{0,1},{1,0},{2,3},{3,2},{4,5},{5,4},{6,7},{7,6},{8,9},{9,8},{10,11... | collective-permute-start | bytes 36872 | tf_op jit(solution)/shard_map/ppermute | solution.py:654
  47.7 1.2 %copy-start.1 = (f32[512,512]{1,0:T(8,128)S(1)}, f32[512,512]{1,0:T(8,128)}, u32[]{:S(2)}) copy-start(f32[512,512]{1,0:T(8,128)} %all-gather.2.cloned.1.call-done.rows) | copy-start | bytes 3145732
  50.0 7.0 %collective-permute-start.13 = (f32[8,512]{1,0:T(8,128)S(1)}, f32[8,512]{1,0:T(8,128)S(1)}, u32[]{:S(2)}, u32[]{:S(2)}) collective-permute-start(f32[8,512]{1,0:T(8,128)S(1)} %shard_map.104.iterate), channel_id=1, source_target_pairs={{0,16},{1,5},{2,18},{3,7},{4,20},{5,9},{6,22},{7,11},{8,24},{9,13}... | collective-permute-start | bytes 49160 | tf_op jit(solution)/shard_map/ppermute | solution.py:596
  52.0 5.0 %collective-permute-start.14 = (f32[8,512]{1,0:T(8,128)S(1)}, f32[8,512]{1,0:T(8,128)S(1)}, u32[]{:S(2)}, u32[]{:S(2)}) collective-permute-start(f32[8,512]{1,0:T(8,128)S(1)} %shard_map.104.iterate), channel_id=1, source_target_pairs={{0,12},{1,21},{2,14},{3,23},{4,0},{5,25},{6,2},{7,27},{8,4},{9,29}... | collective-permute-start | bytes 49160 | tf_op jit(solution)/shard_map/ppermute | solution.py:596
  54.5 4.6 %collective-permute-start.15 = (f32[8,512]{1,0:T(8,128)S(1)}, f32[8,512]{1,0:T(8,128)S(1)}, u32[]{:S(2)}, u32[]{:S(2)}) collective-permute-start(f32[8,512]{1,0:T(8,128)S(1)} %shard_map.104.iterate), channel_id=1, source_target_pairs={{0,28},{1,17},{2,30},{3,19},{4,16},{5,21},{6,18},{7,23},{8,20},{9,... | collective-permute-start | bytes 49160 | tf_op jit(solution)/shard_map/ppermute | solution.py:596
  59.1 1.2 %collective-permute-start.16 = (f32[24,512]{1,0:T(8,128)S(1)}, f32[24,512]{1,0:T(8,128)S(1)}, u32[]{:S(2)}, u32[]{:S(2)}) collective-permute-start(f32[24,512]{1,0:T(8,128)S(1)} %shard_map.105.got), channel_id=1, source_target_pairs={{0,1},{1,0},{2,3},{3,2},{4,5},{5,4},{6,7},{7,6},{8,9},{9,8},{10,11... | collective-permute-start | bytes 147464 | tf_op jit(solution)/shard_map/ppermute | solution.py:664
  63.4 6.7 %collective-permute-start.17 = (f32[72,128]{1,0:T(8,128)S(1)}, f32[72,128]{1,0:T(8,128)S(1)}, u32[]{:S(2)}, u32[]{:S(2)}) collective-permute-start(f32[72,128]{1,0:T(8,128)S(1)} %get-tuple-element.83), channel_id=1, source_target_pairs={{0,4},{4,0},{8,12},{12,8},{1,5},{5,1},{9,13},{13,9},{2,6},{6,2},{1... | collective-permute-start | bytes 110600 | tf_op jit(solution)/shard_map/ppermute | solution.py:583
  63.5 6.6 %collective-permute-start.18 = (f32[72,128]{1,0:T(8,128)S(1)}, f32[72,128]{1,0:T(8,128)S(1)}, u32[]{:S(2)}, u32[]{:S(2)}) collective-permute-start(f32[72,128]{1,0:T(8,128)S(1)} %get-tuple-element.84), channel_id=1, source_target_pairs={{4,8},{8,4},{12,0},{0,12},{5,9},{9,5},{13,1},{1,13},{6,10},{10,6},... | collective-permute-start | bytes 110600 | tf_op jit(solution)/shard_map/ppermute | solution.py:583
  65.5 1.3 %collective-permute-start.19 = (f32[8,128]{1,0:T(8,128)S(1)}, f32[8,128]{1,0:T(8,128)S(1)}, u32[]{:S(2)}, u32[]{:S(2)}) collective-permute-start(f32[8,128]{1,0:T(8,128)S(1)} %get-tuple-element.85), channel_id=1, source_target_pairs={{0,1},{1,0},{2,3},{3,2},{4,5},{5,4},{6,7},{7,6},{8,9},{9,8},{10,11... | collective-permute-start | bytes 12296 | tf_op jit(solution)/shard_map/ppermute | solution.py:584
  65.5 4.5 %collective-permute-start.20 = (f32[8,128]{1,0:T(8,128)S(1)}, f32[8,128]{1,0:T(8,128)S(1)}, u32[]{:S(2)}, u32[]{:S(2)}) collective-permute-start(f32[8,128]{1,0:T(8,128)S(1)} %get-tuple-element.86), channel_id=1, source_target_pairs={{1,2},{2,1},{3,0},{0,3},{5,6},{6,5},{7,4},{4,7},{9,10},{10,9},{11,... | collective-permute-start | bytes 12296 | tf_op jit(solution)/shard_map/ppermute | solution.py:582
  73.1 6.3 %collective-permute-start.21 = (f32[3,4,8,128]{3,2,1,0:T(8,128)S(1)}, f32[3,4,8,128]{3,2,1,0:T(8,128)S(1)}, u32[]{:S(2)}, u32[]{:S(2)}) collective-permute-start(f32[3,4,8,128]{3,2,1,0:T(8,128)S(1)} %get-tuple-element.88), channel_id=1, source_target_pairs={{0,112},{16,0},{32,16},{48,32},{64,48},{80,64},{96,80},{112,96},{1... | collective-permute-start | bytes 147464 | tf_op jit(solution)/shard_map/ppermute | solution.py:677
Sparse Core Ops, SparseCore 0:
  9.7 23.3 all-gather.1

commit v2 on v1

--- a/solution.py
+++ b/solution.py
@@ -267,7 +267,7 @@
 
 def first_sweep_kernel(
     flags, force_in, kappa_in, agg_in, tail, by_row, spots, place,
-    force, weight, inverse, agg, velocity, mult, mult_up, face, inverse_t, y1, y2, z1, z2,
+    force, weight, inverse, agg, velocity, mult, mult_up, face, inverse_t, z1, z2,
 ):
     for p in range(NP):
         here = p - TAIL
@@ -292,12 +292,17 @@
     mult_up[...] = pulled.reshape(3, 8, 128)
     velocity[LOW] = (lower - increment * tall(inverse[LOW])).reshape(3, 8, 128)
     velocity[UPP] = (upper + pulled * tall(inverse[UPP])).reshape(3, 8, 128)
-    get = lambda p, c: velocity[p, c]
-    write_lines(flags, get, y1, y2)
-    write_columns(flags, get, z1, z2)
-    label = lambda p, c: agg[p].astype(F32)
-    write_lines(flags, label, y1, y2, LINES, 1)
-    write_columns(flags, label, z1, z2, 8)
+    write_columns(flags, lambda p, c: velocity[p, c], z1, z2)
+    write_columns(flags, lambda p, c: agg[p].astype(F32), z1, z2, 8)
+
+
+def lines_kernel(flags, velocity, y1, y2):
+    write_lines(flags, lambda p, c: velocity[p, c], y1, y2)
+
+
+def lines_and_labels_kernel(flags, velocity, agg, y1, y2):
+    write_lines(flags, lambda p, c: velocity[p, c], y1, y2)
+    write_lines(flags, lambda p, c: agg[p].astype(F32), y1, y2, LINES, 1)
 
 
 def sweep(
@@ -328,29 +333,27 @@
 
 def second_sweep_kernel(
     flags, force, weight, inverse, velocity, mult, mult_up, face, inverse_t, by_row, spots, place,
-    y1, y2, z1, z2, out, out_mult, out_up, oy1, oy2, oz1, oz2,
+    z2, y1, y2, z1, out, out_mult, out_up, oz1, oz2,
 ):
     halo = sides(flags, y1, y2, z1, z2)
     sweep(
         flags, force, weight, inverse, velocity, mult, mult_up, face, inverse_t, by_row, spots, place,
         halo, out, out_mult, out_up,
     )
-    get = lambda p, c: out[p, c]
-    write_lines(flags, get, oy1, oy2)
-    write_columns(flags, get, oz1, oz2)
+    write_columns(flags, lambda p, c: out[p, c], oz1, oz2)
 
 
 def third_sweep_kernel(
     flags, force, weight, inverse, old, mult, mult_up, face, inverse_t, by_row, spots, place,
-    y1, y2, z1, z2, ay1, ay2, az1, az2, agg, iterate, got, swapped,
-    out, out_mult, out_up, oy1, oy2, oz1, oz2, velocity,
+    z2, y1, y2, z1, az2, ay1, ay2, az1, agg, iterate, got, swapped,
+    out, out_mult, out_up, oz1, oz2, velocity,
 ):
     core_zero = yes(flags, 1, (24, NAGG))
     a = jnp.where(core_zero, got[...], swapped[...])
     b = jnp.where(core_zero, swapped[...], got[...])
-    own, prev = table(iterate[...]), table(a[0:8])
-    low, low_prev = table(b[0:8]), table(b[8:16])
-    high, high_prev = table(a[8:16]), table(a[16:24])
+    own, prev = table(iterate[...]), table(a[8:16])
+    low, low_prev = table(b[8:16]), table(b[0:8])
+    high, high_prev = table(a[16:24]), table(a[0:8])
     for p in range(NP):
         at = where_in(agg[p])
         for c in range(3):
@@ -394,14 +397,12 @@
         flags, force, weight, inverse, velocity, mult, mult_up, face, inverse_t, by_row, spots, place,
         halo, out, out_mult, out_up,
     )
-    get = lambda p, c: out[p, c]
-    write_lines(flags, get, oy1, oy2)
-    write_columns(flags, get, oz1, oz2)
+    write_columns(flags, lambda p, c: out[p, c], oz1, oz2)
 
 
 def last_sweep_kernel(
     flags, force, weight, inverse, velocity, mult, mult_up, face, inverse_t, by_row, spots, place,
-    y1, y2, z1, z2, head, tail, out_mult, out, out_up,
+    z2, y1, y2, z1, head, tail, out_mult, out, out_up,
 ):
     halo = sides(flags, y1, y2, z1, z2)
     sweep(
@@ -416,7 +417,7 @@
 
 
 def restrict_kernel(
-    flags, force, weight, velocity, mult, mult_up, agg, diag, y1, y2, z1, z2, out, res,
+    flags, force, weight, velocity, mult, mult_up, agg, diag, z2, y1, y2, z1, out, res,
 ):
     halo = sides(flags, y1, y2, z1, z2)
     for p in range(TAIL - 3, NP - 2):
@@ -467,11 +468,8 @@
     out[24:32] = jnp.where(sub == flags[6:7], jnp.broadcast_to(diag[...], (8, 128)), 0.0)
 
 
-def gather_sums_kernel(flags, mine, first, second, kept, passed):
-    core_zero = yes(flags, 1, (32, 128))
-    across = jnp.where(core_zero, first[...], second[...])
-    above = jnp.where(core_zero, second[...], first[...])
-    kept[...] = mine[...] + across
+def gather_sums_kernel(mine, above, across, after, kept, passed):
+    kept[...] = mine[...] + across[...]
     lane = lax.broadcasted_iota(jnp.int32, (24, 128), 1)
     passed[...] = jnp.where(lane < 64, pltpu.roll(above[0:24], 64, 1), 0.0)
 
@@ -564,6 +562,23 @@
     copy.wait()
 
 
+def write_head_kernel(head, mult, velocity, out_mult, sems):
+    copies = [
+        pltpu.make_async_copy(head, velocity.at[:, pl.ds(0, 16 - RET)], sems.at[0]),
+        pltpu.make_async_copy(mult, out_mult, sems.at[1]),
+    ]
+    for copy in copies:
+        copy.start()
+    for copy in copies:
+        copy.wait()
+
+
+def write_tail_kernel(tail, before, velocity, sem):
+    copy = pltpu.make_async_copy(tail, velocity.at[:, pl.ds(16 - RET, RET)], sem)
+    copy.start()
+    copy.wait()
+
+
 def ring(axis, by):
     n = lax.axis_size(axis)
     return [(i, (i + by) % n) for i in range(n)]
@@ -579,9 +594,12 @@
 
 
 def trade(y1, y2, z1, z2):
-    got_z = lax.ppermute(z2, "gz", swaps("gz", 1))
-    got = [lax.ppermute(y1, "gy", swaps("gy", 0)), lax.ppermute(y2, "gy", swaps("gy", 1))]
-    return got + [lax.ppermute(z1, "gz", swaps("gz", 0)), got_z]
+    return [
+        lax.ppermute(z2, "gz", swaps("gz", 1)),
+        lax.ppermute(y1, "gy", swaps("gy", 0)),
+        lax.ppermute(y2, "gy", swaps("gy", 1)),
+        lax.ppermute(z1, "gz", swaps("gz", 0)),
+    ]
 
 
 def by_core(x, rule_zero, rule_one):
@@ -635,47 +653,61 @@
     out = call(
         first_sweep_kernel,
         [field, ((NP, 8, 128), F32), ((NP, 8, 128), F32), ((NP, 8, 128), jnp.int32), field, plane, plane,
-         turned, turned, y_more, y_more, z_more, z_more],
+         turned, turned, z_more, z_more],
         n_in=8,
     )(flags, force, kappa, agg_map, tail_in, by_row, spots, place)
     force_e, weight, inverse, agg, velocity, mult, mult_up, face, inverse_t = out[:9]
-    labels = trade(*out[9:])
+    lines = call(lines_and_labels_kernel, [y_more, y_more], n_in=3)(flags, velocity, agg)
+    labels = trade(*lines, *out[9:])
     velocity, mult, mult_up, *msgs = call(
-        second_sweep_kernel, [field, plane, plane, y_msg, y_msg, z_msg, z_msg], n_in=16
+        second_sweep_kernel, [field, plane, plane, z_msg, z_msg], n_in=16
     )(flags, force_e, weight, inverse, velocity, mult, mult_up, face, inverse_t, by_row, spots, place, *labels)
-    edges = trade(*msgs)
+    edges = trade(*call(lines_kernel, [y_msg, y_msg], n_in=2)(flags, velocity), *msgs)
     sums = call(
         restrict_kernel, [((32, 128), F32)], [pltpu.VMEM((NP, 3, 8, 128), F32)], n_in=12
     )(flags, force_e, weight, velocity, mult, mult_up, agg, coarse_diag.reshape(1, 128), *edges)[0]
     sums = add(sums, lax.ppermute(sums, "gz", swaps("gz", 0)))
-    first = by_core(sums, (0, 0, 2), (-1, 0, 0))
-    second = by_core(sums, (-1, 0, 2), (0, 0, 2))
-    kept, passed = call(gather_sums_kernel, [((32, 128), F32), ((24, 128), F32)], n_in=4)(flags, sums, first, second)
+    above = by_core(sums, (-1, 0, 2), (-1, 0, 0))
+    across = lax.ppermute(sums, "gz", ring("gz", 2))
+    kept, passed = call(gather_sums_kernel, [((32, 128), F32), ((24, 128), F32)], n_in=4)(
+        sums, above, across, k_high
+    )
     swapped = lax.ppermute(passed, "gz", swaps("gz", 0))
     iterate = call(solve_kernel, [((8, NAGG), F32)], [pltpu.VMEM((8, NAGG), F32)], n_in=5)(
         kept, passed, swapped, k_high, k_low
     )[0]
     got = [
+        by_core(iterate, (1, -1, 0), (1, 1, 0)),
         by_core(iterate, (1, 0, 0), (0, 1, 0)),
-        by_core(iterate, (0, -1, 0), (1, 1, 0)),
-        by_core(iterate, (1, -1, 0), (1, 0, 0)),
+        by_core(iterate, (0, -1, 0), (0, 1, 0)),
     ]
     got = call(join_kernel, [((24, NAGG), F32)], n_in=4)(*got, by_row_again)[0]
     swapped = lax.ppermute(got, "gz", swaps("gz", 0))
     velocity, mult, mult_up, *msgs = call(
-        third_sweep_kernel, [field, plane, plane, y_msg, y_msg, z_msg, z_msg],
+        third_sweep_kernel, [field, plane, plane, z_msg, z_msg],
         [pltpu.VMEM((NP, 3, 8, 128), F32)], n_in=24,
     )(
         flags, force_e, weight, inverse, velocity, mult, mult_up, face, inverse_t, by_row_again, spots, place,
         *edges, *labels, agg, iterate, got, swapped,
     )
-    edges = trade(*msgs)
+    edges = trade(*call(lines_kernel, [y_msg, y_msg], n_in=2)(flags, velocity), *msgs)
     head, tail, mult = call(
         last_sweep_kernel, [((3, 16 - RET, 8, 128), F32), ((3, RET, 8, 128), F32), plane],
-        [pltpu.VMEM((NP, 3, 8, 128), F32), pltpu.VMEM((3, 8, 128), F32)], n_in=16, results=(0, 2),
+        [pltpu.VMEM((NP, 3, 8, 128), F32), pltpu.VMEM((3, 8, 128), F32)], n_in=16,
     )(flags, force_e, weight, inverse, velocity, mult, mult_up, face, inverse_t, by_row_again, spots, place, *edges)
     tail = lax.ppermute(tail, "gx", ring("gx", -1))
-    return jnp.concatenate([head, tail], 1), mult[None]
+    shapes = [pltpu.HBM((3, 16, 8, 128), F32), pltpu.HBM((3, 8, 128), F32)]
+    velocity, mult = pl.pallas_call(
+        write_head_kernel, out_shape=shapes, in_specs=[VMEM] * 2, out_specs=[HBM] * 2,
+        scratch_shapes=[pltpu.SemaphoreType.DMA((2,))],
+        compiler_params=pltpu.CompilerParams(vmem_limit_bytes=12 * 1024 * 1024),
+    )(keep(head), keep(mult))
+    velocity = pl.pallas_call(
+        write_tail_kernel, out_shape=shapes[0], in_specs=[VMEM, HBM], out_specs=HBM,
+        scratch_shapes=[pltpu.SemaphoreType.DMA], input_output_aliases={1: 0},
+        compiler_params=pltpu.CompilerParams(vmem_limit_bytes=12 * 1024 * 1024),
+    )(keep(tail), pltpu.with_memory_space_constraint(velocity, pltpu.HBM))
+    return velocity, mult[None]
 
 
 def solution(mesh):

time: 87.1 us -> 85 us (0.976)
  waiting for transfers between devices: 23.2 us -> 18 us
  starting transfers between devices: 26.6 us -> 29.4 us
  Pallas kernels: 21 us -> 21.9 us
    ppermute x5 -> x4, waiting for transfers between devices: 9.13 us -> 2.88 us  [by_core(): return lax.ppermute(x, ('gx', 'gy', 'gz'), pairs)]
    ppermute x5 -> x4, starting transfers between devices: 8.26 us -> 10.7 us  [by_core(): return lax.ppermute(x, ('gx', 'gy', 'gz'), pairs)]
    pallas_call x0 -> x2, Pallas kernels: none -> 1.31 us  [the longest x1 0.68 us: shards(): pl.pallas_call(write_head_kernel, out_shape=shapes, in_specs=[VMEM] * 2,...]
    ppermute x1, waiting for transfers between devices: 0.01 us -> 1.16 us  [shards(): swapped = lax.ppermute(passed, 'gz', swaps('gz', 0))]
    ppermute x6 -> x7, starting transfers between devices: 8.19 us -> 8.88 us  [the longest x3 5.01 us: trade(): lax.ppermute(z2, 'gz', swaps('gz', 1))]
    pallas_call x13 -> x16, Pallas kernels: 21 us -> 20.5 us  [run(): return kernel(*args[:n_smem], *held, *far)]
    ppermute x6 -> x7, waiting for transfers between devices: 5.96 us -> 6.35 us  [the longest x3 4.9 us: trade(): lax.ppermute(z2, 'gz', swaps('gz', 1))]
  transfers between devices with their start and end apart: 23 -> 23, of which waited for: 9 -> 10; matrix products, arithmetic and copies ran while one was open for 0% -> 0% of each run, Pallas kernels for 15% -> 16%
where the time goes in v2:
time: 85 us; the launch traced here: 84.8 us
  starting transfers between devices  29.4 us (35%)
  Pallas kernels  21.9 us (26%)
  waiting for transfers between devices  18 us (21%)
  between operations  14.2 us (17%)
  local copies, waits for them, and re-layouts  1.24 us (1%)
    pallas_call x16, Pallas kernels, run(): return kernel(*args[:n_smem], *held, *far)  20.5 us
    ppermute x4, starting transfers between devices, by_core(): return lax.ppermute(x, ('gx', 'gy', 'gz'), pairs)  10.7 us
    ppermute x1, waiting for transfers between devices, shards(): tail = lax.ppermute(tail, 'gx', ring('gx', -1))  5.5 us
    ppermute x3, starting transfers between devices, trade(): lax.ppermute(z2, 'gz', swaps('gz', 1))  5.01 us
    ppermute x3, waiting for transfers between devices, trade(): lax.ppermute(z2, 'gz', swaps('gz', 1))  4.9 us
    ppermute x3, starting transfers between devices, trade(): lax.ppermute(y2, 'gy', swaps('gy', 1))  4.04 us
    ppermute x3, starting transfers between devices, trade(): lax.ppermute(z1, 'gz', swaps('gz', 0))  3.74 us
    ppermute x3, starting transfers between devices, trade(): lax.ppermute(y1, 'gy', swaps('gy', 0))  3.28 us
  transfers between devices with their start and end apart: 23, of which 10 were waited for; matrix products, arithmetic and copies ran while one was open for 0% of the time, Pallas kernels for 16%

profile of v2, /device:TPU:6, one launch (start us, length us, event | category | flops | bytes accessed | tf_op | source)
XLA Modules:
  0.0 84.8 jit_solution(13341634480550689829)
XLA Ops:
  7.2 1.0 %shard_map.95 = (f32[7,5,8,128]{3,2,1,0:T(8,128)S(1)}, f32[3,16,8,128]{3,2,1,0:T(8,128)S(1)}, f32[16,8,128]{2,1,0:T(8,128)S(1)}, s32[16,8,128]{2,1,0:T(8,128)S(1)}, s32[8,128]{1,0:T(8,128)S(1)}) custom-call(f32[3,16,8,128]{3,2,1,0:T(8,128)} %force.1, f32[16,8,128]{2,1,0:T(8,128)} %kappa.1, s32[16,8,128]{2,1,0:T(8,128)} %agg.1), custom_call_target="tpu_custom_call" | custom-call | tf_op jit(solution)/shard_map/pallas_call | solution.py:48
  8.2 1.9 %collective-permute-start = (f32[7,5,8,128]{3,2,1,0:T(8,128)S(1)}, f32[7,5,8,128]{3,2,1,0:T(8,128)S(1)}, u32[]{:S(2)}, u32[]{:S(2)}) collective-permute-start(f32[7,5,8,128]{3,2,1,0:T(8,128)S(1)} %get-tuple-element.53), channel_id=1, source_target_pairs={{0,16},{16,32},{32,48},{48,64},{64,80},{80,96},{96,112},{112,0},{1... | collective-permute-start | bytes 430088 | tf_op jit(solution)/shard_map/ppermute | solution.py:627
  10.1 4.2 %shard_map.96 = (f32[2,4096,128]{2,1,0:T(8,128)S(1)}, s32[8,256]{1,0:T(8,128)S(1)}, bf16[128,256]{1,0:T(8,128)(2,1)S(1)}) custom-call(s32[8,128]{1,0:T(8,128)S(1)} %get-tuple-element.49.flags, f32[192,4096]{1,0:T(8,128)} %bitcast.9, s32[4,48]{1,0:T(4,128)} %bitcast.11, s32[1,48]{1,0:T(1,128)} %bitcast.12), custom_call_target="tpu_custom_call" | custom-call | tf_op jit(solution)/shard_map/pallas_call | solution.py:48
  14.4 2.4 %shard_map.97 = (f32[22,3,8,128]{3,2,1,0:T(8,128)S(1)}, f32[22,8,128]{2,1,0:T(8,128)S(1)}, f32[22,8,128]{2,1,0:T(8,128)S(1)}, s32[22,8,128]{2,1,0:T(8,128)S(1)},...) custom-call(s32[8,128]{1,0:T(8,128)S(1)} %get-tuple-element.49.flags, ...), custom_call_target="tpu_custom_call" | custom-call | tf_op jit(solution)/shard_map/pallas_call | solution.py:48
  16.9 1.7 %collective-permute-start.2 = (f32[96,128]{1,0:T(8,128)S(1)}, f32[96,128]{1,0:T(8,128)S(1)}, u32[]{:S(2)}, u32[]{:S(2)}) collective-permute-start(f32[96,128]{1,0:T(8,128)S(1)} %get-tuple-element.67), channel_id=1, source_target_pairs={{0,4},{4,0},{8,12},{12,8},{1,5},{5,1},{9,13},{13,9},{2,6},{6,2},{1... | collective-permute-start | bytes 147464 | tf_op jit(solution)/shard_map/ppermute | solution.py:599
  18.5 2.2 %collective-permute-start.3 = (f32[96,128]{1,0:T(8,128)S(1)}, f32[96,128]{1,0:T(8,128)S(1)}, u32[]{:S(2)}, u32[]{:S(2)}) collective-permute-start(f32[96,128]{1,0:T(8,128)S(1)} %get-tuple-element.68), channel_id=1, source_target_pairs={{4,8},{8,4},{12,0},{0,12},{5,9},{9,5},{13,1},{1,13},{6,10},{10,6},... | collective-permute-start | bytes 147464 | tf_op jit(solution)/shard_map/ppermute | solution.py:600
  20.7 2.2 %collective-permute-start.1 = (f32[16,128]{1,0:T(8,128)S(1)}, f32[16,128]{1,0:T(8,128)S(1)}, u32[]{:S(2)}, u32[]{:S(2)}) collective-permute-start(f32[16,128]{1,0:T(8,128)S(1)} %get-tuple-element.65), channel_id=1, source_target_pairs={{1,2},{2,1},{3,0},{0,3},{5,6},{6,5},{7,4},{4,7},{9,10},{10,9},{11,... | collective-permute-start | bytes 24584 | tf_op jit(solution)/shard_map/ppermute | solution.py:598
  22.9 1.5 %collective-permute-start.4 = (f32[16,128]{1,0:T(8,128)S(1)}, f32[16,128]{1,0:T(8,128)S(1)}, u32[]{:S(2)}, u32[]{:S(2)}) collective-permute-start(f32[16,128]{1,0:T(8,128)S(1)} %get-tuple-element.69), channel_id=1, source_target_pairs={{0,1},{1,0},{2,3},{3,2},{4,5},{5,4},{6,7},{7,6},{8,9},{9,8},{10,11... | collective-permute-start | bytes 24584 | tf_op jit(solution)/shard_map/ppermute | solution.py:601
  24.4 0.9 %collective-permute-done.1.z2.az2 = f32[16,128]{1,0:T(8,128)S(1)} collective-permute-done((f32[16,128]{1,0:T(8,128)S(1)}, f32[16,128]{1,0:T(8,128)S(1)}, u32[]{:S(2)}, u32[]{:S(2)}) %collective-permute-start.1) | collective-permute-done | bytes 8224 | tf_op jit(solution)/shard_map/ppermute | solution.py:598
  25.3 2.6 %shard_map.99 = (f32[22,3,8,128]{3,2,1,0:T(8,128)S(1)}, f32[3,8,128]{2,1,0:T(8,128)S(1)}, f32[3,8,128]{2,1,0:T(8,128)S(1)}, f32[8,128]{1,0:T(8,128)S(1)}, f32[8,128]{1,0:T(8,128)S(1)}) custom-call(s32[8,128]{1,0:T(8,128)S(1)} %get-tuple-element.49.flags, f32[22,3,8,128]{3,2,1,0:T(8,128)S(1)} %get-tuple-element.57.force, ...), custom_call_target="tpu_custom_call" | custom-call | tf_op jit(solution)/shard_map/pallas_call | solution.py:48
  27.9 0.8 collective-permute-start.6
  29.3 2.1 %collective-permute-start.5 = (f32[8,128]{1,0:T(8,128)S(1)}, f32[8,128]{1,0:T(8,128)S(1)}, u32[]{:S(2)}, u32[]{:S(2)}) collective-permute-start(f32[8,128]{1,0:T(8,128)S(1)} %get-tuple-element.75), channel_id=1, source_target_pairs={{1,2},{2,1},{3,0},{0,3},{5,6},{6,5},{7,4},{4,7},{9,10},{10,9},{11,... | collective-permute-start | bytes 12296 | tf_op jit(solution)/shard_map/ppermute | solution.py:598
  31.4 1.6 %collective-permute-start.8 = (f32[8,128]{1,0:T(8,128)S(1)}, f32[8,128]{1,0:T(8,128)S(1)}, u32[]{:S(2)}, u32[]{:S(2)}) collective-permute-start(f32[8,128]{1,0:T(8,128)S(1)} %get-tuple-element.78), channel_id=1, source_target_pairs={{0,1},{1,0},{2,3},{3,2},{4,5},{5,4},{6,7},{7,6},{8,9},{9,8},{10,11... | collective-permute-start | bytes 12296 | tf_op jit(solution)/shard_map/ppermute | solution.py:601
  33.0 0.8 collective-permute-done.5.z2
  33.9 1.4 %shard_map.103.one = f32[32,128]{1,0:T(8,128)S(1)} custom-call(s32[8,128]{1,0:T(8,128)S(1)} %get-tuple-element.49.flags, f32[22,3,8,128]{3,2,1,0:T(8,128)S(1)} %get-tuple-element.57.force, f32[22,8,128]{2,1,0:T(8,128)S(1)} %get-tuple-element.58.weight, f32[22,3,8,128]{3,2,1,0:T(8,128)S(1)} %get-tuple-element.70.velocity.old, ...), custom_call_target="tpu_custom_call" | custom-call | tf_op jit(solution)/shard_map/pallas_call | solution.py:48
  35.8 0.8 collective-permute-done.9.two
  36.6 3.5 %collective-permute-start.10 = (f32[32,128]{1,0:T(8,128)S(1)}, f32[32,128]{1,0:T(8,128)S(1)}, u32[]{:S(2)}, u32[]{:S(2)}) collective-permute-start(f32[32,128]{1,0:T(8,128)S(1)} %shard_map.104.mine), channel_id=1, source_target_pairs={{0,114},{1,113},{2,112},{3,115},{4,118},{5,117},{6,116},{7,119},{8... | collective-permute-start | bytes 49160 | tf_op jit(solution)/shard_map/ppermute | solution.py:614
  40.2 1.2 %copy-done.1 = f32[512,512]{1,0:T(8,128)S(1)} copy-done((f32[512,512]{1,0:T(8,128)S(1)}, f32[512,512]{1,0:T(8,128)}, u32[]{:S(2)}) %copy-start.1) | copy-done | bytes 1048600
  41.8 2.1 %collective-permute-done.10.above = f32[32,128]{1,0:T(8,128)S(1)} collective-permute-done((f32[32,128]{1,0:T(8,128)S(1)}, f32[32,128]{1,0:T(8,128)S(1)}, u32[]{:S(2)}, u32[]{:S(2)}) %collective-permute-start.10) | collective-permute-done | bytes 16416 | tf_op jit(solution)/shard_map/ppermute | solution.py:614
  43.9 1.4 %collective-permute-done.11.across = f32[32,128]{1,0:T(8,128)S(1)} collective-permute-done((f32[32,128]{1,0:T(8,128)S(1)}, f32[32,128]{1,0:T(8,128)S(1)}, u32[]{:S(2)}, u32[]{:S(2)}) %collective-permute-start.11) | collective-permute-done | bytes 16416 | tf_op jit(solution)/shard_map/ppermute | solution.py:671
  45.5 1.2 %collective-permute-done.12.swapped = f32[24,128]{1,0:T(8,128)S(1)} collective-permute-done((f32[24,128]{1,0:T(8,128)S(1)}, f32[24,128]{1,0:T(8,128)S(1)}, u32[]{:S(2)}, u32[]{:S(2)}) %collective-permute-start.12) | collective-permute-done | bytes 12320 | tf_op jit(solution)/shard_map/ppermute | solution.py:675
  47.3 4.2 %collective-permute-start.13 = (f32[8,512]{1,0:T(8,128)S(1)}, f32[8,512]{1,0:T(8,128)S(1)}, u32[]{:S(2)}, u32[]{:S(2)}) collective-permute-start(f32[8,512]{1,0:T(8,128)S(1)} %shard_map.106.iterate), channel_id=1, source_target_pairs={{0,28},{1,21},{2,30},{3,23},{4,16},{5,25},{6,18},{7,27},{8,20},{9,... | collective-permute-start | bytes 49160 | tf_op jit(solution)/shard_map/ppermute | solution.py:614
  51.6 2.2 %collective-permute-start.14 = (f32[8,512]{1,0:T(8,128)S(1)}, f32[8,512]{1,0:T(8,128)S(1)}, u32[]{:S(2)}, u32[]{:S(2)}) collective-permute-start(f32[8,512]{1,0:T(8,128)S(1)} %shard_map.106.iterate), channel_id=1, source_target_pairs={{0,16},{1,5},{2,18},{3,7},{4,20},{5,9},{6,22},{7,11},{8,24},{9,13}... | collective-permute-start | bytes 49160 | tf_op jit(solution)/shard_map/ppermute | solution.py:614
  54.5 2.2 %shard_map.101.after.by_row = f32[2,4096,128]{2,1,0:T(8,128)S(1)} custom-call(bf16[512,512]{1,0:T(8,128)(2,1)S(1)} %get-tuple-element.74.after.high, f32[2,4096,128]{2,1,0:T(8,128)} %copy-done), custom_call_target="tpu_custom_call" | custom-call | tf_op jit(solution)/shard_map/pallas_call | solution.py:48
  56.7 0.8 collective-permute-done.15.c
  57.5 1.2 %collective-permute-done.16.swapped = f32[24,512]{1,0:T(8,128)S(1)} collective-permute-done((f32[24,512]{1,0:T(8,128)S(1)}, f32[24,512]{1,0:T(8,128)S(1)}, u32[]{:S(2)}, u32[]{:S(2)}) %collective-permute-start.16) | collective-permute-done | bytes 49184 | tf_op jit(solution)/shard_map/ppermute | solution.py:685
  58.7 3.1 %shard_map.108 = (f32[22,3,8,128]{3,2,1,0:T(8,128)S(1)}, f32[3,8,128]{2,1,0:T(8,128)S(1)}, f32[3,8,128]{2,1,0:T(8,128)S(1)}, f32[8,128]{1,0:T(8,128)S(1)}, f32[8,128]{1,0:T(8,128)S(1)}) custom-call(s32[8,128]{1,0:T(8,128)S(1)} %get-tuple-element.49.flags, f32[22,3,8,128]{3,2,1,0:T(8,128)S(1)} %get-tuple-element.57.force, ...), custom_call_target="tpu_custom_call" | custom-call | tf_op jit(solution)/shard_map/pallas_call | solution.py:48
  61.9 0.9 %collective-permute-start.18 = (f32[72,128]{1,0:T(8,128)S(1)}, f32[72,128]{1,0:T(8,128)S(1)}, u32[]{:S(2)}, u32[]{:S(2)}) collective-permute-start(f32[72,128]{1,0:T(8,128)S(1)} %get-tuple-element.86), channel_id=1, source_target_pairs={{0,4},{4,0},{8,12},{12,8},{1,5},{5,1},{9,13},{13,9},{2,6},{6,2},{1... | collective-permute-start | bytes 110600 | tf_op jit(solution)/shard_map/ppermute | solution.py:599
  62.7 1.3 %collective-permute-start.19 = (f32[72,128]{1,0:T(8,128)S(1)}, f32[72,128]{1,0:T(8,128)S(1)}, u32[]{:S(2)}, u32[]{:S(2)}) collective-permute-start(f32[72,128]{1,0:T(8,128)S(1)} %get-tuple-element.87), channel_id=1, source_target_pairs={{4,8},{8,4},{12,0},{0,12},{5,9},{9,5},{13,1},{1,13},{6,10},{10,6},... | collective-permute-start | bytes 110600 | tf_op jit(solution)/shard_map/ppermute | solution.py:600
  65.3 3.2 %collective-permute-done.17.z2 = f32[8,128]{1,0:T(8,128)S(1)} collective-permute-done((f32[8,128]{1,0:T(8,128)S(1)}, f32[8,128]{1,0:T(8,128)S(1)}, u32[]{:S(2)}, u32[]{:S(2)}) %collective-permute-start.17) | collective-permute-done | bytes 4128 | tf_op jit(solution)/shard_map/ppermute | solution.py:598
  68.5 2.5 %shard_map.110 = (f32[3,12,8,128]{3,2,1,0:T(8,128)S(1)}, f32[3,4,8,128]{3,2,1,0:T(8,128)S(1)}, f32[3,8,128]{2,1,0:T(8,128)S(1)}) custom-call(s32[8,128]{1,0:T(8,128)S(1)} %get-tuple-element.49.flags, f32[22,3,8,128]{3,2,1,0:T(8,128)S(1)} %get-tuple-element.57.force, f32[22,8,128]{2,1,0:T(8,128)S(1)} %get-tuple-element.58.weight, ...), custom_call_target="tpu_custom_call" | custom-call | tf_op jit(solution)/shard_map/pallas_call | solution.py:48
  71.8 5.5 %collective-permute-done.21.tail = f32[3,4,8,128]{3,2,1,0:T(8,128)S(1)} collective-permute-done((f32[3,4,8,128]{3,2,1,0:T(8,128)S(1)}, f32[3,4,8,128]{3,2,1,0:T(8,128)S(1)}, u32[]{:S(2)}, u32[]{:S(2)}) %collective-permute-start.21) | collective-permute-done | bytes 49184 | tf_op jit(solution)/shard_map/ppermute | solution.py:698
  (39 shorter events, 6.1 us)
Async XLA Ops:
  7.2 33.1 %all-gather.2.cloned.1.call-start = ((), (), s32[]{:S(2)}) async-start(), calls=%async_computation | async-start | bytes 1310720 | tf_op jit(solution)/shard_map/all_gather | solution.py:626
  8.2 6.1 %collective-permute-start = (f32[7,5,8,128]{3,2,1,0:T(8,128)S(1)}, f32[7,5,8,128]{3,2,1,0:T(8,128)S(1)}, u32[]{:S(2)}, u32[]{:S(2)}) collective-permute-start(f32[7,5,8,128]{3,2,1,0:T(8,128)S(1)} %get-tuple-element.53), channel_id=1, source_target_pairs={{0,16},{16,32},{32,48},{48,64},{64,80},{80,96},{96,112},{112,0},{1... | collective-permute-start | bytes 430088 | tf_op jit(solution)/shard_map/ppermute | solution.py:627
  14.4 13.5 %copy-start = (f32[2,4096,128]{2,1,0:T(8,128)}, f32[2,4096,128]{2,1,0:T(8,128)S(1)}, u32[]{:S(2)}) copy-start(f32[2,4096,128]{2,1,0:T(8,128)S(1)} %get-tuple-element.54.by_row.far) | copy-start | bytes 12582916
  14.4 19.5 %copy-start.2 = (f32[1,1,128]{2,1,0:T(1,128)S(1)}, f32[1,1,128]{2,1,0:T(1,128)}, u32[]{:S(2)}) copy-start(f32[1,1,128]{2,1,0:T(1,128)} %param.15) | copy-start | bytes 1540
  16.9 8.4 %collective-permute-start.2 = (f32[96,128]{1,0:T(8,128)S(1)}, f32[96,128]{1,0:T(8,128)S(1)}, u32[]{:S(2)}, u32[]{:S(2)}) collective-permute-start(f32[96,128]{1,0:T(8,128)S(1)} %get-tuple-element.67), channel_id=1, source_target_pairs={{0,4},{4,0},{8,12},{12,8},{1,5},{5,1},{9,13},{13,9},{2,6},{6,2},{1... | collective-permute-start | bytes 147464 | tf_op jit(solution)/shard_map/ppermute | solution.py:599
  18.5 6.8 %collective-permute-start.3 = (f32[96,128]{1,0:T(8,128)S(1)}, f32[96,128]{1,0:T(8,128)S(1)}, u32[]{:S(2)}, u32[]{:S(2)}) collective-permute-start(f32[96,128]{1,0:T(8,128)S(1)} %get-tuple-element.68), channel_id=1, source_target_pairs={{4,8},{8,4},{12,0},{0,12},{5,9},{9,5},{13,1},{1,13},{6,10},{10,6},... | collective-permute-start | bytes 147464 | tf_op jit(solution)/shard_map/ppermute | solution.py:600
  20.7 4.6 %collective-permute-start.1 = (f32[16,128]{1,0:T(8,128)S(1)}, f32[16,128]{1,0:T(8,128)S(1)}, u32[]{:S(2)}, u32[]{:S(2)}) collective-permute-start(f32[16,128]{1,0:T(8,128)S(1)} %get-tuple-element.65), channel_id=1, source_target_pairs={{1,2},{2,1},{3,0},{0,3},{5,6},{6,5},{7,4},{4,7},{9,10},{10,9},{11,... | collective-permute-start | bytes 24584 | tf_op jit(solution)/shard_map/ppermute | solution.py:598
  22.9 2.4 %collective-permute-start.4 = (f32[16,128]{1,0:T(8,128)S(1)}, f32[16,128]{1,0:T(8,128)S(1)}, u32[]{:S(2)}, u32[]{:S(2)}) collective-permute-start(f32[16,128]{1,0:T(8,128)S(1)} %get-tuple-element.69), channel_id=1, source_target_pairs={{0,1},{1,0},{2,3},{3,2},{4,5},{5,4},{6,7},{7,6},{8,9},{9,8},{10,11... | collective-permute-start | bytes 24584 | tf_op jit(solution)/shard_map/ppermute | solution.py:601
  27.9 5.9 %collective-permute-start.6 = (f32[72,128]{1,0:T(8,128)S(1)}, f32[72,128]{1,0:T(8,128)S(1)}, u32[]{:S(2)}, u32[]{:S(2)}) collective-permute-start(f32[72,128]{1,0:T(8,128)S(1)} %get-tuple-element.76), channel_id=1, source_target_pairs={{0,4},{4,0},{8,12},{12,8},{1,5},{5,1},{9,13},{13,9},{2,6},{6,2},{1... | collective-permute-start | bytes 110600 | tf_op jit(solution)/shard_map/ppermute | solution.py:599
  28.7 5.2 %collective-permute-start.7 = (f32[72,128]{1,0:T(8,128)S(1)}, f32[72,128]{1,0:T(8,128)S(1)}, u32[]{:S(2)}, u32[]{:S(2)}) collective-permute-start(f32[72,128]{1,0:T(8,128)S(1)} %get-tuple-element.77), channel_id=1, source_target_pairs={{4,8},{8,4},{12,0},{0,12},{5,9},{9,5},{13,1},{1,13},{6,10},{10,6},... | collective-permute-start | bytes 110600 | tf_op jit(solution)/shard_map/ppermute | solution.py:600
  29.3 4.5 %collective-permute-start.5 = (f32[8,128]{1,0:T(8,128)S(1)}, f32[8,128]{1,0:T(8,128)S(1)}, u32[]{:S(2)}, u32[]{:S(2)}) collective-permute-start(f32[8,128]{1,0:T(8,128)S(1)} %get-tuple-element.75), channel_id=1, source_target_pairs={{1,2},{2,1},{3,0},{0,3},{5,6},{6,5},{7,4},{4,7},{9,10},{10,9},{11,... | collective-permute-start | bytes 12296 | tf_op jit(solution)/shard_map/ppermute | solution.py:598
  31.4 2.4 %collective-permute-start.8 = (f32[8,128]{1,0:T(8,128)S(1)}, f32[8,128]{1,0:T(8,128)S(1)}, u32[]{:S(2)}, u32[]{:S(2)}) collective-permute-start(f32[8,128]{1,0:T(8,128)S(1)} %get-tuple-element.78), channel_id=1, source_target_pairs={{0,1},{1,0},{2,3},{3,2},{4,5},{5,4},{6,7},{7,6},{8,9},{9,8},{10,11... | collective-permute-start | bytes 12296 | tf_op jit(solution)/shard_map/ppermute | solution.py:601
  35.3 1.3 %collective-permute-start.9 = (f32[32,128]{1,0:T(8,128)S(1)}, f32[32,128]{1,0:T(8,128)S(1)}, u32[]{:S(2)}, u32[]{:S(2)}) collective-permute-start(f32[32,128]{1,0:T(8,128)S(1)} %shard_map.103.one), channel_id=1, source_target_pairs={{0,1},{1,0},{2,3},{3,2},{4,5},{5,4},{6,7},{7,6},{8,9},{9,8},{10,11... | collective-permute-start | bytes 49160 | tf_op jit(solution)/shard_map/ppermute | solution.py:669
  36.6 7.3 %collective-permute-start.10 = (f32[32,128]{1,0:T(8,128)S(1)}, f32[32,128]{1,0:T(8,128)S(1)}, u32[]{:S(2)}, u32[]{:S(2)}) collective-permute-start(f32[32,128]{1,0:T(8,128)S(1)} %shard_map.104.mine), channel_id=1, source_target_pairs={{0,114},{1,113},{2,112},{3,115},{4,118},{5,117},{6,116},{7,119},{8... | collective-permute-start | bytes 49160 | tf_op jit(solution)/shard_map/ppermute | solution.py:614
  40.1 5.2 %collective-permute-start.11 = (f32[32,128]{1,0:T(8,128)S(1)}, f32[32,128]{1,0:T(8,128)S(1)}, u32[]{:S(2)}, u32[]{:S(2)}) collective-permute-start(f32[32,128]{1,0:T(8,128)S(1)} %shard_map.104.mine), channel_id=1, source_target_pairs={{0,2},{1,3},{2,0},{3,1},{4,6},{5,7},{6,4},{7,5},{8,10},{9,11},{10,... | collective-permute-start | bytes 49160 | tf_op jit(solution)/shard_map/ppermute | solution.py:671
  40.2 1.2 %copy-start.1 = (f32[512,512]{1,0:T(8,128)S(1)}, f32[512,512]{1,0:T(8,128)}, u32[]{:S(2)}) copy-start(f32[512,512]{1,0:T(8,128)} %all-gather.2.cloned.1.call-done.rows) | copy-start | bytes 3145732
  45.4 1.2 %collective-permute-start.12 = (f32[24,128]{1,0:T(8,128)S(1)}, f32[24,128]{1,0:T(8,128)S(1)}, u32[]{:S(2)}, u32[]{:S(2)}) collective-permute-start(f32[24,128]{1,0:T(8,128)S(1)} %get-tuple-element.80.passed), channel_id=1, source_target_pairs={{0,1},{1,0},{2,3},{3,2},{4,5},{5,4},{6,7},{7,6},{8,9},{9,8},{10,11... | collective-permute-start | bytes 36872 | tf_op jit(solution)/shard_map/ppermute | solution.py:675
  47.3 9.4 %collective-permute-start.13 = (f32[8,512]{1,0:T(8,128)S(1)}, f32[8,512]{1,0:T(8,128)S(1)}, u32[]{:S(2)}, u32[]{:S(2)}) collective-permute-start(f32[8,512]{1,0:T(8,128)S(1)} %shard_map.106.iterate), channel_id=1, source_target_pairs={{0,28},{1,21},{2,30},{3,23},{4,16},{5,25},{6,18},{7,27},{8,20},{9,... | collective-permute-start | bytes 49160 | tf_op jit(solution)/shard_map/ppermute | solution.py:614
  51.6 5.2 %collective-permute-start.14 = (f32[8,512]{1,0:T(8,128)S(1)}, f32[8,512]{1,0:T(8,128)S(1)}, u32[]{:S(2)}, u32[]{:S(2)}) collective-permute-start(f32[8,512]{1,0:T(8,128)S(1)} %shard_map.106.iterate), channel_id=1, source_target_pairs={{0,16},{1,5},{2,18},{3,7},{4,20},{5,9},{6,22},{7,11},{8,24},{9,13}... | collective-permute-start | bytes 49160 | tf_op jit(solution)/shard_map/ppermute | solution.py:614
  53.8 3.7 %collective-permute-start.15 = (f32[8,512]{1,0:T(8,128)S(1)}, f32[8,512]{1,0:T(8,128)S(1)}, u32[]{:S(2)}, u32[]{:S(2)}) collective-permute-start(f32[8,512]{1,0:T(8,128)S(1)} %shard_map.106.iterate), channel_id=1, source_target_pairs={{0,12},{1,5},{2,14},{3,7},{4,0},{5,9},{6,2},{7,11},{8,4},{9,13},{1... | collective-permute-start | bytes 49160 | tf_op jit(solution)/shard_map/ppermute | solution.py:614
  57.5 1.2 %collective-permute-start.16 = (f32[24,512]{1,0:T(8,128)S(1)}, f32[24,512]{1,0:T(8,128)S(1)}, u32[]{:S(2)}, u32[]{:S(2)}) collective-permute-start(f32[24,512]{1,0:T(8,128)S(1)} %shard_map.107.got), channel_id=1, source_target_pairs={{0,1},{1,0},{2,3},{3,2},{4,5},{5,4},{6,7},{7,6},{8,9},{9,8},{10,11... | collective-permute-start | bytes 147464 | tf_op jit(solution)/shard_map/ppermute | solution.py:685
  61.9 6.7 %collective-permute-start.18 = (f32[72,128]{1,0:T(8,128)S(1)}, f32[72,128]{1,0:T(8,128)S(1)}, u32[]{:S(2)}, u32[]{:S(2)}) collective-permute-start(f32[72,128]{1,0:T(8,128)S(1)} %get-tuple-element.86), channel_id=1, source_target_pairs={{0,4},{4,0},{8,12},{12,8},{1,5},{5,1},{9,13},{13,9},{2,6},{6,2},{1... | collective-permute-start | bytes 110600 | tf_op jit(solution)/shard_map/ppermute | solution.py:599
  62.7 5.8 %collective-permute-start.19 = (f32[72,128]{1,0:T(8,128)S(1)}, f32[72,128]{1,0:T(8,128)S(1)}, u32[]{:S(2)}, u32[]{:S(2)}) collective-permute-start(f32[72,128]{1,0:T(8,128)S(1)} %get-tuple-element.87), channel_id=1, source_target_pairs={{4,8},{8,4},{12,0},{0,12},{5,9},{9,5},{13,1},{1,13},{6,10},{10,6},... | collective-permute-start | bytes 110600 | tf_op jit(solution)/shard_map/ppermute | solution.py:600
  64.0 4.5 %collective-permute-start.17 = (f32[8,128]{1,0:T(8,128)S(1)}, f32[8,128]{1,0:T(8,128)S(1)}, u32[]{:S(2)}, u32[]{:S(2)}) collective-permute-start(f32[8,128]{1,0:T(8,128)S(1)} %get-tuple-element.85), channel_id=1, source_target_pairs={{1,2},{2,1},{3,0},{0,3},{5,6},{6,5},{7,4},{4,7},{9,10},{10,9},{11,... | collective-permute-start | bytes 12296 | tf_op jit(solution)/shard_map/ppermute | solution.py:598
  64.7 3.8 %collective-permute-start.20 = (f32[8,128]{1,0:T(8,128)S(1)}, f32[8,128]{1,0:T(8,128)S(1)}, u32[]{:S(2)}, u32[]{:S(2)}) collective-permute-start(f32[8,128]{1,0:T(8,128)S(1)} %get-tuple-element.88), channel_id=1, source_target_pairs={{0,1},{1,0},{2,3},{3,2},{4,5},{5,4},{6,7},{7,6},{8,9},{9,8},{10,11... | collective-permute-start | bytes 12296 | tf_op jit(solution)/shard_map/ppermute | solution.py:601
  71.0 6.3 %collective-permute-start.21 = (f32[3,4,8,128]{3,2,1,0:T(8,128)S(1)}, f32[3,4,8,128]{3,2,1,0:T(8,128)S(1)}, u32[]{:S(2)}, u32[]{:S(2)}) collective-permute-start(f32[3,4,8,128]{3,2,1,0:T(8,128)S(1)} %get-tuple-element.89), channel_id=1, source_target_pairs={{0,112},{16,0},{32,16},{48,32},{64,48},{80,64},{96,80},{112,96},{1... | collective-permute-start | bytes 147464 | tf_op jit(solution)/shard_map/ppermute | solution.py:698
Sparse Core Ops, SparseCore 0:
  9.7 23.2 all-gather.1

commit v3 on v2

--- a/solution.py
+++ b/solution.py
@@ -417,7 +417,7 @@
 
 
 def restrict_kernel(
-    flags, force, weight, velocity, mult, mult_up, agg, diag, z2, y1, y2, z1, out, res,
+    after, flags, force, weight, velocity, mult, mult_up, agg, diag, z2, y1, y2, z1, out, res,
 ):
     halo = sides(flags, y1, y2, z1, z2)
     for p in range(TAIL - 3, NP - 2):
@@ -468,7 +468,7 @@
     out[24:32] = jnp.where(sub == flags[6:7], jnp.broadcast_to(diag[...], (8, 128)), 0.0)
 
 
-def gather_sums_kernel(mine, above, across, after, kept, passed):
+def gather_sums_kernel(mine, above, across, kept, passed):
     kept[...] = mine[...] + across[...]
     lane = lax.broadcasted_iota(jnp.int32, (24, 128), 1)
     passed[...] = jnp.where(lane < 64, pltpu.roll(above[0:24], 64, 1), 0.0)
@@ -478,7 +478,7 @@
     out[...] = one[...] + two[...]
 
 
-def join_kernel(a, b, c, after, out):
+def join_kernel(a, b, c, out):
     out[0:8], out[8:16], out[16:24] = a[...], b[...], c[...]
 
 
@@ -486,16 +486,18 @@
     return call(add_kernel, [(one.shape, F32)], n_in=2)(one, two)[0]
 
 
-def pack_kernel(force, kappa, agg, out, force_near, kappa_near, agg_near, flags, sems):
+def pack_kernel(force, kappa, agg, matrix, out, force_near, kappa_near, agg_near, rows, flags, sems):
     copies = [
         pltpu.make_async_copy(far, near, sems.at[i])
-        for i, (far, near) in enumerate(((force, force_near), (kappa, kappa_near), (agg, agg_near)))
+        for i, (far, near) in enumerate(
+            ((force, force_near), (kappa, kappa_near), (agg, agg_near), (matrix, rows))
+        )
     ]
     for copy in copies:
         copy.start()
     gy, gz = lax.axis_index("gy"), lax.axis_index("gz")
     ny, nz = lax.axis_size("gy"), lax.axis_size("gz")
-    facts = (gy % 2 == 0, gz % 2 == 0, gy > 0, gy < ny - 1, gz > 0, gz < nz - 1, gz, gz)
+    facts = (gy % 2 == 1, gz % 2 == 0, gy > 0, gy < ny - 1, gz > 0, gz < nz - 1, gz, gz < nz // 2)
     for row, fact in enumerate(facts):
         flags[row : row + 1, :] = jnp.full((1, 128), fact.astype(jnp.int32), jnp.int32)
     for copy in copies:
@@ -508,11 +510,20 @@
         out[p, 4] = agg_near[start + p].astype(F32)
 
 
-def split_matrix_kernel(rows, high, low):
-    a = rows[...].T
-    h = a.astype(BF16)
-    high[...] = h
-    low[...] = (a - h.astype(F32)).astype(BF16)
+def stack_kernel(one, two, out):
+    out[0:128], out[128:256] = one[...], two[...]
+
+
+def split_matrix_kernel(flags, mine, other, high, low):
+    core_zero, first_half = yes(flags, 1, (256, NAGG)), yes(flags, 7, (128, NAGG))
+    sets = jnp.where(core_zero, mine[...], other[...]), jnp.where(core_zero, other[...], mine[...])
+    for b in range(4):
+        rows = sets[b % 2]
+        near, far = (rows[0:128], rows[128:256]) if b < 2 else (rows[128:256], rows[0:128])
+        a = jnp.where(first_half, near, far).T
+        h = a.astype(BF16)
+        high[:, 128 * b : 128 * b + 128] = h
+        low[:, 128 * b : 128 * b + 128] = (a - h.astype(F32)).astype(BF16)
 
 
 def solve_kernel(kept, passed, swapped, high, low, out, rhs):
@@ -556,12 +567,6 @@
     return jnp.where(tile < 2, jnp.where(tile == 0, got[0], got[1]), jnp.where(tile == 2, got[2], got[3]))
 
 
-def reload_kernel(after, far, near, sem):
-    copy = pltpu.make_async_copy(far, near, sem)
-    copy.start()
-    copy.wait()
-
-
 def write_head_kernel(head, mult, velocity, out_mult, sems):
     copies = [
         pltpu.make_async_copy(head, velocity.at[:, pl.ds(0, 16 - RET)], sems.at[0]),
@@ -596,8 +601,8 @@
 def trade(y1, y2, z1, z2):
     return [
         lax.ppermute(z2, "gz", swaps("gz", 1)),
-        lax.ppermute(y1, "gy", swaps("gy", 0)),
-        lax.ppermute(y2, "gy", swaps("gy", 1)),
+        lax.ppermute(y1, "gy", swaps("gy", 1)),
+        lax.ppermute(y2, "gy", swaps("gy", 0)),
         lax.ppermute(z1, "gz", swaps("gz", 0)),
     ]
 
@@ -615,16 +620,15 @@
 
 
 def shards(force, kappa, mortar_blocks, mortar_index, mortar_count, agg_map, coarse_matrix, coarse_diag):
-    tail_in, force, kappa, agg_map, flags = call(
+    tail_in, force, kappa, agg_map, rows, flags = call(
         pack_kernel,
         [((TAIL, 5, 8, 128), F32), (force.shape, F32), (kappa.shape, F32), (agg_map.shape, jnp.int32),
-         ((8, 128), jnp.int32)],
-        [pltpu.SemaphoreType.DMA((3,))],
-        n_far=3,
-    )(force, kappa, agg_map)
-    rows, flags = lax.optimization_barrier((coarse_matrix.reshape(128, NAGG), flags))
-    rows = lax.all_gather(rows, "gz", tiled=True)
+         ((128, NAGG), F32), ((8, 128), jnp.int32)],
+        [pltpu.SemaphoreType.DMA((4,))],
+        n_far=4,
+    )(force, kappa, agg_map, coarse_matrix.reshape(128, NAGG))
     tail_in = lax.ppermute(tail_in, "gx", ring("gx", 1))
+    half = lax.ppermute(rows, "gz", ring("gz", 2))
 
     by_row, spots, place = call(
         prepare_kernel,
@@ -640,11 +644,6 @@
         mortar_count.reshape(1, 48),
     )
 
-    k_high, k_low = call(split_matrix_kernel, [((NAGG, NAGG), BF16)] * 2, n_in=1)(rows)
-    by_row_again = call(
-        reload_kernel, [((2, 4096, 128), F32)], [pltpu.SemaphoreType.DMA], n_in=1, n_far=1
-    )(k_high, by_row)[0]
-
     field = ((NP, 3, 8, 128), F32)
     plane = ((3, 8, 128), F32)
     turned = ((64, 128), F32)
@@ -653,24 +652,29 @@
     out = call(
         first_sweep_kernel,
         [field, ((NP, 8, 128), F32), ((NP, 8, 128), F32), ((NP, 8, 128), jnp.int32), field, plane, plane,
-         turned, turned, z_more, z_more],
+         turned, turned, z_more, ((LINES + ROWS + 8, 128), F32)],
         n_in=8,
     )(flags, force, kappa, agg_map, tail_in, by_row, spots, place)
     force_e, weight, inverse, agg, velocity, mult, mult_up, face, inverse_t = out[:9]
+    half, velocity = lax.optimization_barrier((half, velocity))
+    rows = call(stack_kernel, [((256, NAGG), F32)], n_in=2)(rows, half)[0]
+    k_high, k_low = call(split_matrix_kernel, [((NAGG, NAGG), BF16)] * 2, n_in=3)(
+        flags, rows, lax.ppermute(rows, "gz", swaps("gz", 0))
+    )
     lines = call(lines_and_labels_kernel, [y_more, y_more], n_in=3)(flags, velocity, agg)
     labels = trade(*lines, *out[9:])
     velocity, mult, mult_up, *msgs = call(
-        second_sweep_kernel, [field, plane, plane, z_msg, z_msg], n_in=16
+        second_sweep_kernel, [field, plane, plane, z_msg, ((LINES + 8, 128), F32)], n_in=16
     )(flags, force_e, weight, inverse, velocity, mult, mult_up, face, inverse_t, by_row, spots, place, *labels)
     edges = trade(*call(lines_kernel, [y_msg, y_msg], n_in=2)(flags, velocity), *msgs)
     sums = call(
-        restrict_kernel, [((32, 128), F32)], [pltpu.VMEM((NP, 3, 8, 128), F32)], n_in=12
-    )(flags, force_e, weight, velocity, mult, mult_up, agg, coarse_diag.reshape(1, 128), *edges)[0]
+        restrict_kernel, [((32, 128), F32)], [pltpu.VMEM((NP, 3, 8, 128), F32)], n_in=13
+    )(k_high, flags, force_e, weight, velocity, mult, mult_up, agg, coarse_diag.reshape(1, 128), *edges)[0]
     sums = add(sums, lax.ppermute(sums, "gz", swaps("gz", 0)))
     above = by_core(sums, (-1, 0, 2), (-1, 0, 0))
     across = lax.ppermute(sums, "gz", ring("gz", 2))
-    kept, passed = call(gather_sums_kernel, [((32, 128), F32), ((24, 128), F32)], n_in=4)(
-        sums, above, across, k_high
+    kept, passed = call(gather_sums_kernel, [((32, 128), F32), ((24, 128), F32)], n_in=3)(
+        sums, above, across
     )
     swapped = lax.ppermute(passed, "gz", swaps("gz", 0))
     iterate = call(solve_kernel, [((8, NAGG), F32)], [pltpu.VMEM((8, NAGG), F32)], n_in=5)(
@@ -681,20 +685,20 @@
         by_core(iterate, (1, 0, 0), (0, 1, 0)),
         by_core(iterate, (0, -1, 0), (0, 1, 0)),
     ]
-    got = call(join_kernel, [((24, NAGG), F32)], n_in=4)(*got, by_row_again)[0]
+    got = call(join_kernel, [((24, NAGG), F32)], n_in=3)(*got)[0]
     swapped = lax.ppermute(got, "gz", swaps("gz", 0))
     velocity, mult, mult_up, *msgs = call(
-        third_sweep_kernel, [field, plane, plane, z_msg, z_msg],
+        third_sweep_kernel, [field, plane, plane, z_msg, ((LINES + 8, 128), F32)],
         [pltpu.VMEM((NP, 3, 8, 128), F32)], n_in=24,
     )(
-        flags, force_e, weight, inverse, velocity, mult, mult_up, face, inverse_t, by_row_again, spots, place,
+        flags, force_e, weight, inverse, velocity, mult, mult_up, face, inverse_t, by_row, spots, place,
         *edges, *labels, agg, iterate, got, swapped,
     )
     edges = trade(*call(lines_kernel, [y_msg, y_msg], n_in=2)(flags, velocity), *msgs)
     head, tail, mult = call(
         last_sweep_kernel, [((3, 16 - RET, 8, 128), F32), ((3, RET, 8, 128), F32), plane],
         [pltpu.VMEM((NP, 3, 8, 128), F32), pltpu.VMEM((3, 8, 128), F32)], n_in=16,
-    )(flags, force_e, weight, inverse, velocity, mult, mult_up, face, inverse_t, by_row_again, spots, place, *edges)
+    )(flags, force_e, weight, inverse, velocity, mult, mult_up, face, inverse_t, by_row, spots, place, *edges)
     tail = lax.ppermute(tail, "gx", ring("gx", -1))
     shapes = [pltpu.HBM((3, 16, 8, 128), F32), pltpu.HBM((3, 8, 128), F32)]
     velocity, mult = pl.pallas_call(

time: 85 us -> 74.9 us (0.88)
  between operations: 14.2 us -> 0.95 us
  waiting for transfers between devices: 18 us -> 25.9 us
  Pallas kernels: 21.9 us -> 19.9 us
  starting transfers between devices: 29.4 us -> 28.1 us
  local copies, waits for them, and re-layouts: 1.24 us -> 0.01 us
    ppermute x6 -> x8, waiting for transfers between devices: 0.03 us -> 7.46 us  [the longest x3 5.2 us: trade(): lax.ppermute(y1, 'gy', swaps('gy', 1))]
    ppermute x3, waiting for transfers between devices: 4.9 us -> 0.01 us  [trade(): lax.ppermute(z2, 'gz', swaps('gz', 1))]
    ppermute x4, waiting for transfers between devices: 2.88 us -> 6.51 us  [by_core(): return lax.ppermute(x, ('gx', 'gy', 'gz'), pairs)]
    ppermute x6 -> x8, starting transfers between devices: 7.33 us -> 10.2 us  [the longest x3 6.06 us: trade(): lax.ppermute(y1, 'gy', swaps('gy', 1))]
    ppermute x3, waiting for transfers between devices: 0.01 us -> 2.73 us  [trade(): lax.ppermute(z1, 'gz', swaps('gz', 0))]
    ppermute x3, starting transfers between devices: 3.74 us -> 1.37 us  [trade(): lax.ppermute(z1, 'gz', swaps('gz', 0))]
    pallas_call x16, Pallas kernels: 20.5 us -> 18.6 us  [run(): return kernel(*args[:n_smem], *held, *far)]
    ppermute x4, starting transfers between devices: 10.7 us -> 8.9 us  [by_core(): return lax.ppermute(x, ('gx', 'gy', 'gz'), pairs)]
  transfers between devices with their start and end apart: 23 -> 24, of which waited for: 10 -> 18; matrix products, arithmetic and copies ran while one was open for 0% -> 0% of each run, Pallas kernels for 16% -> 14%
where the time goes in v3:
time: 74.9 us; the launch traced here: 74.8 us
  starting transfers between devices  28.1 us (38%)
  waiting for transfers between devices  25.9 us (35%)
  Pallas kernels  19.9 us (27%)
  between operations  0.95 us (1%)
    pallas_call x16, Pallas kernels, run(): return kernel(*args[:n_smem], *held, *far)  18.6 us
    ppermute x4, starting transfers between devices, by_core(): return lax.ppermute(x, ('gx', 'gy', 'gz'), pairs)  8.9 us
    ppermute x4, waiting for transfers between devices, by_core(): return lax.ppermute(x, ('gx', 'gy', 'gz'), pairs)  6.51 us
    ppermute x3, starting transfers between devices, trade(): lax.ppermute(y1, 'gy', swaps('gy', 1))  6.06 us
    ppermute x1, waiting for transfers between devices, shards(): tail = lax.ppermute(tail, 'gx', ring('gx', -1))  5.5 us
    ppermute x3, waiting for transfers between devices, trade(): lax.ppermute(y1, 'gy', swaps('gy', 1))  5.2 us
    ppermute x3, starting transfers between devices, trade(): lax.ppermute(z2, 'gz', swaps('gz', 1))  4.26 us
    ppermute x1, starting transfers between devices, shards(): half = lax.ppermute(rows, 'gz', ring('gz', 2))  3.96 us
  transfers between devices with their start and end apart: 24, of which 18 were waited for; matrix products, arithmetic and copies ran while one was open for 0% of the time, Pallas kernels for 14%

profile of v3, /device:TPU:6, one launch (start us, length us, event | category | flops | bytes accessed | tf_op | source)
XLA Modules:
  0.0 74.8 jit_solution(282122264043681953)
XLA Ops:
  0.6 1.2 %shard_map.95 = (f32[7,5,8,128]{3,2,1,0:T(8,128)S(1)}, f32[3,16,8,128]{3,2,1,0:T(8,128)S(1)}, f32[16,8,128]{2,1,0:T(8,128)S(1)}, s32[16,8,128]{2,1,0:T(8,128)S(1...) custom-call(f32[3,16,8,128]{3,2,1,0:T(8,128)} %force.1, f32[16,8,128]{2,1,0:T(8,128)} %kappa.1, s32[16,8,128]{2,1,0:T(8,128)} %agg.1, ...), custom_call_target="tpu_custom_call" | custom-call | tf_op jit(solution)/shard_map/pallas_call | solution.py:48
  1.8 4.0 %collective-permute-start.1 = (f32[128,512]{1,0:T(8,128)S(1)}, f32[128,512]{1,0:T(8,128)S(1)}, u32[]{:S(2)}, u32[]{:S(2)}) collective-permute-start(f32[128,512]{1,0:T(8,128)S(1)} %get-tuple-element.60.one), channel_id=1, source_target_pairs={{0,2},{1,3},{2,0},{3,1},{4,6},{5,7},{6,4},{7,5},{8,10},{9,11},{10,... | collective-permute-start | bytes 786440 | tf_op jit(solution)/shard_map/ppermute | solution.py:631
  5.8 0.9 %collective-permute-start = (f32[7,5,8,128]{3,2,1,0:T(8,128)S(1)}, f32[7,5,8,128]{3,2,1,0:T(8,128)S(1)}, u32[]{:S(2)}, u32[]{:S(2)}) collective-permute-start(f32[7,5,8,128]{3,2,1,0:T(8,128)S(1)} %get-tuple-element.53), channel_id=1, source_target_pairs={{0,16},{16,32},{32,48},{48,64},{64,80},{80,96},{96,112},{112,0},{1... | collective-permute-start | bytes 430088 | tf_op jit(solution)/shard_map/ppermute | solution.py:630
  6.7 4.2 %shard_map.96 = (f32[2,4096,128]{2,1,0:T(8,128)S(1)}, s32[8,256]{1,0:T(8,128)S(1)}, bf16[128,256]{1,0:T(8,128)(2,1)S(1)}) custom-call(s32[8,128]{1,0:T(8,128)S(1)} %get-tuple-element.49.flags, f32[192,4096]{1,0:T(8,128)} %bitcast.9, s32[4,48]{1,0:T(4,128)} %bitcast.11, s32[1,48]{1,0:T(1,128)} %bitcast.12), custom_call_target="tpu_custom_call" | custom-call | tf_op jit(solution)/shard_map/pallas_call | solution.py:48
  11.0 2.4 %shard_map.97 = (f32[22,3,8,128]{3,2,1,0:T(8,128)S(1)}, f32[22,8,128]{2,1,0:T(8,128)S(1)}, f32[22,8,128]{2,1,0:T(8,128)S(1)}, s32[22,8,128]{2,1,0:T(8,128)S(1)},...) custom-call(s32[8,128]{1,0:T(8,128)S(1)} %get-tuple-element.49.flags, ...), custom_call_target="tpu_custom_call" | custom-call | tf_op jit(solution)/shard_map/pallas_call | solution.py:48
  13.5 2.0 %collective-permute-start.2 = (f32[104,128]{1,0:T(8,128)S(1)}, f32[104,128]{1,0:T(8,128)S(1)}, u32[]{:S(2)}, u32[]{:S(2)}) collective-permute-start(f32[104,128]{1,0:T(8,128)S(1)} %get-tuple-element.67), channel_id=1, source_target_pairs={{1,2},{2,1},{3,0},{0,3},{5,6},{6,5},{7,4},{4,7},{9,10},{10,9},{11,... | collective-permute-start | bytes 159752 | tf_op jit(solution)/shard_map/ppermute | solution.py:603
  15.6 3.1 %collective-permute-start.3 = (f32[96,128]{1,0:T(8,128)S(1)}, f32[96,128]{1,0:T(8,128)S(1)}, u32[]{:S(2)}, u32[]{:S(2)}) collective-permute-start(f32[96,128]{1,0:T(8,128)S(1)} %get-tuple-element.69), channel_id=1, source_target_pairs={{4,8},{8,4},{12,0},{0,12},{5,9},{9,5},{13,1},{1,13},{6,10},{10,6},... | collective-permute-start | bytes 147464 | tf_op jit(solution)/shard_map/ppermute | solution.py:604
  18.8 1.2 %collective-permute-done.5.z1.az1 = f32[16,128]{1,0:T(8,128)S(1)} collective-permute-done((f32[16,128]{1,0:T(8,128)S(1)}, f32[16,128]{1,0:T(8,128)S(1)}, u32[]{:S(2)}, u32[]{:S(2)}) %collective-permute-start.5) | collective-permute-done | bytes 8224 | tf_op jit(solution)/shard_map/ppermute | solution.py:606
  20.0 1.0 %collective-permute-done.3.y1.ay1 = f32[96,128]{1,0:T(8,128)S(1)} collective-permute-done((f32[96,128]{1,0:T(8,128)S(1)}, f32[96,128]{1,0:T(8,128)S(1)}, u32[]{:S(2)}, u32[]{:S(2)}) %collective-permute-start.3) | collective-permute-done | bytes 49184 | tf_op jit(solution)/shard_map/ppermute | solution.py:604
  21.0 1.8 %collective-permute-done.4.y2.ay2 = f32[96,128]{1,0:T(8,128)S(1)} collective-permute-done((f32[96,128]{1,0:T(8,128)S(1)}, f32[96,128]{1,0:T(8,128)S(1)}, u32[]{:S(2)}, u32[]{:S(2)}) %collective-permute-start.4) | collective-permute-done | bytes 49184 | tf_op jit(solution)/shard_map/ppermute | solution.py:605
  22.8 2.6 %shard_map.99 = (f32[22,3,8,128]{3,2,1,0:T(8,128)S(1)}, f32[3,8,128]{2,1,0:T(8,128)S(1)}, f32[3,8,128]{2,1,0:T(8,128)S(1)}, f32[8,128]{1,0:T(8,128)S(1)}, f32[80,128]{1,0:T(8,128)S(1)}) custom-call(s32[8,128]{1,0:T(8,128)S(1)} %get-tuple-element.49.flags, f32[22,3,8,128]{3,2,1,0:T(8,128)S(1)} %get-tuple-element.57.force, ...), custom_call_target="tpu_custom_call" | custom-call | tf_op jit(solution)/shard_map/pallas_call | solution.py:48
  25.5 1.4 %collective-permute-start.7 = (f32[72,128]{1,0:T(8,128)S(1)}, f32[72,128]{1,0:T(8,128)S(1)}, u32[]{:S(2)}, u32[]{:S(2)}) collective-permute-start(f32[72,128]{1,0:T(8,128)S(1)} %get-tuple-element.76), channel_id=1, source_target_pairs={{4,8},{8,4},{12,0},{0,12},{5,9},{9,5},{13,1},{1,13},{6,10},{10,6},... | collective-permute-start | bytes 110600 | tf_op jit(solution)/shard_map/ppermute | solution.py:604
  27.0 1.3 %collective-permute-start.9 = (f32[8,128]{1,0:T(8,128)S(1)}, f32[8,128]{1,0:T(8,128)S(1)}, u32[]{:S(2)}, u32[]{:S(2)}) collective-permute-start(f32[8,128]{1,0:T(8,128)S(1)} %get-tuple-element.78), channel_id=1, source_target_pairs={{0,1},{1,0},{2,3},{3,2},{4,5},{5,4},{6,7},{7,6},{8,9},{9,8},{10,11... | collective-permute-start | bytes 12296 | tf_op jit(solution)/shard_map/ppermute | solution.py:606
  29.1 1.7 %collective-permute-done.7.y1 = f32[72,128]{1,0:T(8,128)S(1)} collective-permute-done((f32[72,128]{1,0:T(8,128)S(1)}, f32[72,128]{1,0:T(8,128)S(1)}, u32[]{:S(2)}, u32[]{:S(2)}) %collective-permute-start.7) | collective-permute-done | bytes 36896 | tf_op jit(solution)/shard_map/ppermute | solution.py:604
  31.0 1.4 %shard_map.103.one = f32[32,128]{1,0:T(8,128)S(1)} custom-call(bf16[512,512]{1,0:T(8,128)(2,1)S(1)} %get-tuple-element.80.after.high, s32[8,128]{1,0:T(8,128)S(1)} %get-tuple-element.49.flags, f32[22,3,8,128]{3,2,1,0:T(8,128)S(1)} %get-tuple-element.57.force, f32[22,8,128]{2,1,0:T(8,128)S(1)} %get-tuple-element.58.weight, ...), custom_call_target="tpu_custom_call" | custom-call | tf_op jit(solution)/shard_map/pallas_call | solution.py:48
  32.8 0.8 %collective-permute-done.11.two = f32[32,128]{1,0:T(8,128)S(1)} collective-permute-done((f32[32,128]{1,0:T(8,128)S(1)}, f32[32,128]{1,0:T(8,128)S(1)}, u32[]{:S(2)}, u32[]{:S(2)}) %collective-permute-start.11) | collective-permute-done | bytes 16416 | tf_op jit(solution)/shard_map/ppermute | solution.py:673
  33.7 2.2 %collective-permute-start.12 = (f32[32,128]{1,0:T(8,128)S(1)}, f32[32,128]{1,0:T(8,128)S(1)}, u32[]{:S(2)}, u32[]{:S(2)}) collective-permute-start(f32[32,128]{1,0:T(8,128)S(1)} %shard_map.104.mine), channel_id=1, source_target_pairs={{0,114},{1,113},{2,112},{3,115},{4,118},{5,117},{6,116},{7,119},{8... | collective-permute-start | bytes 49160 | tf_op jit(solution)/shard_map/ppermute | solution.py:619
  35.9 1.8 %collective-permute-start.13 = (f32[32,128]{1,0:T(8,128)S(1)}, f32[32,128]{1,0:T(8,128)S(1)}, u32[]{:S(2)}, u32[]{:S(2)}) collective-permute-start(f32[32,128]{1,0:T(8,128)S(1)} %shard_map.104.mine), channel_id=1, source_target_pairs={{0,2},{1,3},{2,0},{3,1},{4,6},{5,7},{6,4},{7,5},{8,10},{9,11},{10,... | collective-permute-start | bytes 49160 | tf_op jit(solution)/shard_map/ppermute | solution.py:675
  37.7 3.1 %collective-permute-done.12.above = f32[32,128]{1,0:T(8,128)S(1)} collective-permute-done((f32[32,128]{1,0:T(8,128)S(1)}, f32[32,128]{1,0:T(8,128)S(1)}, u32[]{:S(2)}, u32[]{:S(2)}) %collective-permute-start.12) | collective-permute-done | bytes 16416 | tf_op jit(solution)/shard_map/ppermute | solution.py:619
  41.2 1.2 %collective-permute-done.14.swapped = f32[24,128]{1,0:T(8,128)S(1)} collective-permute-done((f32[24,128]{1,0:T(8,128)S(1)}, f32[24,128]{1,0:T(8,128)S(1)}, u32[]{:S(2)}, u32[]{:S(2)}) %collective-permute-start.14) | collective-permute-done | bytes 12320 | tf_op jit(solution)/shard_map/ppermute | solution.py:679
  43.1 4.0 %collective-permute-start.15 = (f32[8,512]{1,0:T(8,128)S(1)}, f32[8,512]{1,0:T(8,128)S(1)}, u32[]{:S(2)}, u32[]{:S(2)}) collective-permute-start(f32[8,512]{1,0:T(8,128)S(1)} %shard_map.106.iterate), channel_id=1, source_target_pairs={{0,28},{1,21},{2,30},{3,23},{4,16},{5,25},{6,18},{7,27},{8,20},{9,... | collective-permute-start | bytes 49160 | tf_op jit(solution)/shard_map/ppermute | solution.py:619
  47.1 2.4 %collective-permute-start.16 = (f32[8,512]{1,0:T(8,128)S(1)}, f32[8,512]{1,0:T(8,128)S(1)}, u32[]{:S(2)}, u32[]{:S(2)}) collective-permute-start(f32[8,512]{1,0:T(8,128)S(1)} %shard_map.106.iterate), channel_id=1, source_target_pairs={{0,16},{1,5},{2,18},{3,7},{4,20},{5,9},{6,22},{7,11},{8,24},{9,13}... | collective-permute-start | bytes 49160 | tf_op jit(solution)/shard_map/ppermute | solution.py:619
  49.8 1.1 %collective-permute-done.16.b = f32[8,512]{1,0:T(8,128)S(1)} collective-permute-done((f32[8,512]{1,0:T(8,128)S(1)}, f32[8,512]{1,0:T(8,128)S(1)}, u32[]{:S(2)}, u32[]{:S(2)}) %collective-permute-start.16) | collective-permute-done | bytes 16416 | tf_op jit(solution)/shard_map/ppermute | solution.py:619
  50.9 2.3 %collective-permute-done.17.c = f32[8,512]{1,0:T(8,128)S(1)} collective-permute-done((f32[8,512]{1,0:T(8,128)S(1)}, f32[8,512]{1,0:T(8,128)S(1)}, u32[]{:S(2)}, u32[]{:S(2)}) %collective-permute-start.17) | collective-permute-done | bytes 16416 | tf_op jit(solution)/shard_map/ppermute | solution.py:619
  53.2 1.2 %collective-permute-done.18.swapped = f32[24,512]{1,0:T(8,128)S(1)} collective-permute-done((f32[24,512]{1,0:T(8,128)S(1)}, f32[24,512]{1,0:T(8,128)S(1)}, u32[]{:S(2)}, u32[]{:S(2)}) %collective-permute-start.18) | collective-permute-done | bytes 49184 | tf_op jit(solution)/shard_map/ppermute | solution.py:689
  54.5 3.1 %shard_map.108 = (f32[22,3,8,128]{3,2,1,0:T(8,128)S(1)}, f32[3,8,128]{2,1,0:T(8,128)S(1)}, f32[3,8,128]{2,1,0:T(8,128)S(1)}, f32[8,128]{1,0:T(8,128)S(1)}, f32[80,128]{1,0:T(8,128)S(1)}) custom-call(s32[8,128]{1,0:T(8,128)S(1)} %get-tuple-element.49.flags, f32[22,3,8,128]{3,2,1,0:T(8,128)S(1)} %get-tuple-element.57.force, ...), custom_call_target="tpu_custom_call" | custom-call | tf_op jit(solution)/shard_map/pallas_call | solution.py:48
  57.5 2.1 %collective-permute-start.19 = (f32[80,128]{1,0:T(8,128)S(1)}, f32[80,128]{1,0:T(8,128)S(1)}, u32[]{:S(2)}, u32[]{:S(2)}) collective-permute-start(f32[80,128]{1,0:T(8,128)S(1)} %get-tuple-element.87), channel_id=1, source_target_pairs={{1,2},{2,1},{3,0},{0,3},{5,6},{6,5},{7,4},{4,7},{9,10},{10,9},{11,... | collective-permute-start | bytes 122888 | tf_op jit(solution)/shard_map/ppermute | solution.py:603
  59.7 1.5 %collective-permute-start.20 = (f32[72,128]{1,0:T(8,128)S(1)}, f32[72,128]{1,0:T(8,128)S(1)}, u32[]{:S(2)}, u32[]{:S(2)}) collective-permute-start(f32[72,128]{1,0:T(8,128)S(1)} %get-tuple-element.88), channel_id=1, source_target_pairs={{4,8},{8,4},{12,0},{0,12},{5,9},{9,5},{13,1},{1,13},{6,10},{10,6},... | collective-permute-start | bytes 110600 | tf_op jit(solution)/shard_map/ppermute | solution.py:604
  61.3 1.1 %collective-permute-done.22.z1 = f32[8,128]{1,0:T(8,128)S(1)} collective-permute-done((f32[8,128]{1,0:T(8,128)S(1)}, f32[8,128]{1,0:T(8,128)S(1)}, u32[]{:S(2)}, u32[]{:S(2)}) %collective-permute-start.22) | collective-permute-done | bytes 4128 | tf_op jit(solution)/shard_map/ppermute | solution.py:606
  62.4 2.5 %collective-permute-done.20.y1 = f32[72,128]{1,0:T(8,128)S(1)} collective-permute-done((f32[72,128]{1,0:T(8,128)S(1)}, f32[72,128]{1,0:T(8,128)S(1)}, u32[]{:S(2)}, u32[]{:S(2)}) %collective-permute-start.20) | collective-permute-done | bytes 36896 | tf_op jit(solution)/shard_map/ppermute | solution.py:604
  65.2 2.5 %shard_map.110 = (f32[3,12,8,128]{3,2,1,0:T(8,128)S(1)}, f32[3,4,8,128]{3,2,1,0:T(8,128)S(1)}, f32[3,8,128]{2,1,0:T(8,128)S(1)}) custom-call(s32[8,128]{1,0:T(8,128)S(1)} %get-tuple-element.49.flags, f32[22,3,8,128]{3,2,1,0:T(8,128)S(1)} %get-tuple-element.57.force, f32[22,8,128]{2,1,0:T(8,128)S(1)} %get-tuple-element.58.weight, ...), custom_call_target="tpu_custom_call" | custom-call | tf_op jit(solution)/shard_map/pallas_call | solution.py:48
  68.5 5.5 %collective-permute-done.23.tail = f32[3,4,8,128]{3,2,1,0:T(8,128)S(1)} collective-permute-done((f32[3,4,8,128]{3,2,1,0:T(8,128)S(1)}, f32[3,4,8,128]{3,2,1,0:T(8,128)S(1)}, u32[]{:S(2)}, u32[]{:S(2)}) %collective-permute-start.23) | collective-permute-done | bytes 49184 | tf_op jit(solution)/shard_map/ppermute | solution.py:702
  (36 shorter events, 5.2 us)
Async XLA Ops:
  1.8 11.6 %collective-permute-start.1 = (f32[128,512]{1,0:T(8,128)S(1)}, f32[128,512]{1,0:T(8,128)S(1)}, u32[]{:S(2)}, u32[]{:S(2)}) collective-permute-start(f32[128,512]{1,0:T(8,128)S(1)} %get-tuple-element.60.one), channel_id=1, source_target_pairs={{0,2},{1,3},{2,0},{3,1},{4,6},{5,7},{6,4},{7,5},{8,10},{9,11},{10,... | collective-permute-start | bytes 786440 | tf_op jit(solution)/shard_map/ppermute | solution.py:631
  5.8 5.2 %collective-permute-start = (f32[7,5,8,128]{3,2,1,0:T(8,128)S(1)}, f32[7,5,8,128]{3,2,1,0:T(8,128)S(1)}, u32[]{:S(2)}, u32[]{:S(2)}) collective-permute-start(f32[7,5,8,128]{3,2,1,0:T(8,128)S(1)} %get-tuple-element.53), channel_id=1, source_target_pairs={{0,16},{16,32},{32,48},{48,64},{64,80},{80,96},{96,112},{112,0},{1... | collective-permute-start | bytes 430088 | tf_op jit(solution)/shard_map/ppermute | solution.py:630
  13.4 17.6 %copy-start = (f32[1,1,128]{2,1,0:T(1,128)S(1)}, f32[1,1,128]{2,1,0:T(1,128)}, u32[]{:S(2)}) copy-start(f32[1,1,128]{2,1,0:T(1,128)} %param.15) | copy-start | bytes 1540
  13.4 14.8 %collective-permute-start.10 = (f32[256,512]{1,0:T(8,128)S(1)}, f32[256,512]{1,0:T(8,128)S(1)}, u32[]{:S(2)}, u32[]{:S(2)}) collective-permute-start(f32[256,512]{1,0:T(8,128)S(1)} %shard_map.101.mine), channel_id=1, source_target_pairs={{0,1},{1,0},{2,3},{3,2},{4,5},{5,4},{6,7},{7,6},{8,9},{9,8},{10,11... | collective-permute-start | bytes 1572872 | tf_op jit(solution)/shard_map/ppermute | solution.py:662
  13.5 6.5 %collective-permute-start.2 = (f32[104,128]{1,0:T(8,128)S(1)}, f32[104,128]{1,0:T(8,128)S(1)}, u32[]{:S(2)}, u32[]{:S(2)}) collective-permute-start(f32[104,128]{1,0:T(8,128)S(1)} %get-tuple-element.67), channel_id=1, source_target_pairs={{1,2},{2,1},{3,0},{0,3},{5,6},{6,5},{7,4},{4,7},{9,10},{10,9},{11,... | collective-permute-start | bytes 159752 | tf_op jit(solution)/shard_map/ppermute | solution.py:603
  15.6 5.4 %collective-permute-start.3 = (f32[96,128]{1,0:T(8,128)S(1)}, f32[96,128]{1,0:T(8,128)S(1)}, u32[]{:S(2)}, u32[]{:S(2)}) collective-permute-start(f32[96,128]{1,0:T(8,128)S(1)} %get-tuple-element.69), channel_id=1, source_target_pairs={{4,8},{8,4},{12,0},{0,12},{5,9},{9,5},{13,1},{1,13},{6,10},{10,6},... | collective-permute-start | bytes 147464 | tf_op jit(solution)/shard_map/ppermute | solution.py:604
  18.7 4.1 %collective-permute-start.4 = (f32[96,128]{1,0:T(8,128)S(1)}, f32[96,128]{1,0:T(8,128)S(1)}, u32[]{:S(2)}, u32[]{:S(2)}) collective-permute-start(f32[96,128]{1,0:T(8,128)S(1)} %get-tuple-element.70), channel_id=1, source_target_pairs={{0,4},{4,0},{8,12},{12,8},{1,5},{5,1},{9,13},{13,9},{2,6},{6,2},{1... | collective-permute-start | bytes 147464 | tf_op jit(solution)/shard_map/ppermute | solution.py:605
  18.8 1.2 %collective-permute-start.5 = (f32[16,128]{1,0:T(8,128)S(1)}, f32[16,128]{1,0:T(8,128)S(1)}, u32[]{:S(2)}, u32[]{:S(2)}) collective-permute-start(f32[16,128]{1,0:T(8,128)S(1)} %get-tuple-element.71), channel_id=1, source_target_pairs={{0,1},{1,0},{2,3},{3,2},{4,5},{5,4},{6,7},{7,6},{8,9},{9,8},{10,11... | collective-permute-start | bytes 24584 | tf_op jit(solution)/shard_map/ppermute | solution.py:606
  25.4 5.6 %collective-permute-start.6 = (f32[80,128]{1,0:T(8,128)S(1)}, f32[80,128]{1,0:T(8,128)S(1)}, u32[]{:S(2)}, u32[]{:S(2)}) collective-permute-start(f32[80,128]{1,0:T(8,128)S(1)} %get-tuple-element.75), channel_id=1, source_target_pairs={{1,2},{2,1},{3,0},{0,3},{5,6},{6,5},{7,4},{4,7},{9,10},{10,9},{11,... | collective-permute-start | bytes 122888 | tf_op jit(solution)/shard_map/ppermute | solution.py:603
  25.5 5.2 %collective-permute-start.7 = (f32[72,128]{1,0:T(8,128)S(1)}, f32[72,128]{1,0:T(8,128)S(1)}, u32[]{:S(2)}, u32[]{:S(2)}) collective-permute-start(f32[72,128]{1,0:T(8,128)S(1)} %get-tuple-element.76), channel_id=1, source_target_pairs={{4,8},{8,4},{12,0},{0,12},{5,9},{9,5},{13,1},{1,13},{6,10},{10,6},... | collective-permute-start | bytes 110600 | tf_op jit(solution)/shard_map/ppermute | solution.py:604
  27.0 4.0 %collective-permute-start.8 = (f32[72,128]{1,0:T(8,128)S(1)}, f32[72,128]{1,0:T(8,128)S(1)}, u32[]{:S(2)}, u32[]{:S(2)}) collective-permute-start(f32[72,128]{1,0:T(8,128)S(1)} %get-tuple-element.77), channel_id=1, source_target_pairs={{0,4},{4,0},{8,12},{12,8},{1,5},{5,1},{9,13},{13,9},{2,6},{6,2},{1... | collective-permute-start | bytes 110600 | tf_op jit(solution)/shard_map/ppermute | solution.py:605
  27.0 2.1 %collective-permute-start.9 = (f32[8,128]{1,0:T(8,128)S(1)}, f32[8,128]{1,0:T(8,128)S(1)}, u32[]{:S(2)}, u32[]{:S(2)}) collective-permute-start(f32[8,128]{1,0:T(8,128)S(1)} %get-tuple-element.78), channel_id=1, source_target_pairs={{0,1},{1,0},{2,3},{3,2},{4,5},{5,4},{6,7},{7,6},{8,9},{9,8},{10,11... | collective-permute-start | bytes 12296 | tf_op jit(solution)/shard_map/ppermute | solution.py:606
  32.4 1.3 %collective-permute-start.11 = (f32[32,128]{1,0:T(8,128)S(1)}, f32[32,128]{1,0:T(8,128)S(1)}, u32[]{:S(2)}, u32[]{:S(2)}) collective-permute-start(f32[32,128]{1,0:T(8,128)S(1)} %shard_map.103.one), channel_id=1, source_target_pairs={{0,1},{1,0},{2,3},{3,2},{4,5},{5,4},{6,7},{7,6},{8,9},{9,8},{10,11... | collective-permute-start | bytes 49160 | tf_op jit(solution)/shard_map/ppermute | solution.py:673
  33.7 7.1 %collective-permute-start.12 = (f32[32,128]{1,0:T(8,128)S(1)}, f32[32,128]{1,0:T(8,128)S(1)}, u32[]{:S(2)}, u32[]{:S(2)}) collective-permute-start(f32[32,128]{1,0:T(8,128)S(1)} %shard_map.104.mine), channel_id=1, source_target_pairs={{0,114},{1,113},{2,112},{3,115},{4,118},{5,117},{6,116},{7,119},{8... | collective-permute-start | bytes 49160 | tf_op jit(solution)/shard_map/ppermute | solution.py:619
  35.9 5.2 %collective-permute-start.13 = (f32[32,128]{1,0:T(8,128)S(1)}, f32[32,128]{1,0:T(8,128)S(1)}, u32[]{:S(2)}, u32[]{:S(2)}) collective-permute-start(f32[32,128]{1,0:T(8,128)S(1)} %shard_map.104.mine), channel_id=1, source_target_pairs={{0,2},{1,3},{2,0},{3,1},{4,6},{5,7},{6,4},{7,5},{8,10},{9,11},{10,... | collective-permute-start | bytes 49160 | tf_op jit(solution)/shard_map/ppermute | solution.py:675
  41.2 1.2 %collective-permute-start.14 = (f32[24,128]{1,0:T(8,128)S(1)}, f32[24,128]{1,0:T(8,128)S(1)}, u32[]{:S(2)}, u32[]{:S(2)}) collective-permute-start(f32[24,128]{1,0:T(8,128)S(1)} %get-tuple-element.82.passed), channel_id=1, source_target_pairs={{0,1},{1,0},{2,3},{3,2},{4,5},{5,4},{6,7},{7,6},{8,9},{9,8},{10,11... | collective-permute-start | bytes 36872 | tf_op jit(solution)/shard_map/ppermute | solution.py:679
  43.1 6.7 %collective-permute-start.15 = (f32[8,512]{1,0:T(8,128)S(1)}, f32[8,512]{1,0:T(8,128)S(1)}, u32[]{:S(2)}, u32[]{:S(2)}) collective-permute-start(f32[8,512]{1,0:T(8,128)S(1)} %shard_map.106.iterate), channel_id=1, source_target_pairs={{0,28},{1,21},{2,30},{3,23},{4,16},{5,25},{6,18},{7,27},{8,20},{9,... | collective-permute-start | bytes 49160 | tf_op jit(solution)/shard_map/ppermute | solution.py:619
  47.1 3.8 %collective-permute-start.16 = (f32[8,512]{1,0:T(8,128)S(1)}, f32[8,512]{1,0:T(8,128)S(1)}, u32[]{:S(2)}, u32[]{:S(2)}) collective-permute-start(f32[8,512]{1,0:T(8,128)S(1)} %shard_map.106.iterate), channel_id=1, source_target_pairs={{0,16},{1,5},{2,18},{3,7},{4,20},{5,9},{6,22},{7,11},{8,24},{9,13}... | collective-permute-start | bytes 49160 | tf_op jit(solution)/shard_map/ppermute | solution.py:619
  49.5 3.7 %collective-permute-start.17 = (f32[8,512]{1,0:T(8,128)S(1)}, f32[8,512]{1,0:T(8,128)S(1)}, u32[]{:S(2)}, u32[]{:S(2)}) collective-permute-start(f32[8,512]{1,0:T(8,128)S(1)} %shard_map.106.iterate), channel_id=1, source_target_pairs={{0,12},{1,5},{2,14},{3,7},{4,0},{5,9},{6,2},{7,11},{8,4},{9,13},{1... | collective-permute-start | bytes 49160 | tf_op jit(solution)/shard_map/ppermute | solution.py:619
  53.2 1.2 %collective-permute-start.18 = (f32[24,512]{1,0:T(8,128)S(1)}, f32[24,512]{1,0:T(8,128)S(1)}, u32[]{:S(2)}, u32[]{:S(2)}) collective-permute-start(f32[24,512]{1,0:T(8,128)S(1)} %shard_map.107.got), channel_id=1, source_target_pairs={{0,1},{1,0},{2,3},{3,2},{4,5},{5,4},{6,7},{7,6},{8,9},{9,8},{10,11... | collective-permute-start | bytes 147464 | tf_op jit(solution)/shard_map/ppermute | solution.py:689
  57.5 7.7 %collective-permute-start.19 = (f32[80,128]{1,0:T(8,128)S(1)}, f32[80,128]{1,0:T(8,128)S(1)}, u32[]{:S(2)}, u32[]{:S(2)}) collective-permute-start(f32[80,128]{1,0:T(8,128)S(1)} %get-tuple-element.87), channel_id=1, source_target_pairs={{1,2},{2,1},{3,0},{0,3},{5,6},{6,5},{7,4},{4,7},{9,10},{10,9},{11,... | collective-permute-start | bytes 122888 | tf_op jit(solution)/shard_map/ppermute | solution.py:603
  59.7 5.2 %collective-permute-start.20 = (f32[72,128]{1,0:T(8,128)S(1)}, f32[72,128]{1,0:T(8,128)S(1)}, u32[]{:S(2)}, u32[]{:S(2)}) collective-permute-start(f32[72,128]{1,0:T(8,128)S(1)} %get-tuple-element.88), channel_id=1, source_target_pairs={{4,8},{8,4},{12,0},{0,12},{5,9},{9,5},{13,1},{1,13},{6,10},{10,6},... | collective-permute-start | bytes 110600 | tf_op jit(solution)/shard_map/ppermute | solution.py:604
  61.3 4.0 %collective-permute-start.21 = (f32[72,128]{1,0:T(8,128)S(1)}, f32[72,128]{1,0:T(8,128)S(1)}, u32[]{:S(2)}, u32[]{:S(2)}) collective-permute-start(f32[72,128]{1,0:T(8,128)S(1)} %get-tuple-element.89), channel_id=1, source_target_pairs={{0,4},{4,0},{8,12},{12,8},{1,5},{5,1},{9,13},{13,9},{2,6},{6,2},{1... | collective-permute-start | bytes 110600 | tf_op jit(solution)/shard_map/ppermute | solution.py:605
  61.3 1.2 %collective-permute-start.22 = (f32[8,128]{1,0:T(8,128)S(1)}, f32[8,128]{1,0:T(8,128)S(1)}, u32[]{:S(2)}, u32[]{:S(2)}) collective-permute-start(f32[8,128]{1,0:T(8,128)S(1)} %get-tuple-element.90), channel_id=1, source_target_pairs={{0,1},{1,0},{2,3},{3,2},{4,5},{5,4},{6,7},{7,6},{8,9},{9,8},{10,11... | collective-permute-start | bytes 12296 | tf_op jit(solution)/shard_map/ppermute | solution.py:606
  67.7 6.3 %collective-permute-start.23 = (f32[3,4,8,128]{3,2,1,0:T(8,128)S(1)}, f32[3,4,8,128]{3,2,1,0:T(8,128)S(1)}, u32[]{:S(2)}, u32[]{:S(2)}) collective-permute-start(f32[3,4,8,128]{3,2,1,0:T(8,128)S(1)} %get-tuple-element.91), channel_id=1, source_target_pairs={{0,112},{16,0},{32,16},{48,32},{64,48},{80,64},{96,80},{112,96},{1... | collective-permute-start | bytes 147464 | tf_op jit(solution)/shard_map/ppermute | solution.py:702

commit v4 on v3

--- a/solution.py
+++ b/solution.py
@@ -207,7 +207,7 @@
 def sides(flags, y_first, y_second, z_first, z_second):
     tall_shape, zero = (LINES, 128), jnp.zeros((LINES, 128), F32)
     y_even, z_even = yes(flags, 0, tall_shape), yes(flags, 1, (8, 128))
-    a, b, c, d = y_first[0:LINES], y_second[0:LINES], z_first[0:8], z_second[0:8]
+    a, b, c, d = y_first[0:LINES], y_second[0:LINES], z_first[0:8, 0:128], z_second[0:8]
     return (
         jnp.where(yes(flags, 2, tall_shape), jnp.where(y_even, b, a), zero),
         jnp.where(yes(flags, 3, tall_shape), jnp.where(y_even, a, b), zero),
@@ -361,7 +361,7 @@
 
     y_low, y_high, z_low, z_high = sides(flags, y1, y2, z1, z2)
     y_even, z_even = yes(flags, 0, (ROWS, 128)), yes(flags, 1, (8, 128))
-    ay1, ay2, az1, az2 = ay1[LINES : LINES + ROWS], ay2[LINES : LINES + ROWS], az1[8:16], az2[8:16]
+    ay1, ay2, az1, az2 = ay1[LINES : LINES + ROWS], ay2[LINES : LINES + ROWS], az1[0:8, 128:256], az2[8:16]
     sub = lax.broadcasted_iota(jnp.int32, (8, 128), 0)
     lane = lax.broadcasted_iota(jnp.int32, (8, 128), 1)
 
@@ -486,11 +486,14 @@
     return call(add_kernel, [(one.shape, F32)], n_in=2)(one, two)[0]
 
 
-def pack_kernel(force, kappa, agg, matrix, out, force_near, kappa_near, agg_near, rows, flags, sems):
+def pack_kernel(force, kappa, agg, matrix, out, force_near, kappa_near, agg_near, rows, more_rows, flags, sems):
     copies = [
         pltpu.make_async_copy(far, near, sems.at[i])
         for i, (far, near) in enumerate(
-            ((force, force_near), (kappa, kappa_near), (agg, agg_near), (matrix, rows))
+            (
+                (force, force_near), (kappa, kappa_near), (agg, agg_near),
+                (matrix.at[pl.ds(0, 64)], rows), (matrix.at[pl.ds(64, 64)], more_rows),
+            )
         )
     ]
     for copy in copies:
@@ -510,13 +513,17 @@
         out[p, 4] = agg_near[start + p].astype(F32)
 
 
-def stack_kernel(one, two, out):
-    out[0:128], out[128:256] = one[...], two[...]
+def stack_kernel(columns, one, two, three, four, out):
+    out[0:8, 0:128], out[0:8, 128:256] = columns[0:8], columns[8:16]
+    out[0:8, 256:NAGG] = jnp.zeros((8, NAGG - 256), F32)
+    for i, part in enumerate((one, two, three, four)):
+        out[8 + 64 * i : 72 + 64 * i] = part[...]
 
 
 def split_matrix_kernel(flags, mine, other, high, low):
     core_zero, first_half = yes(flags, 1, (256, NAGG)), yes(flags, 7, (128, NAGG))
-    sets = jnp.where(core_zero, mine[...], other[...]), jnp.where(core_zero, other[...], mine[...])
+    one, two = mine[8:264], other[8:264]
+    sets = jnp.where(core_zero, one, two), jnp.where(core_zero, two, one)
     for b in range(4):
         rows = sets[b % 2]
         near, far = (rows[0:128], rows[128:256]) if b < 2 else (rows[128:256], rows[0:128])
@@ -620,15 +627,15 @@
 
 
 def shards(force, kappa, mortar_blocks, mortar_index, mortar_count, agg_map, coarse_matrix, coarse_diag):
-    tail_in, force, kappa, agg_map, rows, flags = call(
+    tail_in, force, kappa, agg_map, rows, more_rows, flags = call(
         pack_kernel,
         [((TAIL, 5, 8, 128), F32), (force.shape, F32), (kappa.shape, F32), (agg_map.shape, jnp.int32),
-         ((128, NAGG), F32), ((8, 128), jnp.int32)],
-        [pltpu.SemaphoreType.DMA((4,))],
+         ((64, NAGG), F32), ((64, NAGG), F32), ((8, 128), jnp.int32)],
+        [pltpu.SemaphoreType.DMA((5,))],
         n_far=4,
     )(force, kappa, agg_map, coarse_matrix.reshape(128, NAGG))
     tail_in = lax.ppermute(tail_in, "gx", ring("gx", 1))
-    half = lax.ppermute(rows, "gz", ring("gz", 2))
+    half, more_half = [lax.ppermute(x, "gz", ring("gz", 2)) for x in (rows, more_rows)]
 
     by_row, spots, place = call(
         prepare_kernel,
@@ -656,13 +663,10 @@
         n_in=8,
     )(flags, force, kappa, agg_map, tail_in, by_row, spots, place)
     force_e, weight, inverse, agg, velocity, mult, mult_up, face, inverse_t = out[:9]
-    half, velocity = lax.optimization_barrier((half, velocity))
-    rows = call(stack_kernel, [((256, NAGG), F32)], n_in=2)(rows, half)[0]
-    k_high, k_low = call(split_matrix_kernel, [((NAGG, NAGG), BF16)] * 2, n_in=3)(
-        flags, rows, lax.ppermute(rows, "gz", swaps("gz", 0))
-    )
     lines = call(lines_and_labels_kernel, [y_more, y_more], n_in=3)(flags, velocity, agg)
-    labels = trade(*lines, *out[9:])
+    stacked = call(stack_kernel, [((264, NAGG), F32)], n_in=5)(out[9], rows, more_rows, half, more_half)[0]
+    labels = trade(*lines, stacked, out[10])
+    k_high, k_low = call(split_matrix_kernel, [((NAGG, NAGG), BF16)] * 2, n_in=3)(flags, stacked, labels[3])
     velocity, mult, mult_up, *msgs = call(
         second_sweep_kernel, [field, plane, plane, z_msg, ((LINES + 8, 128), F32)], n_in=16
     )(flags, force_e, weight, inverse, velocity, mult, mult_up, face, inverse_t, by_row, spots, place, *labels)

time: 74.9 us -> 74.4 us (level)
  waiting for transfers between devices: 25.9 us -> 27.2 us
  starting transfers between devices: 28.1 us -> 26.9 us
    ppermute x3, waiting for transfers between devices: 5.2 us -> 7.43 us  [trade(): lax.ppermute(y1, 'gy', swaps('gy', 1))]
    ppermute x4, starting transfers between devices: 8.9 us -> 6.94 us  [by_core(): return lax.ppermute(x, ('gx', 'gy', 'gz'), pairs)]
    ppermute x3, starting transfers between devices: 4.26 us -> 5.73 us  [trade(): lax.ppermute(z2, 'gz', swaps('gz', 1))]
    ppermute x3, starting transfers between devices: 1.37 us -> 0.16 us  [trade(): lax.ppermute(z1, 'gz', swaps('gz', 0))]
    ppermute x1, starting transfers between devices: 0.93 us -> 1.9 us  [shards(): tail_in = lax.ppermute(tail_in, 'gx', ring('gx', 1))]
    ppermute x1, starting transfers between devices: 0.07 us -> 1 us  [shards(): tail = lax.ppermute(tail, 'gx', ring('gx', -1))]
    ppermute x1, waiting for transfers between devices: 5.5 us -> 4.58 us  [shards(): tail = lax.ppermute(tail, 'gx', ring('gx', -1))]
    ppermute x4, waiting for transfers between devices: 6.51 us -> 7.34 us  [by_core(): return lax.ppermute(x, ('gx', 'gy', 'gz'), pairs)]
  transfers between devices with their start and end apart: 24 -> 24, of which waited for: 18 -> 15; matrix products, arithmetic and copies ran while one was open for 0% -> 0% of each run, Pallas kernels for 14% -> 10%
where the time goes in v4:
time: 74.4 us; the launch traced here: 74.3 us
  waiting for transfers between devices  27.2 us (37%)
  starting transfers between devices  26.9 us (36%)
  Pallas kernels  19.2 us (26%)
  between operations  0.97 us (1%)
    pallas_call x16, Pallas kernels, run(): return kernel(*args[:n_smem], *held, *far)  17.9 us
    ppermute x3, waiting for transfers between devices, trade(): lax.ppermute(y1, 'gy', swaps('gy', 1))  7.43 us
    ppermute x4, waiting for transfers between devices, by_core(): return lax.ppermute(x, ('gx', 'gy', 'gz'), pairs)  7.34 us
    ppermute x4, starting transfers between devices, by_core(): return lax.ppermute(x, ('gx', 'gy', 'gz'), pairs)  6.94 us
    ppermute x3, starting transfers between devices, trade(): lax.ppermute(y1, 'gy', swaps('gy', 1))  5.96 us
    ppermute x3, starting transfers between devices, trade(): lax.ppermute(z2, 'gz', swaps('gz', 1))  5.73 us
    ppermute x1, waiting for transfers between devices, shards(): tail = lax.ppermute(tail, 'gx', ring('gx', -1))  4.58 us
    ppermute x2, starting transfers between devices, shards(): lax.ppermute(x, 'gz', ring('gz', 2))  3.62 us
  transfers between devices with their start and end apart: 24, of which 15 were waited for; matrix products, arithmetic and copies ran while one was open for 0% of the time, Pallas kernels for 10%

profile of v4, /device:TPU:6, one launch (start us, length us, event | category | flops | bytes accessed | tf_op | source)
XLA Modules:
  0.0 74.3 jit_solution(74362432324864182)
XLA Ops:
  0.6 1.2 %shard_map.95 = (f32[7,5,8,128]{3,2,1,0:T(8,128)S(1)}, f32[3,16,8,128]{3,2,1,0:T(8,128)S(1)}, f32[16,8,128]{2,1,0:T(8,128)S(1)}, s32[16,8,128]{2,1,0:T(8,128)S(1...) custom-call(f32[3,16,8,128]{3,2,1,0:T(8,128)} %force.1, f32[16,8,128]{2,1,0:T(8,128)} %kappa.1, ...), custom_call_target="tpu_custom_call" | custom-call | tf_op jit(solution)/shard_map/pallas_call | solution.py:48
  1.8 1.9 %collective-permute-start = (f32[7,5,8,128]{3,2,1,0:T(8,128)S(1)}, f32[7,5,8,128]{3,2,1,0:T(8,128)S(1)}, u32[]{:S(2)}, u32[]{:S(2)}) collective-permute-start(f32[7,5,8,128]{3,2,1,0:T(8,128)S(1)} %get-tuple-element.52), channel_id=1, source_target_pairs={{0,16},{16,32},{32,48},{48,64},{64,80},{80,96},{96,112},{112,0},{1... | collective-permute-start | bytes 430088 | tf_op jit(solution)/shard_map/ppermute | solution.py:637
  3.7 3.6 %collective-permute-start.4 = (f32[64,512]{1,0:T(8,128)S(1)}, f32[64,512]{1,0:T(8,128)S(1)}, u32[]{:S(2)}, u32[]{:S(2)}) collective-permute-start(f32[64,512]{1,0:T(8,128)S(1)} %get-tuple-element.69.one), channel_id=1, source_target_pairs={{0,2},{1,3},{2,0},{3,1},{4,6},{5,7},{6,4},{7,5},{8,10},{9,11},{10,... | collective-permute-start | bytes 393224 | tf_op jit(solution)/shard_map/ppermute | solution.py:638
  7.3 4.2 %shard_map.96 = (f32[2,4096,128]{2,1,0:T(8,128)S(1)}, s32[8,256]{1,0:T(8,128)S(1)}, bf16[128,256]{1,0:T(8,128)(2,1)S(1)}) custom-call(s32[8,128]{1,0:T(8,128)S(1)} %get-tuple-element.48.flags, f32[192,4096]{1,0:T(8,128)} %bitcast.9, s32[4,48]{1,0:T(4,128)} %bitcast.11, s32[1,48]{1,0:T(1,128)} %bitcast.12), custom_call_target="tpu_custom_call" | custom-call | tf_op jit(solution)/shard_map/pallas_call | solution.py:48
  11.6 2.3 %shard_map.97 = (f32[22,3,8,128]{3,2,1,0:T(8,128)S(1)}, f32[22,8,128]{2,1,0:T(8,128)S(1)}, f32[22,8,128]{2,1,0:T(8,128)S(1)}, s32[22,8,128]{2,1,0:T(8,128)S(1)},...) custom-call(s32[8,128]{1,0:T(8,128)S(1)} %get-tuple-element.48.flags, ...), custom_call_target="tpu_custom_call" | custom-call | tf_op jit(solution)/shard_map/pallas_call | solution.py:48
  14.0 3.6 %collective-permute-start.1 = (f32[104,128]{1,0:T(8,128)S(1)}, f32[104,128]{1,0:T(8,128)S(1)}, u32[]{:S(2)}, u32[]{:S(2)}) collective-permute-start(f32[104,128]{1,0:T(8,128)S(1)} %get-tuple-element.64), channel_id=1, source_target_pairs={{1,2},{2,1},{3,0},{0,3},{5,6},{6,5},{7,4},{4,7},{9,10},{10,9},{11,... | collective-permute-start | bytes 159752 | tf_op jit(solution)/shard_map/ppermute | solution.py:610
  17.7 3.1 %collective-permute-start.2 = (f32[96,128]{1,0:T(8,128)S(1)}, f32[96,128]{1,0:T(8,128)S(1)}, u32[]{:S(2)}, u32[]{:S(2)}) collective-permute-start(f32[96,128]{1,0:T(8,128)S(1)} %get-tuple-element.66), channel_id=1, source_target_pairs={{4,8},{8,4},{12,0},{0,12},{5,9},{9,5},{13,1},{1,13},{6,10},{10,6},... | collective-permute-start | bytes 147464 | tf_op jit(solution)/shard_map/ppermute | solution.py:611
  20.9 2.1 %collective-permute-done.2.y1.ay1 = f32[96,128]{1,0:T(8,128)S(1)} collective-permute-done((f32[96,128]{1,0:T(8,128)S(1)}, f32[96,128]{1,0:T(8,128)S(1)}, u32[]{:S(2)}, u32[]{:S(2)}) %collective-permute-start.2) | collective-permute-done | bytes 49184 | tf_op jit(solution)/shard_map/ppermute | solution.py:611
  23.1 1.8 %collective-permute-done.3.y2.ay2 = f32[96,128]{1,0:T(8,128)S(1)} collective-permute-done((f32[96,128]{1,0:T(8,128)S(1)}, f32[96,128]{1,0:T(8,128)S(1)}, u32[]{:S(2)}, u32[]{:S(2)}) %collective-permute-start.3) | collective-permute-done | bytes 49184 | tf_op jit(solution)/shard_map/ppermute | solution.py:612
  24.9 2.4 %shard_map.100 = (f32[22,3,8,128]{3,2,1,0:T(8,128)S(1)}, f32[3,8,128]{2,1,0:T(8,128)S(1)}, f32[3,8,128]{2,1,0:T(8,128)S(1)}, f32[8,128]{1,0:T(8,128)S(1)}, f32[80,128]{1,0:T(8,128)S(1)}) custom-call(s32[8,128]{1,0:T(8,128)S(1)} %get-tuple-element.48.flags, f32[22,3,8,128]{3,2,1,0:T(8,128)S(1)} %get-tuple-element.56.force, ...), custom_call_target="tpu_custom_call" | custom-call | tf_op jit(solution)/shard_map/pallas_call | solution.py:48
  27.5 1.3 %collective-permute-start.8 = (f32[72,128]{1,0:T(8,128)S(1)}, f32[72,128]{1,0:T(8,128)S(1)}, u32[]{:S(2)}, u32[]{:S(2)}) collective-permute-start(f32[72,128]{1,0:T(8,128)S(1)} %get-tuple-element.75), channel_id=1, source_target_pairs={{4,8},{8,4},{12,0},{0,12},{5,9},{9,5},{13,1},{1,13},{6,10},{10,6},... | collective-permute-start | bytes 110600 | tf_op jit(solution)/shard_map/ppermute | solution.py:611
  29.1 0.8 %collective-permute-done.10.z1 = f32[8,128]{1,0:T(8,128)S(1)} collective-permute-done((f32[8,128]{1,0:T(8,128)S(1)}, f32[8,128]{1,0:T(8,128)S(1)}, u32[]{:S(2)}, u32[]{:S(2)}) %collective-permute-start.10) | collective-permute-done | bytes 4128 | tf_op jit(solution)/shard_map/ppermute | solution.py:613
  29.9 2.8 %collective-permute-done.8.y1 = f32[72,128]{1,0:T(8,128)S(1)} collective-permute-done((f32[72,128]{1,0:T(8,128)S(1)}, f32[72,128]{1,0:T(8,128)S(1)}, u32[]{:S(2)}, u32[]{:S(2)}) %collective-permute-start.8) | collective-permute-done | bytes 36896 | tf_op jit(solution)/shard_map/ppermute | solution.py:611
  32.7 1.4 %shard_map.103.one = f32[32,128]{1,0:T(8,128)S(1)} custom-call(bf16[512,512]{1,0:T(8,128)(2,1)S(1)} %get-tuple-element.78.after.high, s32[8,128]{1,0:T(8,128)S(1)} %get-tuple-element.48.flags, f32[22,3,8,128]{3,2,1,0:T(8,128)S(1)} %get-tuple-element.56.force, f32[22,8,128]{2,1,0:T(8,128)S(1)} %get-tuple-element.57.weight, ...), custom_call_target="tpu_custom_call" | custom-call | tf_op jit(solution)/shard_map/pallas_call | solution.py:48
  34.2 1.2 %collective-permute-done.11.two = f32[32,128]{1,0:T(8,128)S(1)} collective-permute-done((f32[32,128]{1,0:T(8,128)S(1)}, f32[32,128]{1,0:T(8,128)S(1)}, u32[]{:S(2)}, u32[]{:S(2)}) %collective-permute-start.11) | collective-permute-done | bytes 16416 | tf_op jit(solution)/shard_map/ppermute | solution.py:677
  35.4 2.1 %collective-permute-start.12 = (f32[32,128]{1,0:T(8,128)S(1)}, f32[32,128]{1,0:T(8,128)S(1)}, u32[]{:S(2)}, u32[]{:S(2)}) collective-permute-start(f32[32,128]{1,0:T(8,128)S(1)} %shard_map.104.mine), channel_id=1, source_target_pairs={{0,114},{1,113},{2,112},{3,115},{4,118},{5,117},{6,116},{7,119},{8... | collective-permute-start | bytes 49160 | tf_op jit(solution)/shard_map/ppermute | solution.py:626
  37.4 1.4 %collective-permute-start.13 = (f32[32,128]{1,0:T(8,128)S(1)}, f32[32,128]{1,0:T(8,128)S(1)}, u32[]{:S(2)}, u32[]{:S(2)}) collective-permute-start(f32[32,128]{1,0:T(8,128)S(1)} %shard_map.104.mine), channel_id=1, source_target_pairs={{0,2},{1,3},{2,0},{3,1},{4,6},{5,7},{6,4},{7,5},{8,10},{9,11},{10,... | collective-permute-start | bytes 49160 | tf_op jit(solution)/shard_map/ppermute | solution.py:679
  38.8 3.6 %collective-permute-done.12.above = f32[32,128]{1,0:T(8,128)S(1)} collective-permute-done((f32[32,128]{1,0:T(8,128)S(1)}, f32[32,128]{1,0:T(8,128)S(1)}, u32[]{:S(2)}, u32[]{:S(2)}) %collective-permute-start.12) | collective-permute-done | bytes 16416 | tf_op jit(solution)/shard_map/ppermute | solution.py:626
  42.8 1.2 %collective-permute-done.14.swapped = f32[24,128]{1,0:T(8,128)S(1)} collective-permute-done((f32[24,128]{1,0:T(8,128)S(1)}, f32[24,128]{1,0:T(8,128)S(1)}, u32[]{:S(2)}, u32[]{:S(2)}) %collective-permute-start.14) | collective-permute-done | bytes 12320 | tf_op jit(solution)/shard_map/ppermute | solution.py:683
  44.6 3.4 %collective-permute-start.15 = (f32[8,512]{1,0:T(8,128)S(1)}, f32[8,512]{1,0:T(8,128)S(1)}, u32[]{:S(2)}, u32[]{:S(2)}) collective-permute-start(f32[8,512]{1,0:T(8,128)S(1)} %shard_map.106.iterate), channel_id=1, source_target_pairs={{0,28},{1,21},{2,30},{3,23},{4,16},{5,25},{6,18},{7,27},{8,20},{9,... | collective-permute-start | bytes 49160 | tf_op jit(solution)/shard_map/ppermute | solution.py:626
  48.0 1.5 %collective-permute-start.16 = (f32[8,512]{1,0:T(8,128)S(1)}, f32[8,512]{1,0:T(8,128)S(1)}, u32[]{:S(2)}, u32[]{:S(2)}) collective-permute-start(f32[8,512]{1,0:T(8,128)S(1)} %shard_map.106.iterate), channel_id=1, source_target_pairs={{0,16},{1,5},{2,18},{3,7},{4,20},{5,9},{6,22},{7,11},{8,24},{9,13}... | collective-permute-start | bytes 49160 | tf_op jit(solution)/shard_map/ppermute | solution.py:626
  49.5 2.2 %collective-permute-done.16.b = f32[8,512]{1,0:T(8,128)S(1)} collective-permute-done((f32[8,512]{1,0:T(8,128)S(1)}, f32[8,512]{1,0:T(8,128)S(1)}, u32[]{:S(2)}, u32[]{:S(2)}) %collective-permute-start.16) | collective-permute-done | bytes 16416 | tf_op jit(solution)/shard_map/ppermute | solution.py:626
  51.7 1.5 %collective-permute-done.17.c = f32[8,512]{1,0:T(8,128)S(1)} collective-permute-done((f32[8,512]{1,0:T(8,128)S(1)}, f32[8,512]{1,0:T(8,128)S(1)}, u32[]{:S(2)}, u32[]{:S(2)}) %collective-permute-start.17) | collective-permute-done | bytes 16416 | tf_op jit(solution)/shard_map/ppermute | solution.py:626
  53.3 1.2 %collective-permute-done.18.swapped = f32[24,512]{1,0:T(8,128)S(1)} collective-permute-done((f32[24,512]{1,0:T(8,128)S(1)}, f32[24,512]{1,0:T(8,128)S(1)}, u32[]{:S(2)}, u32[]{:S(2)}) %collective-permute-start.18) | collective-permute-done | bytes 49184 | tf_op jit(solution)/shard_map/ppermute | solution.py:693
  54.5 2.9 %shard_map.108 = (f32[22,3,8,128]{3,2,1,0:T(8,128)S(1)}, f32[3,8,128]{2,1,0:T(8,128)S(1)}, f32[3,8,128]{2,1,0:T(8,128)S(1)}, f32[8,128]{1,0:T(8,128)S(1)}, f32[80,128]{1,0:T(8,128)S(1)}) custom-call(s32[8,128]{1,0:T(8,128)S(1)} %get-tuple-element.48.flags, f32[22,3,8,128]{3,2,1,0:T(8,128)S(1)} %get-tuple-element.56.force, ...), custom_call_target="tpu_custom_call" | custom-call | tf_op jit(solution)/shard_map/pallas_call | solution.py:48
  57.3 2.0 %collective-permute-start.19 = (f32[80,128]{1,0:T(8,128)S(1)}, f32[80,128]{1,0:T(8,128)S(1)}, u32[]{:S(2)}, u32[]{:S(2)}) collective-permute-start(f32[80,128]{1,0:T(8,128)S(1)} %get-tuple-element.85), channel_id=1, source_target_pairs={{1,2},{2,1},{3,0},{0,3},{5,6},{6,5},{7,4},{4,7},{9,10},{10,9},{11,... | collective-permute-start | bytes 122888 | tf_op jit(solution)/shard_map/ppermute | solution.py:610
  59.4 1.6 %collective-permute-start.20 = (f32[72,128]{1,0:T(8,128)S(1)}, f32[72,128]{1,0:T(8,128)S(1)}, u32[]{:S(2)}, u32[]{:S(2)}) collective-permute-start(f32[72,128]{1,0:T(8,128)S(1)} %get-tuple-element.86), channel_id=1, source_target_pairs={{4,8},{8,4},{12,0},{0,12},{5,9},{9,5},{13,1},{1,13},{6,10},{10,6},... | collective-permute-start | bytes 110600 | tf_op jit(solution)/shard_map/ppermute | solution.py:611
  61.1 1.1 %collective-permute-done.22.z1 = f32[8,128]{1,0:T(8,128)S(1)} collective-permute-done((f32[8,128]{1,0:T(8,128)S(1)}, f32[8,128]{1,0:T(8,128)S(1)}, u32[]{:S(2)}, u32[]{:S(2)}) %collective-permute-start.22) | collective-permute-done | bytes 4128 | tf_op jit(solution)/shard_map/ppermute | solution.py:613
  62.2 2.5 %collective-permute-done.20.y1 = f32[72,128]{1,0:T(8,128)S(1)} collective-permute-done((f32[72,128]{1,0:T(8,128)S(1)}, f32[72,128]{1,0:T(8,128)S(1)}, u32[]{:S(2)}, u32[]{:S(2)}) %collective-permute-start.20) | collective-permute-done | bytes 36896 | tf_op jit(solution)/shard_map/ppermute | solution.py:611
  65.0 2.3 %shard_map.110 = (f32[3,12,8,128]{3,2,1,0:T(8,128)S(1)}, f32[3,4,8,128]{3,2,1,0:T(8,128)S(1)}, f32[3,8,128]{2,1,0:T(8,128)S(1)}) custom-call(s32[8,128]{1,0:T(8,128)S(1)} %get-tuple-element.48.flags, f32[22,3,8,128]{3,2,1,0:T(8,128)S(1)} %get-tuple-element.56.force, f32[22,8,128]{2,1,0:T(8,128)S(1)} %get-tuple-element.57.weight, ...), custom_call_target="tpu_custom_call" | custom-call | tf_op jit(solution)/shard_map/pallas_call | solution.py:48
  67.2 1.0 %collective-permute-start.23 = (f32[3,4,8,128]{3,2,1,0:T(8,128)S(1)}, f32[3,4,8,128]{3,2,1,0:T(8,128)S(1)}, u32[]{:S(2)}, u32[]{:S(2)}) collective-permute-start(f32[3,4,8,128]{3,2,1,0:T(8,128)S(1)} %get-tuple-element.89), channel_id=1, source_target_pairs={{0,112},{16,0},{32,16},{48,32},{64,48},{80,64},{96,80},{112,96},{1... | collective-permute-start | bytes 147464 | tf_op jit(solution)/shard_map/ppermute | solution.py:706
  68.9 4.6 %collective-permute-done.23.tail = f32[3,4,8,128]{3,2,1,0:T(8,128)S(1)} collective-permute-done((f32[3,4,8,128]{3,2,1,0:T(8,128)S(1)}, f32[3,4,8,128]{3,2,1,0:T(8,128)S(1)}, u32[]{:S(2)}, u32[]{:S(2)}) %collective-permute-start.23) | collective-permute-done | bytes 49184 | tf_op jit(solution)/shard_map/ppermute | solution.py:706
  (36 shorter events, 3.7 us)
Async XLA Ops:
  1.8 9.7 %collective-permute-start = (f32[7,5,8,128]{3,2,1,0:T(8,128)S(1)}, f32[7,5,8,128]{3,2,1,0:T(8,128)S(1)}, u32[]{:S(2)}, u32[]{:S(2)}) collective-permute-start(f32[7,5,8,128]{3,2,1,0:T(8,128)S(1)} %get-tuple-element.52), channel_id=1, source_target_pairs={{0,16},{16,32},{32,48},{48,64},{64,80},{80,96},{96,112},{112,0},{1... | collective-permute-start | bytes 430088 | tf_op jit(solution)/shard_map/ppermute | solution.py:637
  3.7 10.1 %collective-permute-start.4 = (f32[64,512]{1,0:T(8,128)S(1)}, f32[64,512]{1,0:T(8,128)S(1)}, u32[]{:S(2)}, u32[]{:S(2)}) collective-permute-start(f32[64,512]{1,0:T(8,128)S(1)} %get-tuple-element.69.one), channel_id=1, source_target_pairs={{0,2},{1,3},{2,0},{3,1},{4,6},{5,7},{6,4},{7,5},{8,10},{9,11},{10,... | collective-permute-start | bytes 393224 | tf_op jit(solution)/shard_map/ppermute | solution.py:638
  7.3 6.6 %collective-permute-start.5 = (f32[64,512]{1,0:T(8,128)S(1)}, f32[64,512]{1,0:T(8,128)S(1)}, u32[]{:S(2)}, u32[]{:S(2)}) collective-permute-start(f32[64,512]{1,0:T(8,128)S(1)} %get-tuple-element.70.two), channel_id=1, source_target_pairs={{0,2},{1,3},{2,0},{3,1},{4,6},{5,7},{6,4},{7,5},{8,10},{9,11},{10,... | collective-permute-start | bytes 393224 | tf_op jit(solution)/shard_map/ppermute | solution.py:638
  13.9 18.8 %copy-start = (f32[1,1,128]{2,1,0:T(1,128)S(1)}, f32[1,1,128]{2,1,0:T(1,128)}, u32[]{:S(2)}) copy-start(f32[1,1,128]{2,1,0:T(1,128)} %param.15) | copy-start | bytes 1540
  13.9 11.0 %collective-permute-start.6 = (f32[264,512]{1,0:T(8,128)S(1)}, f32[264,512]{1,0:T(8,128)S(1)}, u32[]{:S(2)}, u32[]{:S(2)}) collective-permute-start(f32[264,512]{1,0:T(8,128)S(1)} %shard_map.99.mine), channel_id=1, source_target_pairs={{0,1},{1,0},{2,3},{3,2},{4,5},{5,4},{6,7},{7,6},{8,9},{9,8},{10,11... | collective-permute-start | bytes 1622024 | tf_op jit(solution)/shard_map/ppermute | solution.py:613
  14.0 10.9 %collective-permute-start.1 = (f32[104,128]{1,0:T(8,128)S(1)}, f32[104,128]{1,0:T(8,128)S(1)}, u32[]{:S(2)}, u32[]{:S(2)}) collective-permute-start(f32[104,128]{1,0:T(8,128)S(1)} %get-tuple-element.64), channel_id=1, source_target_pairs={{1,2},{2,1},{3,0},{0,3},{5,6},{6,5},{7,4},{4,7},{9,10},{10,9},{11,... | collective-permute-start | bytes 159752 | tf_op jit(solution)/shard_map/ppermute | solution.py:610
  17.7 5.4 %collective-permute-start.2 = (f32[96,128]{1,0:T(8,128)S(1)}, f32[96,128]{1,0:T(8,128)S(1)}, u32[]{:S(2)}, u32[]{:S(2)}) collective-permute-start(f32[96,128]{1,0:T(8,128)S(1)} %get-tuple-element.66), channel_id=1, source_target_pairs={{4,8},{8,4},{12,0},{0,12},{5,9},{9,5},{13,1},{1,13},{6,10},{10,6},... | collective-permute-start | bytes 147464 | tf_op jit(solution)/shard_map/ppermute | solution.py:611
  20.8 4.1 %collective-permute-start.3 = (f32[96,128]{1,0:T(8,128)S(1)}, f32[96,128]{1,0:T(8,128)S(1)}, u32[]{:S(2)}, u32[]{:S(2)}) collective-permute-start(f32[96,128]{1,0:T(8,128)S(1)} %get-tuple-element.67), channel_id=1, source_target_pairs={{0,4},{4,0},{8,12},{12,8},{1,5},{5,1},{9,13},{13,9},{2,6},{6,2},{1... | collective-permute-start | bytes 147464 | tf_op jit(solution)/shard_map/ppermute | solution.py:612
  27.3 5.4 %collective-permute-start.7 = (f32[80,128]{1,0:T(8,128)S(1)}, f32[80,128]{1,0:T(8,128)S(1)}, u32[]{:S(2)}, u32[]{:S(2)}) collective-permute-start(f32[80,128]{1,0:T(8,128)S(1)} %get-tuple-element.74), channel_id=1, source_target_pairs={{1,2},{2,1},{3,0},{0,3},{5,6},{6,5},{7,4},{4,7},{9,10},{10,9},{11,... | collective-permute-start | bytes 122888 | tf_op jit(solution)/shard_map/ppermute | solution.py:610
  27.5 5.2 %collective-permute-start.8 = (f32[72,128]{1,0:T(8,128)S(1)}, f32[72,128]{1,0:T(8,128)S(1)}, u32[]{:S(2)}, u32[]{:S(2)}) collective-permute-start(f32[72,128]{1,0:T(8,128)S(1)} %get-tuple-element.75), channel_id=1, source_target_pairs={{4,8},{8,4},{12,0},{0,12},{5,9},{9,5},{13,1},{1,13},{6,10},{10,6},... | collective-permute-start | bytes 110600 | tf_op jit(solution)/shard_map/ppermute | solution.py:611
  28.8 4.0 %collective-permute-start.9 = (f32[72,128]{1,0:T(8,128)S(1)}, f32[72,128]{1,0:T(8,128)S(1)}, u32[]{:S(2)}, u32[]{:S(2)}) collective-permute-start(f32[72,128]{1,0:T(8,128)S(1)} %get-tuple-element.76), channel_id=1, source_target_pairs={{0,4},{4,0},{8,12},{12,8},{1,5},{5,1},{9,13},{13,9},{2,6},{6,2},{1... | collective-permute-start | bytes 110600 | tf_op jit(solution)/shard_map/ppermute | solution.py:612
  28.8 1.2 %collective-permute-start.10 = (f32[8,128]{1,0:T(8,128)S(1)}, f32[8,128]{1,0:T(8,128)S(1)}, u32[]{:S(2)}, u32[]{:S(2)}) collective-permute-start(f32[8,128]{1,0:T(8,128)S(1)} %get-tuple-element.77), channel_id=1, source_target_pairs={{0,1},{1,0},{2,3},{3,2},{4,5},{5,4},{6,7},{7,6},{8,9},{9,8},{10,11... | collective-permute-start | bytes 12296 | tf_op jit(solution)/shard_map/ppermute | solution.py:613
  34.1 1.2 %collective-permute-start.11 = (f32[32,128]{1,0:T(8,128)S(1)}, f32[32,128]{1,0:T(8,128)S(1)}, u32[]{:S(2)}, u32[]{:S(2)}) collective-permute-start(f32[32,128]{1,0:T(8,128)S(1)} %shard_map.103.one), channel_id=1, source_target_pairs={{0,1},{1,0},{2,3},{3,2},{4,5},{5,4},{6,7},{7,6},{8,9},{9,8},{10,11... | collective-permute-start | bytes 49160 | tf_op jit(solution)/shard_map/ppermute | solution.py:677
  35.4 7.1 %collective-permute-start.12 = (f32[32,128]{1,0:T(8,128)S(1)}, f32[32,128]{1,0:T(8,128)S(1)}, u32[]{:S(2)}, u32[]{:S(2)}) collective-permute-start(f32[32,128]{1,0:T(8,128)S(1)} %shard_map.104.mine), channel_id=1, source_target_pairs={{0,114},{1,113},{2,112},{3,115},{4,118},{5,117},{6,116},{7,119},{8... | collective-permute-start | bytes 49160 | tf_op jit(solution)/shard_map/ppermute | solution.py:626
  37.4 5.2 %collective-permute-start.13 = (f32[32,128]{1,0:T(8,128)S(1)}, f32[32,128]{1,0:T(8,128)S(1)}, u32[]{:S(2)}, u32[]{:S(2)}) collective-permute-start(f32[32,128]{1,0:T(8,128)S(1)} %shard_map.104.mine), channel_id=1, source_target_pairs={{0,2},{1,3},{2,0},{3,1},{4,6},{5,7},{6,4},{7,5},{8,10},{9,11},{10,... | collective-permute-start | bytes 49160 | tf_op jit(solution)/shard_map/ppermute | solution.py:679
  42.7 1.2 %collective-permute-start.14 = (f32[24,128]{1,0:T(8,128)S(1)}, f32[24,128]{1,0:T(8,128)S(1)}, u32[]{:S(2)}, u32[]{:S(2)}) collective-permute-start(f32[24,128]{1,0:T(8,128)S(1)} %get-tuple-element.80.passed), channel_id=1, source_target_pairs={{0,1},{1,0},{2,3},{3,2},{4,5},{5,4},{6,7},{7,6},{8,9},{9,8},{10,11... | collective-permute-start | bytes 36872 | tf_op jit(solution)/shard_map/ppermute | solution.py:683
  44.6 4.9 %collective-permute-start.15 = (f32[8,512]{1,0:T(8,128)S(1)}, f32[8,512]{1,0:T(8,128)S(1)}, u32[]{:S(2)}, u32[]{:S(2)}) collective-permute-start(f32[8,512]{1,0:T(8,128)S(1)} %shard_map.106.iterate), channel_id=1, source_target_pairs={{0,28},{1,21},{2,30},{3,23},{4,16},{5,25},{6,18},{7,27},{8,20},{9,... | collective-permute-start | bytes 49160 | tf_op jit(solution)/shard_map/ppermute | solution.py:626
  48.0 3.7 %collective-permute-start.16 = (f32[8,512]{1,0:T(8,128)S(1)}, f32[8,512]{1,0:T(8,128)S(1)}, u32[]{:S(2)}, u32[]{:S(2)}) collective-permute-start(f32[8,512]{1,0:T(8,128)S(1)} %shard_map.106.iterate), channel_id=1, source_target_pairs={{0,16},{1,5},{2,18},{3,7},{4,20},{5,9},{6,22},{7,11},{8,24},{9,13}... | collective-permute-start | bytes 49160 | tf_op jit(solution)/shard_map/ppermute | solution.py:626
  49.5 3.7 %collective-permute-start.17 = (f32[8,512]{1,0:T(8,128)S(1)}, f32[8,512]{1,0:T(8,128)S(1)}, u32[]{:S(2)}, u32[]{:S(2)}) collective-permute-start(f32[8,512]{1,0:T(8,128)S(1)} %shard_map.106.iterate), channel_id=1, source_target_pairs={{0,12},{1,5},{2,14},{3,7},{4,0},{5,9},{6,2},{7,11},{8,4},{9,13},{1... | collective-permute-start | bytes 49160 | tf_op jit(solution)/shard_map/ppermute | solution.py:626
  53.2 1.2 %collective-permute-start.18 = (f32[24,512]{1,0:T(8,128)S(1)}, f32[24,512]{1,0:T(8,128)S(1)}, u32[]{:S(2)}, u32[]{:S(2)}) collective-permute-start(f32[24,512]{1,0:T(8,128)S(1)} %shard_map.107.got), channel_id=1, source_target_pairs={{0,1},{1,0},{2,3},{3,2},{4,5},{5,4},{6,7},{7,6},{8,9},{9,8},{10,11... | collective-permute-start | bytes 147464 | tf_op jit(solution)/shard_map/ppermute | solution.py:693
  57.3 7.6 %collective-permute-start.19 = (f32[80,128]{1,0:T(8,128)S(1)}, f32[80,128]{1,0:T(8,128)S(1)}, u32[]{:S(2)}, u32[]{:S(2)}) collective-permute-start(f32[80,128]{1,0:T(8,128)S(1)} %get-tuple-element.85), channel_id=1, source_target_pairs={{1,2},{2,1},{3,0},{0,3},{5,6},{6,5},{7,4},{4,7},{9,10},{10,9},{11,... | collective-permute-start | bytes 122888 | tf_op jit(solution)/shard_map/ppermute | solution.py:610
  59.4 5.2 %collective-permute-start.20 = (f32[72,128]{1,0:T(8,128)S(1)}, f32[72,128]{1,0:T(8,128)S(1)}, u32[]{:S(2)}, u32[]{:S(2)}) collective-permute-start(f32[72,128]{1,0:T(8,128)S(1)} %get-tuple-element.86), channel_id=1, source_target_pairs={{4,8},{8,4},{12,0},{0,12},{5,9},{9,5},{13,1},{1,13},{6,10},{10,6},... | collective-permute-start | bytes 110600 | tf_op jit(solution)/shard_map/ppermute | solution.py:611
  61.0 4.0 %collective-permute-start.21 = (f32[72,128]{1,0:T(8,128)S(1)}, f32[72,128]{1,0:T(8,128)S(1)}, u32[]{:S(2)}, u32[]{:S(2)}) collective-permute-start(f32[72,128]{1,0:T(8,128)S(1)} %get-tuple-element.87), channel_id=1, source_target_pairs={{0,4},{4,0},{8,12},{12,8},{1,5},{5,1},{9,13},{13,9},{2,6},{6,2},{1... | collective-permute-start | bytes 110600 | tf_op jit(solution)/shard_map/ppermute | solution.py:612
  61.0 1.2 %collective-permute-start.22 = (f32[8,128]{1,0:T(8,128)S(1)}, f32[8,128]{1,0:T(8,128)S(1)}, u32[]{:S(2)}, u32[]{:S(2)}) collective-permute-start(f32[8,128]{1,0:T(8,128)S(1)} %get-tuple-element.88), channel_id=1, source_target_pairs={{0,1},{1,0},{2,3},{3,2},{4,5},{5,4},{6,7},{7,6},{8,9},{9,8},{10,11... | collective-permute-start | bytes 12296 | tf_op jit(solution)/shard_map/ppermute | solution.py:613
  67.2 6.3 %collective-permute-start.23 = (f32[3,4,8,128]{3,2,1,0:T(8,128)S(1)}, f32[3,4,8,128]{3,2,1,0:T(8,128)S(1)}, u32[]{:S(2)}, u32[]{:S(2)}) collective-permute-start(f32[3,4,8,128]{3,2,1,0:T(8,128)S(1)} %get-tuple-element.89), channel_id=1, source_target_pairs={{0,112},{16,0},{32,16},{48,32},{64,48},{80,64},{96,80},{112,96},{1... | collective-permute-start | bytes 147464 | tf_op jit(solution)/shard_map/ppermute | solution.py:706

commit v5 on v4

--- a/solution.py
+++ b/solution.py
@@ -343,10 +343,28 @@
     write_columns(flags, lambda p, c: out[p, c], oz1, oz2)
 
 
+class Joined:
+    def __init__(self, tail, head):
+        self.tail, self.head = tail, head
+
+    def __getitem__(self, at):
+        p, *rest = at if isinstance(at, tuple) else (at,)
+        array, p = (self.tail, p) if p < TAIL else (self.head, p - TAIL)
+        return array[(p, *rest)]
+
+
+def spread_kernel(velocity, agg, iterate, out):
+    own = table(iterate[...])
+    for p in range(HEAD):
+        at = where_in(agg[TAIL + p])
+        for c in range(3):
+            out[p, c] = velocity[TAIL + p, c] + pick(own[c], at)
+
+
 def third_sweep_kernel(
     flags, force, weight, inverse, old, mult, mult_up, face, inverse_t, by_row, spots, place,
-    z2, y1, y2, z1, az2, ay1, ay2, az1, agg, iterate, got, swapped,
-    out, out_mult, out_up, oz1, oz2, velocity,
+    z2, y1, y2, z1, az2, ay1, ay2, az1, agg, iterate, got, swapped, lifted,
+    out, out_mult, out_up, oz1, oz2, lower_part,
 ):
     core_zero = yes(flags, 1, (24, NAGG))
     a = jnp.where(core_zero, got[...], swapped[...])
@@ -354,10 +372,11 @@
     own, prev = table(iterate[...]), table(a[8:16])
     low, low_prev = table(b[8:16]), table(b[0:8])
     high, high_prev = table(a[16:24]), table(a[0:8])
-    for p in range(NP):
+    for p in range(TAIL):
         at = where_in(agg[p])
         for c in range(3):
-            velocity[p, c] = old[p, c] + pick((prev if p < TAIL else own)[c], at)
+            lower_part[p, c] = old[p, c] + pick(prev[c], at)
+    velocity = Joined(lower_part, lifted)
 
     y_low, y_high, z_low, z_high = sides(flags, y1, y2, z1, z2)
     y_even, z_even = yes(flags, 0, (ROWS, 128)), yes(flags, 1, (8, 128))
@@ -684,6 +703,7 @@
     iterate = call(solve_kernel, [((8, NAGG), F32)], [pltpu.VMEM((8, NAGG), F32)], n_in=5)(
         kept, passed, swapped, k_high, k_low
     )[0]
+    lifted = call(spread_kernel, [((HEAD, 3, 8, 128), F32)], n_in=3)(velocity, agg, iterate)[0]
     got = [
         by_core(iterate, (1, -1, 0), (1, 1, 0)),
         by_core(iterate, (1, 0, 0), (0, 1, 0)),
@@ -693,10 +713,10 @@
     swapped = lax.ppermute(got, "gz", swaps("gz", 0))
     velocity, mult, mult_up, *msgs = call(
         third_sweep_kernel, [field, plane, plane, z_msg, ((LINES + 8, 128), F32)],
-        [pltpu.VMEM((NP, 3, 8, 128), F32)], n_in=24,
+        [pltpu.VMEM((TAIL, 3, 8, 128), F32)], n_in=25,
     )(
         flags, force_e, weight, inverse, velocity, mult, mult_up, face, inverse_t, by_row, spots, place,
-        *edges, *labels, agg, iterate, got, swapped,
+        *edges, *labels, agg, iterate, got, swapped, lifted,
     )
     edges = trade(*call(lines_kernel, [y_msg, y_msg], n_in=2)(flags, velocity), *msgs)
     head, tail, mult = call(

time: 74.4 us -> 74.8 us (level)
    pallas_call x16 -> x17, Pallas kernels: 17.9 us -> 18.6 us  [run(): return kernel(*args[:n_smem], *held, *far)]
  transfers between devices with their start and end apart: 24 -> 24, of which waited for: 15 -> 15; matrix products, arithmetic and copies ran while one was open for 0% -> 0% of each run, Pallas kernels for 10% -> 11%
where the time goes in v5:
time: 74.8 us; the launch traced here: 74.6 us
  starting transfers between devices  27 us (36%)
  waiting for transfers between devices  26.8 us (36%)
  Pallas kernels  19.9 us (27%)
  between operations  0.97 us (1%)
    pallas_call x17, Pallas kernels, run(): return kernel(*args[:n_smem], *held, *far)  18.6 us
    ppermute x3, waiting for transfers between devices, trade(): lax.ppermute(y1, 'gy', swaps('gy', 1))  7.43 us
    ppermute x4, waiting for transfers between devices, by_core(): return lax.ppermute(x, ('gx', 'gy', 'gz'), pairs)  7.33 us
    ppermute x4, starting transfers between devices, by_core(): return lax.ppermute(x, ('gx', 'gy', 'gz'), pairs)  6.87 us
    ppermute x3, starting transfers between devices, trade(): lax.ppermute(y1, 'gy', swaps('gy', 1))  5.97 us
    ppermute x3, starting transfers between devices, trade(): lax.ppermute(z2, 'gz', swaps('gz', 1))  5.7 us
    ppermute x1, waiting for transfers between devices, shards(): tail = lax.ppermute(tail, 'gx', ring('gx', -1))  4.48 us
    ppermute x2, starting transfers between devices, shards(): lax.ppermute(x, 'gz', ring('gz', 2))  3.62 us
  transfers between devices with their start and end apart: 24, of which 15 were waited for; matrix products, arithmetic and copies ran while one was open for 0% of the time, Pallas kernels for 11%

profile of v5, /device:TPU:6, one launch (start us, length us, event | category | flops | bytes accessed | tf_op | source)
XLA Modules:
  0.0 74.6 jit_solution(9666214296572841217)
XLA Ops:
  0.6 1.2 %shard_map.95 = (f32[7,5,8,128]{3,2,1,0:T(8,128)S(1)}, f32[3,16,8,128]{3,2,1,0:T(8,128)S(1)}, f32[16,8,128]{2,1,0:T(8,128)S(1)}, s32[16,8,128]{2,1,0:T(8,128)S(1...) custom-call(f32[3,16,8,128]{3,2,1,0:T(8,128)} %force.1, f32[16,8,128]{2,1,0:T(8,128)} %kappa.1, ...), custom_call_target="tpu_custom_call" | custom-call | tf_op jit(solution)/shard_map/pallas_call | solution.py:48
  1.8 1.9 %collective-permute-start = (f32[7,5,8,128]{3,2,1,0:T(8,128)S(1)}, f32[7,5,8,128]{3,2,1,0:T(8,128)S(1)}, u32[]{:S(2)}, u32[]{:S(2)}) collective-permute-start(f32[7,5,8,128]{3,2,1,0:T(8,128)S(1)} %get-tuple-element.52), channel_id=1, source_target_pairs={{0,16},{16,32},{32,48},{48,64},{64,80},{80,96},{96,112},{112,0},{1... | collective-permute-start | bytes 430088 | tf_op jit(solution)/shard_map/ppermute | solution.py:656
  3.7 3.6 %collective-permute-start.4 = (f32[64,512]{1,0:T(8,128)S(1)}, f32[64,512]{1,0:T(8,128)S(1)}, u32[]{:S(2)}, u32[]{:S(2)}) collective-permute-start(f32[64,512]{1,0:T(8,128)S(1)} %get-tuple-element.69.one), channel_id=1, source_target_pairs={{0,2},{1,3},{2,0},{3,1},{4,6},{5,7},{6,4},{7,5},{8,10},{9,11},{10,... | collective-permute-start | bytes 393224 | tf_op jit(solution)/shard_map/ppermute | solution.py:657
  7.3 4.2 %shard_map.96 = (f32[2,4096,128]{2,1,0:T(8,128)S(1)}, s32[8,256]{1,0:T(8,128)S(1)}, bf16[128,256]{1,0:T(8,128)(2,1)S(1)}) custom-call(s32[8,128]{1,0:T(8,128)S(1)} %get-tuple-element.48.flags, f32[192,4096]{1,0:T(8,128)} %bitcast.9, s32[4,48]{1,0:T(4,128)} %bitcast.11, s32[1,48]{1,0:T(1,128)} %bitcast.12), custom_call_target="tpu_custom_call" | custom-call | tf_op jit(solution)/shard_map/pallas_call | solution.py:48
  11.6 2.4 %shard_map.97 = (f32[22,3,8,128]{3,2,1,0:T(8,128)S(1)}, f32[22,8,128]{2,1,0:T(8,128)S(1)}, f32[22,8,128]{2,1,0:T(8,128)S(1)}, s32[22,8,128]{2,1,0:T(8,128)S(1)},...) custom-call(s32[8,128]{1,0:T(8,128)S(1)} %get-tuple-element.48.flags, ...), custom_call_target="tpu_custom_call" | custom-call | tf_op jit(solution)/shard_map/pallas_call | solution.py:48
  14.1 3.6 %collective-permute-start.1 = (f32[104,128]{1,0:T(8,128)S(1)}, f32[104,128]{1,0:T(8,128)S(1)}, u32[]{:S(2)}, u32[]{:S(2)}) collective-permute-start(f32[104,128]{1,0:T(8,128)S(1)} %get-tuple-element.64), channel_id=1, source_target_pairs={{1,2},{2,1},{3,0},{0,3},{5,6},{6,5},{7,4},{4,7},{9,10},{10,9},{11,... | collective-permute-start | bytes 159752 | tf_op jit(solution)/shard_map/ppermute | solution.py:629
  17.8 3.1 %collective-permute-start.2 = (f32[96,128]{1,0:T(8,128)S(1)}, f32[96,128]{1,0:T(8,128)S(1)}, u32[]{:S(2)}, u32[]{:S(2)}) collective-permute-start(f32[96,128]{1,0:T(8,128)S(1)} %get-tuple-element.66), channel_id=1, source_target_pairs={{4,8},{8,4},{12,0},{0,12},{5,9},{9,5},{13,1},{1,13},{6,10},{10,6},... | collective-permute-start | bytes 147464 | tf_op jit(solution)/shard_map/ppermute | solution.py:630
  21.0 2.1 %collective-permute-done.2.y1.ay1 = f32[96,128]{1,0:T(8,128)S(1)} collective-permute-done((f32[96,128]{1,0:T(8,128)S(1)}, f32[96,128]{1,0:T(8,128)S(1)}, u32[]{:S(2)}, u32[]{:S(2)}) %collective-permute-start.2) | collective-permute-done | bytes 49184 | tf_op jit(solution)/shard_map/ppermute | solution.py:630
  23.2 1.8 %collective-permute-done.3.y2.ay2 = f32[96,128]{1,0:T(8,128)S(1)} collective-permute-done((f32[96,128]{1,0:T(8,128)S(1)}, f32[96,128]{1,0:T(8,128)S(1)}, u32[]{:S(2)}, u32[]{:S(2)}) %collective-permute-start.3) | collective-permute-done | bytes 49184 | tf_op jit(solution)/shard_map/ppermute | solution.py:631
  25.0 2.6 %shard_map.100 = (f32[22,3,8,128]{3,2,1,0:T(8,128)S(1)}, f32[3,8,128]{2,1,0:T(8,128)S(1)}, f32[3,8,128]{2,1,0:T(8,128)S(1)}, f32[8,128]{1,0:T(8,128)S(1)}, f32[80,128]{1,0:T(8,128)S(1)}) custom-call(s32[8,128]{1,0:T(8,128)S(1)} %get-tuple-element.48.flags, f32[22,3,8,128]{3,2,1,0:T(8,128)S(1)} %get-tuple-element.56.force, ...), custom_call_target="tpu_custom_call" | custom-call | tf_op jit(solution)/shard_map/pallas_call | solution.py:48
  27.7 1.3 %collective-permute-start.8 = (f32[72,128]{1,0:T(8,128)S(1)}, f32[72,128]{1,0:T(8,128)S(1)}, u32[]{:S(2)}, u32[]{:S(2)}) collective-permute-start(f32[72,128]{1,0:T(8,128)S(1)} %get-tuple-element.75), channel_id=1, source_target_pairs={{4,8},{8,4},{12,0},{0,12},{5,9},{9,5},{13,1},{1,13},{6,10},{10,6},... | collective-permute-start | bytes 110600 | tf_op jit(solution)/shard_map/ppermute | solution.py:630
  29.4 0.8 %collective-permute-done.10.z1 = f32[8,128]{1,0:T(8,128)S(1)} collective-permute-done((f32[8,128]{1,0:T(8,128)S(1)}, f32[8,128]{1,0:T(8,128)S(1)}, u32[]{:S(2)}, u32[]{:S(2)}) %collective-permute-start.10) | collective-permute-done | bytes 4128 | tf_op jit(solution)/shard_map/ppermute | solution.py:632
  30.2 2.8 %collective-permute-done.8.y1 = f32[72,128]{1,0:T(8,128)S(1)} collective-permute-done((f32[72,128]{1,0:T(8,128)S(1)}, f32[72,128]{1,0:T(8,128)S(1)}, u32[]{:S(2)}, u32[]{:S(2)}) %collective-permute-start.8) | collective-permute-done | bytes 36896 | tf_op jit(solution)/shard_map/ppermute | solution.py:630
  33.0 1.4 %shard_map.103.one = f32[32,128]{1,0:T(8,128)S(1)} custom-call(bf16[512,512]{1,0:T(8,128)(2,1)S(1)} %get-tuple-element.78.after.high, s32[8,128]{1,0:T(8,128)S(1)} %get-tuple-element.48.flags, f32[22,3,8,128]{3,2,1,0:T(8,128)S(1)} %get-tuple-element.56.force, f32[22,8,128]{2,1,0:T(8,128)S(1)} %get-tuple-element.57.weight, ...), custom_call_target="tpu_custom_call" | custom-call | tf_op jit(solution)/shard_map/pallas_call | solution.py:48
  34.5 1.2 %collective-permute-done.11.two = f32[32,128]{1,0:T(8,128)S(1)} collective-permute-done((f32[32,128]{1,0:T(8,128)S(1)}, f32[32,128]{1,0:T(8,128)S(1)}, u32[]{:S(2)}, u32[]{:S(2)}) %collective-permute-start.11) | collective-permute-done | bytes 16416 | tf_op jit(solution)/shard_map/ppermute | solution.py:696
  35.6 2.1 %collective-permute-start.12 = (f32[32,128]{1,0:T(8,128)S(1)}, f32[32,128]{1,0:T(8,128)S(1)}, u32[]{:S(2)}, u32[]{:S(2)}) collective-permute-start(f32[32,128]{1,0:T(8,128)S(1)} %shard_map.104.mine), channel_id=1, source_target_pairs={{0,114},{1,113},{2,112},{3,115},{4,118},{5,117},{6,116},{7,119},{8... | collective-permute-start | bytes 49160 | tf_op jit(solution)/shard_map/ppermute | solution.py:645
  37.7 1.4 %collective-permute-start.13 = (f32[32,128]{1,0:T(8,128)S(1)}, f32[32,128]{1,0:T(8,128)S(1)}, u32[]{:S(2)}, u32[]{:S(2)}) collective-permute-start(f32[32,128]{1,0:T(8,128)S(1)} %shard_map.104.mine), channel_id=1, source_target_pairs={{0,2},{1,3},{2,0},{3,1},{4,6},{5,7},{6,4},{7,5},{8,10},{9,11},{10,... | collective-permute-start | bytes 49160 | tf_op jit(solution)/shard_map/ppermute | solution.py:698
  39.1 3.6 %collective-permute-done.12.above = f32[32,128]{1,0:T(8,128)S(1)} collective-permute-done((f32[32,128]{1,0:T(8,128)S(1)}, f32[32,128]{1,0:T(8,128)S(1)}, u32[]{:S(2)}, u32[]{:S(2)}) %collective-permute-start.12) | collective-permute-done | bytes 16416 | tf_op jit(solution)/shard_map/ppermute | solution.py:645
  43.0 1.2 %collective-permute-done.14.swapped = f32[24,128]{1,0:T(8,128)S(1)} collective-permute-done((f32[24,128]{1,0:T(8,128)S(1)}, f32[24,128]{1,0:T(8,128)S(1)}, u32[]{:S(2)}, u32[]{:S(2)}) %collective-permute-start.14) | collective-permute-done | bytes 12320 | tf_op jit(solution)/shard_map/ppermute | solution.py:702
  44.9 3.4 %collective-permute-start.15 = (f32[8,512]{1,0:T(8,128)S(1)}, f32[8,512]{1,0:T(8,128)S(1)}, u32[]{:S(2)}, u32[]{:S(2)}) collective-permute-start(f32[8,512]{1,0:T(8,128)S(1)} %shard_map.106.iterate), channel_id=1, source_target_pairs={{0,28},{1,21},{2,30},{3,23},{4,16},{5,25},{6,18},{7,27},{8,20},{9,... | collective-permute-start | bytes 49160 | tf_op jit(solution)/shard_map/ppermute | solution.py:645
  48.3 1.4 %collective-permute-start.16 = (f32[8,512]{1,0:T(8,128)S(1)}, f32[8,512]{1,0:T(8,128)S(1)}, u32[]{:S(2)}, u32[]{:S(2)}) collective-permute-start(f32[8,512]{1,0:T(8,128)S(1)} %shard_map.106.iterate), channel_id=1, source_target_pairs={{0,16},{1,5},{2,18},{3,7},{4,20},{5,9},{6,22},{7,11},{8,24},{9,13}... | collective-permute-start | bytes 49160 | tf_op jit(solution)/shard_map/ppermute | solution.py:645
  49.7 2.3 %collective-permute-done.16.b = f32[8,512]{1,0:T(8,128)S(1)} collective-permute-done((f32[8,512]{1,0:T(8,128)S(1)}, f32[8,512]{1,0:T(8,128)S(1)}, u32[]{:S(2)}, u32[]{:S(2)}) %collective-permute-start.16) | collective-permute-done | bytes 16416 | tf_op jit(solution)/shard_map/ppermute | solution.py:645
  52.0 1.4 %collective-permute-done.17.c = f32[8,512]{1,0:T(8,128)S(1)} collective-permute-done((f32[8,512]{1,0:T(8,128)S(1)}, f32[8,512]{1,0:T(8,128)S(1)}, u32[]{:S(2)}, u32[]{:S(2)}) %collective-permute-start.17) | collective-permute-done | bytes 16416 | tf_op jit(solution)/shard_map/ppermute | solution.py:645
  53.8 0.9 %collective-permute-done.18.swapped = f32[24,512]{1,0:T(8,128)S(1)} collective-permute-done((f32[24,512]{1,0:T(8,128)S(1)}, f32[24,512]{1,0:T(8,128)S(1)}, u32[]{:S(2)}, u32[]{:S(2)}) %collective-permute-start.18) | collective-permute-done | bytes 49184 | tf_op jit(solution)/shard_map/ppermute | solution.py:713
  54.7 2.9 %shard_map.109 = (f32[22,3,8,128]{3,2,1,0:T(8,128)S(1)}, f32[3,8,128]{2,1,0:T(8,128)S(1)}, f32[3,8,128]{2,1,0:T(8,128)S(1)}, f32[8,128]{1,0:T(8,128)S(1)}, f32[80,128]{1,0:T(8,128)S(1)}) custom-call(s32[8,128]{1,0:T(8,128)S(1)} %get-tuple-element.48.flags, f32[22,3,8,128]{3,2,1,0:T(8,128)S(1)} %get-tuple-element.56.force, ...), custom_call_target="tpu_custom_call" | custom-call | tf_op jit(solution)/shard_map/pallas_call | solution.py:48
  57.5 2.0 %collective-permute-start.19 = (f32[80,128]{1,0:T(8,128)S(1)}, f32[80,128]{1,0:T(8,128)S(1)}, u32[]{:S(2)}, u32[]{:S(2)}) collective-permute-start(f32[80,128]{1,0:T(8,128)S(1)} %get-tuple-element.85), channel_id=1, source_target_pairs={{1,2},{2,1},{3,0},{0,3},{5,6},{6,5},{7,4},{4,7},{9,10},{10,9},{11,... | collective-permute-start | bytes 122888 | tf_op jit(solution)/shard_map/ppermute | solution.py:629
  59.6 1.6 %collective-permute-start.20 = (f32[72,128]{1,0:T(8,128)S(1)}, f32[72,128]{1,0:T(8,128)S(1)}, u32[]{:S(2)}, u32[]{:S(2)}) collective-permute-start(f32[72,128]{1,0:T(8,128)S(1)} %get-tuple-element.86), channel_id=1, source_target_pairs={{4,8},{8,4},{12,0},{0,12},{5,9},{9,5},{13,1},{1,13},{6,10},{10,6},... | collective-permute-start | bytes 110600 | tf_op jit(solution)/shard_map/ppermute | solution.py:630
  61.2 1.1 %collective-permute-done.22.z1 = f32[8,128]{1,0:T(8,128)S(1)} collective-permute-done((f32[8,128]{1,0:T(8,128)S(1)}, f32[8,128]{1,0:T(8,128)S(1)}, u32[]{:S(2)}, u32[]{:S(2)}) %collective-permute-start.22) | collective-permute-done | bytes 4128 | tf_op jit(solution)/shard_map/ppermute | solution.py:632
  62.3 2.5 %collective-permute-done.20.y1 = f32[72,128]{1,0:T(8,128)S(1)} collective-permute-done((f32[72,128]{1,0:T(8,128)S(1)}, f32[72,128]{1,0:T(8,128)S(1)}, u32[]{:S(2)}, u32[]{:S(2)}) %collective-permute-start.20) | collective-permute-done | bytes 36896 | tf_op jit(solution)/shard_map/ppermute | solution.py:630
  65.1 2.4 %shard_map.111 = (f32[3,12,8,128]{3,2,1,0:T(8,128)S(1)}, f32[3,4,8,128]{3,2,1,0:T(8,128)S(1)}, f32[3,8,128]{2,1,0:T(8,128)S(1)}) custom-call(s32[8,128]{1,0:T(8,128)S(1)} %get-tuple-element.48.flags, f32[22,3,8,128]{3,2,1,0:T(8,128)S(1)} %get-tuple-element.56.force, f32[22,8,128]{2,1,0:T(8,128)S(1)} %get-tuple-element.57.weight, ...), custom_call_target="tpu_custom_call" | custom-call | tf_op jit(solution)/shard_map/pallas_call | solution.py:48
  67.6 1.1 %collective-permute-start.23 = (f32[3,4,8,128]{3,2,1,0:T(8,128)S(1)}, f32[3,4,8,128]{3,2,1,0:T(8,128)S(1)}, u32[]{:S(2)}, u32[]{:S(2)}) collective-permute-start(f32[3,4,8,128]{3,2,1,0:T(8,128)S(1)} %get-tuple-element.89), channel_id=1, source_target_pairs={{0,112},{16,0},{32,16},{48,32},{64,48},{80,64},{96,80},{112,96},{1... | collective-permute-start | bytes 147464 | tf_op jit(solution)/shard_map/ppermute | solution.py:726
  69.4 4.5 %collective-permute-done.23.tail = f32[3,4,8,128]{3,2,1,0:T(8,128)S(1)} collective-permute-done((f32[3,4,8,128]{3,2,1,0:T(8,128)S(1)}, f32[3,4,8,128]{3,2,1,0:T(8,128)S(1)}, u32[]{:S(2)}, u32[]{:S(2)}) %collective-permute-start.23) | collective-permute-done | bytes 49184 | tf_op jit(solution)/shard_map/ppermute | solution.py:726
  (37 shorter events, 4.0 us)
Async XLA Ops:
  1.8 9.7 %collective-permute-start = (f32[7,5,8,128]{3,2,1,0:T(8,128)S(1)}, f32[7,5,8,128]{3,2,1,0:T(8,128)S(1)}, u32[]{:S(2)}, u32[]{:S(2)}) collective-permute-start(f32[7,5,8,128]{3,2,1,0:T(8,128)S(1)} %get-tuple-element.52), channel_id=1, source_target_pairs={{0,16},{16,32},{32,48},{48,64},{64,80},{80,96},{96,112},{112,0},{1... | collective-permute-start | bytes 430088 | tf_op jit(solution)/shard_map/ppermute | solution.py:656
  3.7 10.2 %collective-permute-start.4 = (f32[64,512]{1,0:T(8,128)S(1)}, f32[64,512]{1,0:T(8,128)S(1)}, u32[]{:S(2)}, u32[]{:S(2)}) collective-permute-start(f32[64,512]{1,0:T(8,128)S(1)} %get-tuple-element.69.one), channel_id=1, source_target_pairs={{0,2},{1,3},{2,0},{3,1},{4,6},{5,7},{6,4},{7,5},{8,10},{9,11},{10,... | collective-permute-start | bytes 393224 | tf_op jit(solution)/shard_map/ppermute | solution.py:657
  7.3 6.7 %collective-permute-start.5 = (f32[64,512]{1,0:T(8,128)S(1)}, f32[64,512]{1,0:T(8,128)S(1)}, u32[]{:S(2)}, u32[]{:S(2)}) collective-permute-start(f32[64,512]{1,0:T(8,128)S(1)} %get-tuple-element.70.two), channel_id=1, source_target_pairs={{0,2},{1,3},{2,0},{3,1},{4,6},{5,7},{6,4},{7,5},{8,10},{9,11},{10,... | collective-permute-start | bytes 393224 | tf_op jit(solution)/shard_map/ppermute | solution.py:657
  14.0 19.0 %copy-start = (f32[1,1,128]{2,1,0:T(1,128)S(1)}, f32[1,1,128]{2,1,0:T(1,128)}, u32[]{:S(2)}) copy-start(f32[1,1,128]{2,1,0:T(1,128)} %param.15) | copy-start | bytes 1540
  14.0 11.0 %collective-permute-start.6 = (f32[264,512]{1,0:T(8,128)S(1)}, f32[264,512]{1,0:T(8,128)S(1)}, u32[]{:S(2)}, u32[]{:S(2)}) collective-permute-start(f32[264,512]{1,0:T(8,128)S(1)} %shard_map.99.mine), channel_id=1, source_target_pairs={{0,1},{1,0},{2,3},{3,2},{4,5},{5,4},{6,7},{7,6},{8,9},{9,8},{10,11... | collective-permute-start | bytes 1622024 | tf_op jit(solution)/shard_map/ppermute | solution.py:632
  14.1 10.9 %collective-permute-start.1 = (f32[104,128]{1,0:T(8,128)S(1)}, f32[104,128]{1,0:T(8,128)S(1)}, u32[]{:S(2)}, u32[]{:S(2)}) collective-permute-start(f32[104,128]{1,0:T(8,128)S(1)} %get-tuple-element.64), channel_id=1, source_target_pairs={{1,2},{2,1},{3,0},{0,3},{5,6},{6,5},{7,4},{4,7},{9,10},{10,9},{11,... | collective-permute-start | bytes 159752 | tf_op jit(solution)/shard_map/ppermute | solution.py:629
  17.8 5.4 %collective-permute-start.2 = (f32[96,128]{1,0:T(8,128)S(1)}, f32[96,128]{1,0:T(8,128)S(1)}, u32[]{:S(2)}, u32[]{:S(2)}) collective-permute-start(f32[96,128]{1,0:T(8,128)S(1)} %get-tuple-element.66), channel_id=1, source_target_pairs={{4,8},{8,4},{12,0},{0,12},{5,9},{9,5},{13,1},{1,13},{6,10},{10,6},... | collective-permute-start | bytes 147464 | tf_op jit(solution)/shard_map/ppermute | solution.py:630
  20.9 4.1 %collective-permute-start.3 = (f32[96,128]{1,0:T(8,128)S(1)}, f32[96,128]{1,0:T(8,128)S(1)}, u32[]{:S(2)}, u32[]{:S(2)}) collective-permute-start(f32[96,128]{1,0:T(8,128)S(1)} %get-tuple-element.67), channel_id=1, source_target_pairs={{0,4},{4,0},{8,12},{12,8},{1,5},{5,1},{9,13},{13,9},{2,6},{6,2},{1... | collective-permute-start | bytes 147464 | tf_op jit(solution)/shard_map/ppermute | solution.py:631
  27.6 5.4 %collective-permute-start.7 = (f32[80,128]{1,0:T(8,128)S(1)}, f32[80,128]{1,0:T(8,128)S(1)}, u32[]{:S(2)}, u32[]{:S(2)}) collective-permute-start(f32[80,128]{1,0:T(8,128)S(1)} %get-tuple-element.74), channel_id=1, source_target_pairs={{1,2},{2,1},{3,0},{0,3},{5,6},{6,5},{7,4},{4,7},{9,10},{10,9},{11,... | collective-permute-start | bytes 122888 | tf_op jit(solution)/shard_map/ppermute | solution.py:629
  27.7 5.2 %collective-permute-start.8 = (f32[72,128]{1,0:T(8,128)S(1)}, f32[72,128]{1,0:T(8,128)S(1)}, u32[]{:S(2)}, u32[]{:S(2)}) collective-permute-start(f32[72,128]{1,0:T(8,128)S(1)} %get-tuple-element.75), channel_id=1, source_target_pairs={{4,8},{8,4},{12,0},{0,12},{5,9},{9,5},{13,1},{1,13},{6,10},{10,6},... | collective-permute-start | bytes 110600 | tf_op jit(solution)/shard_map/ppermute | solution.py:630
  29.0 4.0 %collective-permute-start.9 = (f32[72,128]{1,0:T(8,128)S(1)}, f32[72,128]{1,0:T(8,128)S(1)}, u32[]{:S(2)}, u32[]{:S(2)}) collective-permute-start(f32[72,128]{1,0:T(8,128)S(1)} %get-tuple-element.76), channel_id=1, source_target_pairs={{0,4},{4,0},{8,12},{12,8},{1,5},{5,1},{9,13},{13,9},{2,6},{6,2},{1... | collective-permute-start | bytes 110600 | tf_op jit(solution)/shard_map/ppermute | solution.py:631
  29.0 1.2 %collective-permute-start.10 = (f32[8,128]{1,0:T(8,128)S(1)}, f32[8,128]{1,0:T(8,128)S(1)}, u32[]{:S(2)}, u32[]{:S(2)}) collective-permute-start(f32[8,128]{1,0:T(8,128)S(1)} %get-tuple-element.77), channel_id=1, source_target_pairs={{0,1},{1,0},{2,3},{3,2},{4,5},{5,4},{6,7},{7,6},{8,9},{9,8},{10,11... | collective-permute-start | bytes 12296 | tf_op jit(solution)/shard_map/ppermute | solution.py:632
  34.4 1.2 %collective-permute-start.11 = (f32[32,128]{1,0:T(8,128)S(1)}, f32[32,128]{1,0:T(8,128)S(1)}, u32[]{:S(2)}, u32[]{:S(2)}) collective-permute-start(f32[32,128]{1,0:T(8,128)S(1)} %shard_map.103.one), channel_id=1, source_target_pairs={{0,1},{1,0},{2,3},{3,2},{4,5},{5,4},{6,7},{7,6},{8,9},{9,8},{10,11... | collective-permute-start | bytes 49160 | tf_op jit(solution)/shard_map/ppermute | solution.py:696
  35.6 7.1 %collective-permute-start.12 = (f32[32,128]{1,0:T(8,128)S(1)}, f32[32,128]{1,0:T(8,128)S(1)}, u32[]{:S(2)}, u32[]{:S(2)}) collective-permute-start(f32[32,128]{1,0:T(8,128)S(1)} %shard_map.104.mine), channel_id=1, source_target_pairs={{0,114},{1,113},{2,112},{3,115},{4,118},{5,117},{6,116},{7,119},{8... | collective-permute-start | bytes 49160 | tf_op jit(solution)/shard_map/ppermute | solution.py:645
  37.7 5.2 %collective-permute-start.13 = (f32[32,128]{1,0:T(8,128)S(1)}, f32[32,128]{1,0:T(8,128)S(1)}, u32[]{:S(2)}, u32[]{:S(2)}) collective-permute-start(f32[32,128]{1,0:T(8,128)S(1)} %shard_map.104.mine), channel_id=1, source_target_pairs={{0,2},{1,3},{2,0},{3,1},{4,6},{5,7},{6,4},{7,5},{8,10},{9,11},{10,... | collective-permute-start | bytes 49160 | tf_op jit(solution)/shard_map/ppermute | solution.py:698
  43.0 1.2 %collective-permute-start.14 = (f32[24,128]{1,0:T(8,128)S(1)}, f32[24,128]{1,0:T(8,128)S(1)}, u32[]{:S(2)}, u32[]{:S(2)}) collective-permute-start(f32[24,128]{1,0:T(8,128)S(1)} %get-tuple-element.80.passed), channel_id=1, source_target_pairs={{0,1},{1,0},{2,3},{3,2},{4,5},{5,4},{6,7},{7,6},{8,9},{9,8},{10,11... | collective-permute-start | bytes 36872 | tf_op jit(solution)/shard_map/ppermute | solution.py:702
  44.9 4.8 %collective-permute-start.15 = (f32[8,512]{1,0:T(8,128)S(1)}, f32[8,512]{1,0:T(8,128)S(1)}, u32[]{:S(2)}, u32[]{:S(2)}) collective-permute-start(f32[8,512]{1,0:T(8,128)S(1)} %shard_map.106.iterate), channel_id=1, source_target_pairs={{0,28},{1,21},{2,30},{3,23},{4,16},{5,25},{6,18},{7,27},{8,20},{9,... | collective-permute-start | bytes 49160 | tf_op jit(solution)/shard_map/ppermute | solution.py:645
  48.3 3.7 %collective-permute-start.16 = (f32[8,512]{1,0:T(8,128)S(1)}, f32[8,512]{1,0:T(8,128)S(1)}, u32[]{:S(2)}, u32[]{:S(2)}) collective-permute-start(f32[8,512]{1,0:T(8,128)S(1)} %shard_map.106.iterate), channel_id=1, source_target_pairs={{0,16},{1,5},{2,18},{3,7},{4,20},{5,9},{6,22},{7,11},{8,24},{9,13}... | collective-permute-start | bytes 49160 | tf_op jit(solution)/shard_map/ppermute | solution.py:645
  49.7 3.7 %collective-permute-start.17 = (f32[8,512]{1,0:T(8,128)S(1)}, f32[8,512]{1,0:T(8,128)S(1)}, u32[]{:S(2)}, u32[]{:S(2)}) collective-permute-start(f32[8,512]{1,0:T(8,128)S(1)} %shard_map.106.iterate), channel_id=1, source_target_pairs={{0,12},{1,5},{2,14},{3,7},{4,0},{5,9},{6,2},{7,11},{8,4},{9,13},{1... | collective-permute-start | bytes 49160 | tf_op jit(solution)/shard_map/ppermute | solution.py:645
  53.4 1.2 %collective-permute-start.18 = (f32[24,512]{1,0:T(8,128)S(1)}, f32[24,512]{1,0:T(8,128)S(1)}, u32[]{:S(2)}, u32[]{:S(2)}) collective-permute-start(f32[24,512]{1,0:T(8,128)S(1)} %shard_map.107.got), channel_id=1, source_target_pairs={{0,1},{1,0},{2,3},{3,2},{4,5},{5,4},{6,7},{7,6},{8,9},{9,8},{10,11... | collective-permute-start | bytes 147464 | tf_op jit(solution)/shard_map/ppermute | solution.py:713
  57.5 7.6 %collective-permute-start.19 = (f32[80,128]{1,0:T(8,128)S(1)}, f32[80,128]{1,0:T(8,128)S(1)}, u32[]{:S(2)}, u32[]{:S(2)}) collective-permute-start(f32[80,128]{1,0:T(8,128)S(1)} %get-tuple-element.85), channel_id=1, source_target_pairs={{1,2},{2,1},{3,0},{0,3},{5,6},{6,5},{7,4},{4,7},{9,10},{10,9},{11,... | collective-permute-start | bytes 122888 | tf_op jit(solution)/shard_map/ppermute | solution.py:629
  59.6 5.2 %collective-permute-start.20 = (f32[72,128]{1,0:T(8,128)S(1)}, f32[72,128]{1,0:T(8,128)S(1)}, u32[]{:S(2)}, u32[]{:S(2)}) collective-permute-start(f32[72,128]{1,0:T(8,128)S(1)} %get-tuple-element.86), channel_id=1, source_target_pairs={{4,8},{8,4},{12,0},{0,12},{5,9},{9,5},{13,1},{1,13},{6,10},{10,6},... | collective-permute-start | bytes 110600 | tf_op jit(solution)/shard_map/ppermute | solution.py:630
  61.2 4.0 %collective-permute-start.21 = (f32[72,128]{1,0:T(8,128)S(1)}, f32[72,128]{1,0:T(8,128)S(1)}, u32[]{:S(2)}, u32[]{:S(2)}) collective-permute-start(f32[72,128]{1,0:T(8,128)S(1)} %get-tuple-element.87), channel_id=1, source_target_pairs={{0,4},{4,0},{8,12},{12,8},{1,5},{5,1},{9,13},{13,9},{2,6},{6,2},{1... | collective-permute-start | bytes 110600 | tf_op jit(solution)/shard_map/ppermute | solution.py:631
  61.2 1.2 %collective-permute-start.22 = (f32[8,128]{1,0:T(8,128)S(1)}, f32[8,128]{1,0:T(8,128)S(1)}, u32[]{:S(2)}, u32[]{:S(2)}) collective-permute-start(f32[8,128]{1,0:T(8,128)S(1)} %get-tuple-element.88), channel_id=1, source_target_pairs={{0,1},{1,0},{2,3},{3,2},{4,5},{5,4},{6,7},{7,6},{8,9},{9,8},{10,11... | collective-permute-start | bytes 12296 | tf_op jit(solution)/shard_map/ppermute | solution.py:632
  67.6 6.3 %collective-permute-start.23 = (f32[3,4,8,128]{3,2,1,0:T(8,128)S(1)}, f32[3,4,8,128]{3,2,1,0:T(8,128)S(1)}, u32[]{:S(2)}, u32[]{:S(2)}) collective-permute-start(f32[3,4,8,128]{3,2,1,0:T(8,128)S(1)} %get-tuple-element.89), channel_id=1, source_target_pairs={{0,112},{16,0},{32,16},{48,32},{64,48},{80,64},{96,80},{112,96},{1... | collective-permute-start | bytes 147464 | tf_op jit(solution)/shard_map/ppermute | solution.py:726
